TPU v7x, 32 devices: a whole 2x2x4 slice. The times are simulated.
32 devices in a mesh: seq: 4 (over y, core), fsdp: 8 (over z, x).
Axes of the slice: x: 2, y: 2, z: 4, core: 2. Of those that a mesh axis runs over, the one named last changes fastest.
Arguments:
- tokens: bfloat16 [32, 200, 768], P(('fsdp', 'seq')), may hold values from -6 to 6
- key_mask: int32 [32, 200], P('fsdp'), may hold values from 0 to 1, as said below
- expert_ids: int32 [32, 200, 2], P(('fsdp', 'seq')), may hold values from 0 to 3, all different within a row; in each aligned block of 200 rows (0 to 199, 200 to 399, ..., all dimensions but the last counted through in order) at most 142 rows name the same one
- cotangent: bfloat16 [32, 200, 768], P(('fsdp', 'seq')), may hold values from -6 to 6
- norm1_gain: bfloat16 [768], P('fsdp'), may hold values from 0.5 to 1.5
- norm1_bias: bfloat16 [768], P('fsdp'), may hold values from -1 to 1
- w_qkv: bfloat16 [768, 2304], P('fsdp'), may hold values from -0.21875 to 0.21875
- w_proj: bfloat16 [768, 768], P('fsdp'), may hold values from -1.75 to 1.75
- proj_bias: bfloat16 [768], P('fsdp'), may hold values from -1 to 1
- norm2_gain: bfloat16 [768], P('fsdp'), may hold values from 0.5 to 1.5
- norm2_bias: bfloat16 [768], P('fsdp'), may hold values from -1 to 1
- w_router: bfloat16 [768, 4], P('fsdp'), may hold values from -0.15625 to 0.15625
- w_in: bfloat16 [4, 768, 3072], P(None, 'fsdp'), may hold values from -0.21875 to 0.21875
- b_in: bfloat16 [4, 3072], P(None, 'fsdp'), may hold values from -1 to 1
- w_out: bfloat16 [4, 3072, 768], P(None, 'fsdp'), may hold values from -0.3125 to 0.3125
- b_out: bfloat16 [4, 768], P(None, 'fsdp'), may hold values from -1 to 1
Outputs:
- mixed: bfloat16 [32, 200, 768], P(('fsdp', 'seq'))
- token_grad: bfloat16 [32, 200, 768], P(('fsdp', 'seq'))
- norm1_gain_grad: float32 [768], P('fsdp')
- norm1_bias_grad: float32 [768], P('fsdp')
- w_qkv_grad: float32 [768, 2304], P('fsdp')
- w_proj_grad: float32 [768, 768], P('fsdp')
- proj_bias_grad: float32 [768], P('fsdp')
- norm2_gain_grad: float32 [768], P('fsdp')
- norm2_bias_grad: float32 [768], P('fsdp')
- w_router_grad: float32 [768, 4], P('fsdp')
- w_in_grad: float32 [4, 768, 3072], P(None, 'fsdp')
- b_in_grad: float32 [4, 3072], P(None, 'fsdp')
- w_out_grad: float32 [4, 3072, 768], P(None, 'fsdp')
- b_out_grad: float32 [4, 768], P(None, 'fsdp')
Inputs may be any that keep to these rules, and one draw needn't show every extreme that they name: `expert_ids`: each token names two different experts. Among the 200 tokens of one device (aligned blocks of rows) no expert is named more than 142 times, and some expert of some device is named exactly 142 times. `key_mask`: each image's mask is 1 on a prefix of 160 to 200 tokens and 0 after it; both ends occur.
All inputs are finite; a program needn't handle non-finite values.
Results may differ from a plain program's by a relative error of at most 0.018.
Values may be sent and summed in bfloat16 or wider, within the bound.
A program may use at most 320 MiB of HBM per device.

v0:
```python
import jax
import jax.numpy as jnp
from jax import lax
from jax.sharding import PartitionSpec as P

HEADS = 12
CAP = 142


epsilon = 1e-06
masked_score = -1e30


def norm_rows(values, gain, offset):
    center = values - jnp.mean(values, axis=-1, keepdims=True)
    spread = jnp.mean(center * center, axis=-1, keepdims=True)
    return center * lax.rsqrt(spread + epsilon) * gain + offset


def softmax_rows(values):
    shifted = jnp.exp(values - jnp.max(values, axis=-1, keepdims=True))
    return shifted / jnp.sum(shifted, axis=-1, keepdims=True)


def exact_gelu(values):
    return jax.nn.gelu(values, approximate=False)


def expert_slots(chosen, experts):
    flat_ids = chosen.reshape(-1)
    onehot = (flat_ids[:, None] == jnp.arange(experts, dtype=jnp.int32)[None, :]).astype(jnp.int32)
    ranks = jnp.cumsum(onehot, axis=0, dtype=jnp.int32)
    slot_pos = jnp.sum(onehot * ranks, axis=1, dtype=jnp.int32) - 1
    return (flat_ids, slot_pos)


def per_device(
    tokens,
    key_mask,
    expert_ids,
    cotangent,
    norm1_gain,
    norm1_bias,
    w_qkv,
    w_proj,
    proj_bias,
    norm2_gain,
    norm2_bias,
    w_router,
    w_in,
    b_in,
    w_out,
    b_out,
):
    images, seq_len, width = tokens.shape
    experts = w_in.shape[0]
    head_dim = width // HEADS
    scaling = head_dim ** (-0.5)
    row_count = images * seq_len
    dense_set = (
        lax.all_gather(norm1_gain, "fsdp", axis=0, tiled=True),
        lax.all_gather(norm1_bias, "fsdp", axis=0, tiled=True),
        lax.all_gather(w_qkv, "fsdp", axis=0, tiled=True),
        lax.all_gather(w_proj, "fsdp", axis=0, tiled=True),
        lax.all_gather(proj_bias, "fsdp", axis=0, tiled=True),
        lax.all_gather(norm2_gain, "fsdp", axis=0, tiled=True),
        lax.all_gather(norm2_bias, "fsdp", axis=0, tiled=True),
        lax.all_gather(w_router, "fsdp", axis=0, tiled=True),
    )
    gain_first = dense_set[0].astype(jnp.float32)
    bias_first = dense_set[1].astype(jnp.float32)
    full_qkv = dense_set[2]
    full_proj = dense_set[3]
    bias_proj = dense_set[4].astype(jnp.float32)
    gain_second = dense_set[5].astype(jnp.float32)
    bias_second = dense_set[6].astype(jnp.float32)
    full_router = dense_set[7]
    expert_set = (
        lax.all_gather(w_in, "fsdp", axis=1, tiled=True),
        lax.all_gather(b_in, "fsdp", axis=1, tiled=True),
        lax.all_gather(w_out, "fsdp", axis=1, tiled=True),
        lax.all_gather(b_out, "fsdp", axis=1, tiled=True),
    )
    inner_weight = expert_set[0]
    inner_bias = expert_set[1].astype(jnp.float32)
    outer_weight = expert_set[2]
    outer_bias = expert_set[3].astype(jnp.float32)
    own_mask = lax.dynamic_slice_in_dim(key_mask, lax.axis_index("seq") * images, images, 0)
    keep_rows = own_mask.reshape(row_count, 1).astype(jnp.float32)
    usable = (key_mask > 0)[:, None, None, :]
    flat_tokens = tokens.astype(jnp.float32).reshape(row_count, width)
    normed_in = norm_rows(flat_tokens, gain_first, bias_first).astype(jnp.bfloat16)
    mixed_qkv = jnp.dot(normed_in, full_qkv, preferred_element_type=jnp.float32).astype(
        jnp.bfloat16
    )
    mixed_qkv = mixed_qkv.reshape(images, seq_len, 3, HEADS, head_dim)
    head_qkv = lax.all_to_all(mixed_qkv, "seq", split_axis=3, concat_axis=0, tiled=True)
    queries = head_qkv[:, :, 0]
    key_rows = head_qkv[:, :, 1]
    value_rows = head_qkv[:, :, 2]

    def score_block():
        raw = (
            jnp.einsum("gahd,gbhd->ghab", queries, key_rows, preferred_element_type=jnp.float32)
            * scaling
        )
        return jnp.where(usable, raw, masked_score)

    scores = score_block()
    row_top = jnp.max(scores, axis=-1, keepdims=True)
    shifted = jnp.exp(scores - row_top)
    row_total = jnp.sum(shifted, axis=-1, keepdims=True)
    attn_probs = (shifted / row_total).astype(jnp.bfloat16)
    log_total = row_top + jnp.log(row_total)
    head_out = jnp.einsum(
        "ghab,gbhd->gahd", attn_probs, value_rows, preferred_element_type=jnp.float32
    ).astype(jnp.bfloat16)
    attended = lax.all_to_all(head_out, "seq", split_axis=0, concat_axis=2, tiled=True).reshape(
        row_count, width
    )
    middle = (
        flat_tokens + jnp.dot(attended, full_proj, preferred_element_type=jnp.float32) + bias_proj
    )
    normed_mid = norm_rows(middle, gain_second, bias_second).astype(jnp.bfloat16)
    routing = softmax_rows(jnp.dot(normed_mid, full_router, preferred_element_type=jnp.float32))
    chosen = expert_ids.reshape(row_count, 2)
    flat_ids, slot_pos = expert_slots(chosen, experts)
    gating = jnp.take_along_axis(routing, chosen, axis=1)
    buffer = (
        jnp.zeros((experts, CAP, width), jnp.bfloat16)
        .at[flat_ids, slot_pos]
        .set(jnp.repeat(normed_mid, 2, axis=0))
    )
    pre_act = (
        jnp.einsum("ecd,edf->ecf", buffer, inner_weight, preferred_element_type=jnp.float32)
        + inner_bias[:, None, :]
    )
    activated = exact_gelu(pre_act).astype(jnp.bfloat16)
    expert_out = (
        jnp.einsum("ecf,efd->ecd", activated, outer_weight, preferred_element_type=jnp.float32)
        + outer_bias[:, None, :]
    )
    picked = expert_out[flat_ids, slot_pos].reshape(row_count, 2, width)
    mixture = jnp.sum(gating[:, :, None] * picked, axis=1)
    mixed = (keep_rows * (middle + mixture)).astype(jnp.bfloat16).reshape(images, seq_len, width)
    grad_out = cotangent.astype(jnp.float32).reshape(row_count, width) * keep_rows
    grad_gate = jnp.sum(grad_out[:, None, :] * picked, axis=2)
    grad_picked = (
        (gating[:, :, None] * grad_out[:, None, :])
        .astype(jnp.bfloat16)
        .reshape(2 * row_count, width)
    )
    grad_expert_out = (
        jnp.zeros((experts, CAP, width), jnp.bfloat16).at[flat_ids, slot_pos].set(grad_picked)
    )
    grad_outer_bias = jnp.sum(grad_expert_out, axis=1, dtype=jnp.float32)
    hidden_pre = (
        jnp.einsum("ecd,edf->ecf", buffer, inner_weight, preferred_element_type=jnp.float32)
        + inner_bias[:, None, :]
    )
    hidden_act = exact_gelu(hidden_pre).astype(jnp.bfloat16)
    grad_outer_weight = jnp.einsum(
        "ecf,ecd->efd", hidden_act, grad_expert_out, preferred_element_type=jnp.float32
    )
    grad_act = jnp.einsum(
        "ecd,efd->ecf", grad_expert_out, outer_weight, preferred_element_type=jnp.float32
    )
    gelu_pull = jax.vjp(exact_gelu, hidden_pre)[1]
    grad_pre = gelu_pull(grad_act)[0].astype(jnp.bfloat16)
    grad_inner_bias = jnp.sum(grad_pre, axis=1, dtype=jnp.float32)
    grad_inner_weight = jnp.einsum(
        "ecd,ecf->edf", buffer, grad_pre, preferred_element_type=jnp.float32
    )
    grad_buffer = jnp.einsum(
        "ecf,edf->ecd", grad_pre, inner_weight, preferred_element_type=jnp.float32
    )
    grad_rows = jnp.sum(grad_buffer[flat_ids, slot_pos].reshape(row_count, 2, width), axis=1)
    expert_range = jnp.arange(experts, dtype=jnp.int32)[None, None, :]
    grad_route = jnp.sum(
        grad_gate[:, :, None] * (chosen[:, :, None] == expert_range).astype(jnp.float32), axis=1
    )
    grad_logits = (
        routing * (grad_route - jnp.sum(routing * grad_route, axis=-1, keepdims=True))
    ).astype(jnp.bfloat16)
    grad_router = jnp.einsum(
        "nd,ne->de", normed_mid, grad_logits, preferred_element_type=jnp.float32
    )
    grad_normed_mid = grad_rows + jnp.einsum(
        "ne,de->nd", grad_logits, full_router, preferred_element_type=jnp.float32
    )
    second_pull = jax.vjp(norm_rows, middle, gain_second, bias_second)[1]
    grad_mid_norm, grad_gain_second, grad_bias_second = second_pull(grad_normed_mid)
    grad_middle = grad_out + grad_mid_norm
    grad_proj = grad_middle.astype(jnp.bfloat16)
    grad_bias_proj = jnp.sum(grad_proj, axis=0, dtype=jnp.float32)
    grad_proj_weight = jnp.einsum(
        "nd,ne->de", attended, grad_proj, preferred_element_type=jnp.float32
    )
    grad_attended = jnp.einsum(
        "ne,de->nd", grad_proj, full_proj, preferred_element_type=jnp.float32
    ).astype(jnp.bfloat16)
    grad_head_out = lax.all_to_all(
        grad_attended.reshape(images, seq_len, HEADS, head_dim),
        "seq",
        split_axis=2,
        concat_axis=0,
        tiled=True,
    )
    recomputed = jnp.exp(score_block() - log_total)
    grad_values = jnp.einsum(
        "ghab,gahd->gbhd",
        recomputed.astype(jnp.bfloat16),
        grad_head_out,
        preferred_element_type=jnp.float32,
    )
    grad_probs = jnp.einsum(
        "gahd,gbhd->ghab", grad_head_out, value_rows, preferred_element_type=jnp.float32
    )
    grad_scores = (
        recomputed * (grad_probs - jnp.sum(recomputed * grad_probs, axis=-1, keepdims=True))
    ).astype(jnp.bfloat16)
    grad_queries = (
        jnp.einsum("ghab,gbhd->gahd", grad_scores, key_rows, preferred_element_type=jnp.float32)
        * scaling
    )
    grad_keys = (
        jnp.einsum("ghab,gahd->gbhd", grad_scores, queries, preferred_element_type=jnp.float32)
        * scaling
    )
    grad_head_qkv = jnp.stack([grad_queries, grad_keys, grad_values], axis=2).astype(jnp.bfloat16)
    grad_qkv = lax.all_to_all(
        grad_head_qkv, "seq", split_axis=0, concat_axis=3, tiled=True
    ).reshape(row_count, 3 * width)
    grad_qkv_weight = jnp.einsum(
        "nd,ne->de", normed_in, grad_qkv, preferred_element_type=jnp.float32
    )
    grad_normed_in = jnp.einsum("ne,de->nd", grad_qkv, full_qkv, preferred_element_type=jnp.float32)
    first_pull = jax.vjp(norm_rows, flat_tokens, gain_first, bias_first)[1]
    grad_first, grad_gain_first, grad_bias_first = first_pull(grad_normed_in)
    token_grad = (grad_middle + grad_first).astype(jnp.bfloat16).reshape(images, seq_len, width)
    shares = (
        lax.psum_scatter(grad_gain_first, "fsdp", scatter_dimension=0, tiled=True),
        lax.psum_scatter(grad_bias_first, "fsdp", scatter_dimension=0, tiled=True),
        lax.psum_scatter(grad_qkv_weight, "fsdp", scatter_dimension=0, tiled=True),
        lax.psum_scatter(grad_proj_weight, "fsdp", scatter_dimension=0, tiled=True),
        lax.psum_scatter(grad_bias_proj, "fsdp", scatter_dimension=0, tiled=True),
        lax.psum_scatter(grad_gain_second, "fsdp", scatter_dimension=0, tiled=True),
        lax.psum_scatter(grad_bias_second, "fsdp", scatter_dimension=0, tiled=True),
        lax.psum_scatter(grad_router, "fsdp", scatter_dimension=0, tiled=True),
        lax.psum_scatter(grad_inner_weight, "fsdp", scatter_dimension=1, tiled=True),
        lax.psum_scatter(grad_inner_bias, "fsdp", scatter_dimension=1, tiled=True),
        lax.psum_scatter(grad_outer_weight, "fsdp", scatter_dimension=1, tiled=True),
        lax.psum_scatter(grad_outer_bias, "fsdp", scatter_dimension=1, tiled=True),
    )
    parted = (
        lax.psum_scatter(
            shares[0].astype(jnp.bfloat16), "seq", scatter_dimension=0, tiled=True
        ).astype(jnp.float32),
        lax.psum_scatter(
            shares[1].astype(jnp.bfloat16), "seq", scatter_dimension=0, tiled=True
        ).astype(jnp.float32),
        lax.psum_scatter(
            shares[2].astype(jnp.bfloat16), "seq", scatter_dimension=0, tiled=True
        ).astype(jnp.float32),
        lax.psum_scatter(
            shares[3].astype(jnp.bfloat16), "seq", scatter_dimension=0, tiled=True
        ).astype(jnp.float32),
        lax.psum_scatter(
            shares[4].astype(jnp.bfloat16), "seq", scatter_dimension=0, tiled=True
        ).astype(jnp.float32),
        lax.psum_scatter(
            shares[5].astype(jnp.bfloat16), "seq", scatter_dimension=0, tiled=True
        ).astype(jnp.float32),
        lax.psum_scatter(
            shares[6].astype(jnp.bfloat16), "seq", scatter_dimension=0, tiled=True
        ).astype(jnp.float32),
        lax.psum_scatter(
            shares[7].astype(jnp.bfloat16), "seq", scatter_dimension=0, tiled=True
        ).astype(jnp.float32),
        lax.psum_scatter(
            shares[8].astype(jnp.bfloat16), "seq", scatter_dimension=1, tiled=True
        ).astype(jnp.float32),
        lax.psum_scatter(
            shares[9].astype(jnp.bfloat16), "seq", scatter_dimension=1, tiled=True
        ).astype(jnp.float32),
        lax.psum_scatter(
            shares[10].astype(jnp.bfloat16), "seq", scatter_dimension=1, tiled=True
        ).astype(jnp.float32),
        lax.psum_scatter(
            shares[11].astype(jnp.bfloat16), "seq", scatter_dimension=1, tiled=True
        ).astype(jnp.float32),
    )
    totals = (
        lax.all_gather(parted[0].astype(jnp.bfloat16), "seq", axis=0, tiled=True).astype(
            jnp.float32
        ),
        lax.all_gather(parted[1].astype(jnp.bfloat16), "seq", axis=0, tiled=True).astype(
            jnp.float32
        ),
        lax.all_gather(parted[2].astype(jnp.bfloat16), "seq", axis=0, tiled=True).astype(
            jnp.float32
        ),
        lax.all_gather(parted[3].astype(jnp.bfloat16), "seq", axis=0, tiled=True).astype(
            jnp.float32
        ),
        lax.all_gather(parted[4].astype(jnp.bfloat16), "seq", axis=0, tiled=True).astype(
            jnp.float32
        ),
        lax.all_gather(parted[5].astype(jnp.bfloat16), "seq", axis=0, tiled=True).astype(
            jnp.float32
        ),
        lax.all_gather(parted[6].astype(jnp.bfloat16), "seq", axis=0, tiled=True).astype(
            jnp.float32
        ),
        lax.all_gather(parted[7].astype(jnp.bfloat16), "seq", axis=0, tiled=True).astype(
            jnp.float32
        ),
        lax.all_gather(parted[8].astype(jnp.bfloat16), "seq", axis=1, tiled=True).astype(
            jnp.float32
        ),
        lax.all_gather(parted[9].astype(jnp.bfloat16), "seq", axis=1, tiled=True).astype(
            jnp.float32
        ),
        lax.all_gather(parted[10].astype(jnp.bfloat16), "seq", axis=1, tiled=True).astype(
            jnp.float32
        ),
        lax.all_gather(parted[11].astype(jnp.bfloat16), "seq", axis=1, tiled=True).astype(
            jnp.float32
        ),
    )
    return (
        mixed,
        token_grad,
        totals[0],
        totals[1],
        totals[2],
        totals[3],
        totals[4],
        totals[5],
        totals[6],
        totals[7],
        totals[8],
        totals[9],
        totals[10],
        totals[11],
    )


def solution(mesh):
    return jax.shard_map(
        per_device,
        mesh=mesh,
        in_specs=(
            P(("fsdp", "seq"), None, None),
            P("fsdp", None),
            P(("fsdp", "seq"), None, None),
            P(("fsdp", "seq"), None, None),
            P("fsdp"),
            P("fsdp"),
            P("fsdp", None),
            P("fsdp", None),
            P("fsdp"),
            P("fsdp"),
            P("fsdp"),
            P("fsdp", None),
            P(None, "fsdp", None),
            P(None, "fsdp"),
            P(None, "fsdp", None),
            P(None, "fsdp"),
        ),
        out_specs=(
            P(("fsdp", "seq"), None, None),
            P(("fsdp", "seq"), None, None),
            P("fsdp"),
            P("fsdp"),
            P("fsdp", None),
            P("fsdp", None),
            P("fsdp"),
            P("fsdp"),
            P("fsdp"),
            P("fsdp", None),
            P(None, "fsdp", None),
            P(None, "fsdp"),
            P(None, "fsdp", None),
            P(None, "fsdp"),
        ),
        check_vma=False,
    )
```

profile of v0, /device:TPU:0, one launch (start us, length us, event | category | flops | bytes accessed | tf_op | source)
XLA Modules:
  0.0 2666.7 jit_solution(2084386604965361643)
XLA Ops:
  13.0 39.1 %all-reduce.24 = (bf16[768]{0:T(1024)(128)(2,1)S(1)}, bf16[768]{0:T(1024)(128)(2,1)S(1)}, bf16[768]{0:T(1024)(128)(2,1)S(1)}, bf16[768]{0:T(1024)(128)(2,1)S(1)}, bf16[768]{0:T(1024)(128)(2,1)S(1)}) all-reduce(bf16[768]{0:T(1024)(128)(2,1)S(1)} %dynamic-update-slice.1, ...), channel_id=1, replica_groups=mesh['seq'=4,'fsdp'=8] {'fsdp'}, use_global_device_ids=true, to_apply=%add.2 | all-reduce | flops 3840 | bytes 15360
  52.2 16.5 all-gather
  71.0 7.7 all-gather.12.cloned.1.call-done
  78.7 3.0 convolution_convert_fusion
  83.4 3.5 all-to-all-start
  87.2 15.7 all-to-all-done
  106.6 4.1 all-to-all-start.1
  110.8 51.7 %all_gather.81 = bf16[4,3072]{1,0:T(4,128)(2,1)S(1)} all-gather(bf16[4,384]{1,0:T(4,128)(2,1)S(1)} %copy-done.63), channel_id=1, replica_groups=mesh['seq'=4,'fsdp'=8] {'fsdp'}, dimensions={1}, use_global_device_ids=true | all-gather | bytes 27648 | tf_op jit(solution)/shard_map/all_gather | solution.py:80
  164.1 2.0 fusion.81
  168.8 6.1 gather_fusion.2
  175.4 23.6 scatter_fusion.1
  199.2 23.6 scatter_fusion
  222.8 260.9 %all-gather.16.cloned.1.call-done = bf16[4,768,3072]{2,1,0:T(8,128)(2,1)} async-done(((bf16[4,96,3072]{2,1,0:T(8,128)(2,1)}), bf16[4,768,3072]{2,1,0:T(8,128)(2,1)}) %all-gather.16.cloned.1.call-update) | async-done | bytes 18874384 | tf_op jit(solution)/shard_map/all_gather | solution.py:79
  483.7 14.8 fusion.9
  498.5 18.4 multiply_convert_fusion
  516.9 1.8 copy-done.4
  518.7 15.3 fusion.21
  534.1 313.4 %all-gather.18.cloned.1.call-done = bf16[4,3072,768]{2,1,0:T(8,128)(2,1)} async-done(((bf16[4,384,768]{2,1,0:T(8,128)(2,1)}), bf16[4,3072,768]{2,1,0:T(8,128)(2,1)}) %all-gather.18.cloned.1.call-update) | async-done | bytes 18874384 | tf_op jit(solution)/shard_map/all_gather | solution.py:81
  847.5 16.4 convert_reduce_fusion
  863.9 17.2 fusion.27
  881.1 20.5 all-gather.1
  907.6 8.4 convolution_add_fusion
  917.1 10.3 fusion.83
  928.5 6.9 gather_fusion
  935.4 6.8 gather_fusion.1
  942.2 2.1 reshape.345
  944.4 3.1 reshape.341
  947.6 4.3 multiply_reduce_fusion.1
  956.3 2.1 fusion.75
  958.7 3.0 fusion.84
  961.8 2.6 convolution_convert_fusion.3
  964.3 1.9 copy.207
  966.2 3.5 all-to-all-start.2
  969.8 7.3 all-to-all-done.2
  977.1 1.8 multiply_reduce_fusion
  981.3 18.3 all_to_all.66
  999.8 4.3 fusion.51
  1004.2 450.0 %reduce-scatter.35.cloned.1.call-done = f32[4,384,768]{2,1,0:T(8,128)} async-done(((f32[4,3072,768]{2,1,0:T(8,128)}), f32[4,384,768]{2,1,0:T(8,128)}) %reduce-scatter.35.cloned.1.call-update) | async-done | bytes 4718608 | tf_op jit(solution)/shard_map/reduce_scatter | solution.py:252
  1454.2 4.0 convert_element_type.250
  1458.5 603.1 %reduce-scatter.33.cloned.1.call-done = f32[4,96,3072]{2,1,0:T(8,128)} async-done(((f32[4,768,3072]{2,1,0:T(8,128)}), f32[4,96,3072]{2,1,0:T(8,128)}) %reduce-scatter.33.cloned.1.call-update) | async-done | bytes 4718608 | tf_op jit(solution)/shard_map/reduce_scatter | solution.py:250
  2061.5 2.7 convert_element_type.245
  2064.2 1.8 copy.227
  2066.1 2.2 copy.238
  2070.9 58.1 %reduce-scatter.43.cloned.1.call-done = f32[384,4]{1,0:T(8,128)} async-done(((f32[3072,4]{1,0:T(8,128)}), f32[384,4]{1,0:T(8,128)}) %reduce-scatter.43.cloned.1.call-update) | async-done | bytes 6160
  2131.0 70.4 %reduce-scatter.29.cloned.1.call-done = f32[96,768]{1,0:T(8,128)} async-done(((f32[768,768]{1,0:T(8,128)}), f32[96,768]{1,0:T(8,128)}) %reduce-scatter.29.cloned.1.call-update) | async-done | bytes 294928 | tf_op jit(solution)/shard_map/reduce_scatter | solution.py:245
  2203.1 130.5 %reduce-scatter.25.cloned.1.call-done = f32[96,2304]{1,0:T(8,128)} async-done(((f32[768,2304]{1,0:T(8,128)}), f32[96,2304]{1,0:T(8,128)}) %reduce-scatter.25.cloned.1.call-update) | async-done | bytes 884752 | tf_op jit(solution)/shard_map/reduce_scatter | solution.py:244
  2333.7 2.0 convert_element_type.232
  2335.7 32.5 %reduce-scatter.37.cloned.1.call-done = bf16[4,96,768]{2,1,0:T(8,128)(2,1)} async-done(((bf16[4,384,768]{2,1,0:T(8,128)(2,1)}), bf16[4,96,768]{2,1,0:T(8,128)(2,1)}) %reduce-scatter.37.cloned.1.call-update) | async-done | bytes 589840 | tf_op jit(solution)/shard_map/reduce_scatter | solution.py:286
  2368.3 36.3 %reduce-scatter.41.cloned.1.call-done = bf16[24,12288]{1,0:T(8,128)(2,1)} async-done(((bf16[96,12288]{1,0:T(8,128)(2,1)}), bf16[24,12288]{1,0:T(8,128)(2,1)}) %reduce-scatter.41.cloned.1.call-update) | async-done | bytes 589840
  2409.1 60.0 %reduce-scatter.47.cloned.1.call-done = f32[96,4]{1,0:T(8,128)} async-done(((f32[768,4]{1,0:T(8,128)}), f32[96,4]{1,0:T(8,128)}) %reduce-scatter.47.cloned.1.call-update) | async-done | bytes 1552
  2470.0 62.8 %reduce-scatter.39.cloned.1.call-done = f32[96,4]{1,0:T(8,128)} async-done(((f32[768,4]{1,0:T(8,128)}), f32[96,4]{1,0:T(8,128)}) %reduce-scatter.39.cloned.1.call-update) | async-done | bytes 1552
  2533.7 20.6 reduce-scatter.45.cloned.1.call-done
  2555.1 5.1 all-gather.3
  2560.8 3.8 fusion.73
  2565.0 37.1 %all-reduce.23 = (bf16[768]{0:T(1024)(128)(2,1)S(1)}, bf16[768]{0:T(1024)(128)(2,1)S(1)}, bf16[768]{0:T(1024)(128)(2,1)S(1)}, bf16[768]{0:T(1024)(128)(2,1)S(1)}, bf16[768]{0:T(1024)(128)(2,1)S(1)}) all-reduce(f32[768]{0:T(1024)S(1)} %get-tuple-element.20, ...), channel_id=2, replica_groups=mesh['seq'=4,'fsdp'=8] {'fsdp'}, use_global_device_ids=true, to_apply=%region_24.25.clone | all-reduce | flops 3840 | bytes 23040
  2602.5 5.9 all-reduce.26
  2609.8 6.4 all-reduce.25
  2618.9 5.1 all-gather.2
  2624.7 5.1 all-gather.4
  2631.5 5.7 all_gather.87
  2637.9 9.8 all_gather.86
  2648.7 4.3 convert_element_type.251
  2653.0 2.0 all-gather.20.cloned.1.call-done
  2655.0 4.4 convert_element_type.246
  (322 shorter events, 54.5 us)
Async XLA Ops:
  7.3 44.9 %copy-start.66 = (bf16[96,4]{0,1:T(4,128)(2,1)S(1)}, bf16[96,4]{0,1:T(4,128)(2,1)}, u32[]{:S(2)}) copy-start(bf16[96,4]{0,1:T(4,128)(2,1)} %param.27) | copy-start | bytes 2308
  7.3 63.3 %copy-start.62 = (s32[4,200]{1,0:T(4,128)S(1)}, s32[4,200]{1,0:T(4,128)}, u32[]{:S(2)}) copy-start(s32[4,200]{1,0:T(4,128)} %param.17) | copy-start | bytes 9604
  7.3 63.3 %copy-start.9 = (bf16[1,200,768]{2,1,0:T(8,128)(2,1)S(1)}, bf16[1,200,768]{2,1,0:T(8,128)(2,1)}, u32[]{:S(2)}) copy-start(bf16[1,200,768]{2,1,0:T(8,128)(2,1)} %param.16) | copy-start | bytes 921604
  7.3 71.4 %all-gather.12.cloned.1.call-start = ((), (), s32[]{:S(2)}) async-start(), calls=%async_computation.16 | async-start | bytes 3981312 | tf_op jit(solution)/shard_map/all_gather | solution.py:63
  8.0 156.0 %all-gather.14.cloned.1.call-start = ((), (), s32[]{:S(2)}) async-start(), calls=%async_computation.17 | async-start | bytes 1327104 | tf_op jit(solution)/shard_map/all_gather | solution.py:64
  8.8 474.9 %all-gather.16.cloned.1.call-start = ((), (), s32[]{:S(2)}) async-start(), calls=%async_computation.18 | async-start | bytes 21233664 | tf_op jit(solution)/shard_map/all_gather | solution.py:79
  9.5 838.0 %all-gather.18.cloned.1.call-start = ((), (), s32[]{:S(2)}) async-start(), calls=%async_computation.19 | async-start | bytes 21233664 | tf_op jit(solution)/shard_map/all_gather | solution.py:81
  10.2 68.5 %copy-start.21 = (s32[1,200,2]{2,1,0:T(8,128)}, s32[1,200,2]{2,1,0:T(8,128)S(1)}, u32[]{:S(2)}) copy-start(s32[1,200,2]{2,1,0:T(8,128)S(1)} %copy.195) | copy-start | bytes 4804
  52.2 31.3 %copy-start.26 = (f32[768]{0:T(1024)}, f32[768]{0:T(1024)S(1)}, u32[]{:S(2)}) copy-start(f32[768]{0:T(1024)S(1)} %convert_element_type.204) | copy-start | bytes 9220
  52.2 31.3 %copy-start.24 = (f32[768]{0:T(1024)}, f32[768]{0:T(1024)S(1)}, u32[]{:S(2)}) copy-start(f32[768]{0:T(1024)S(1)} %convert_element_type.203) | copy-start | bytes 9220
  68.8 99.7 %copy-start.32 = (bf16[768,4]{0,1:T(4,128)(2,1)}, bf16[768,4]{0,1:T(4,128)(2,1)S(1)}, u32[]{:S(2)}) copy-start(bf16[768,4]{0,1:T(4,128)(2,1)S(1)} %reshape.414) | copy-start | bytes 18436
  70.6 16.5 copy-start.41
  70.7 12.7 copy-start.35
  71.0 12.5 copy-start.56
  71.0 12.4 copy-start.43
  71.0 16.0 copy-start.18
  83.4 19.4 all-to-all-start
  87.2 75.6 %copy-start.11 = (f32[200,768]{1,0:T(8,128)}, f32[200,768]{1,0:T(8,128)S(1)}, u32[]{:S(2)}) copy-start(f32[200,768]{1,0:T(8,128)S(1)} %convert_multiply_fusion) | copy-start | bytes 1843204
  106.6 57.5 %all-to-all-start.1 = ((bf16[4,200,3,64]{1,3,2,0:T(8,128)(2,1)}), bf16[4,200,3,64]{1,3,2,0:T(8,128)(2,1)}, u32[]{:S(2)}, u32[]{:S(2)}) async-start(bf16[4,200,3,64]{1,3,2,0:T(8,128)(2,1)} %fusion.15), calls=%async_computation.1 | async-start | bytes 786432 | tf_op jit(solution)/shard_map/all_to_all | solution.py:118
  110.7 1343.5 %reduce-scatter.35.cloned.1.call-start = ((), (), s32[]{:S(2)}) async-start(), calls=%async_computation.26 | async-start | bytes 42467328 | tf_op jit(solution)/shard_map/reduce_scatter | solution.py:252
  166.3 8.7 copy-start.58
  168.7 6.3 copy-start.37
  175.4 23.8 copy-start.22
  199.0 648.5 %copy-start = (bf16[4,142,768]{2,0,1:T(4,128)(2,1)}, bf16[4,142,768]{2,0,1:T(4,128)(2,1)S(1)}, u32[]{:S(2)}) copy-start(bf16[4,142,768]{2,0,1:T(4,128)(2,1)S(1)} %scatter_fusion.1) | copy-start | bytes 2617348
  534.0 1527.5 %reduce-scatter.33.cloned.1.call-start = ((), (), s32[]{:S(2)}) async-start(), calls=%async_computation.24 | async-start | bytes 42467328 | tf_op jit(solution)/shard_map/reduce_scatter | solution.py:250
  881.0 26.5 copy-start.5
  881.1 1248.0 %reduce-scatter.43.cloned.1.call-start = ((), (), s32[]{:S(2)}) async-start(), calls=%async_computation.31 | async-start | bytes 1769472
  907.6 9.6 copy-start.8
  942.2 9.7 copy-start.34
  944.3 10.8 copy-start.61
  944.4 10.8 copy-start.38
  944.4 10.8 copy-start.46
  944.4 10.8 copy-start.7
  944.4 10.8 copy-start.33
  944.4 10.8 copy-start.40
  944.4 10.8 copy-start.49
  944.4 11.8 copy-start.59
  944.4 11.8 copy-start.42
  951.9 6.6 copy-start.19
  958.6 11.1 copy-start.29
  958.7 11.1 copy-start.31
  958.7 18.5 copy-start.3
  958.7 1242.7 %reduce-scatter.29.cloned.1.call-start = ((), (), s32[]{:S(2)}) async-start(), calls=%async_computation.22 | async-start | bytes 2654208 | tf_op jit(solution)/shard_map/reduce_scatter | solution.py:245
  966.2 10.9 all-to-all-start.2
  969.7 1363.9 %reduce-scatter.25.cloned.1.call-start = ((), (), s32[]{:S(2)}) async-start(), calls=%async_computation.20 | async-start | bytes 7962624 | tf_op jit(solution)/shard_map/reduce_scatter | solution.py:244
  980.9 18.8 copy-start.10
  980.9 18.8 copy-start.25
  980.9 18.8 copy-start.27
  980.9 18.8 copy-start.36
  981.0 18.8 copy-start.44
  1004.1 1364.1 %reduce-scatter.37.cloned.1.call-start = ((), (), s32[]{:S(2)}) async-start(), calls=%async_computation.27 | async-start | bytes 2949120 | tf_op jit(solution)/shard_map/reduce_scatter | solution.py:286
  1458.2 946.4 %reduce-scatter.41.cloned.1.call-start = ((), (), s32[]{:S(2)}) async-start(), calls=%async_computation.30 | async-start | bytes 2949120
  2068.3 400.8 %reduce-scatter.47.cloned.1.call-start = ((), (), s32[]{:S(2)}) async-start(), calls=%async_computation.33 | async-start | bytes 442368
  2069.7 463.1 %reduce-scatter.39.cloned.1.call-start = ((), (), s32[]{:S(2)}) async-start(), calls=%async_computation.29 | async-start | bytes 442368
  2070.9 483.4 %reduce-scatter.45.cloned.1.call-start = ((), (), s32[]{:S(2)}) async-start(), calls=%async_computation.32 | async-start | bytes 122880
  2130.9 500.6 %reduce-scatter.31.cloned.1.call-start = ((), (), s32[]{:S(2)}) async-start(), calls=%async_computation.23 | async-start | bytes 184320 | tf_op jit(solution)/shard_map/reduce_scatter | solution.py:265
  2203.1 434.8 %reduce-scatter.27.cloned.1.call-start = ((), (), s32[]{:S(2)}) async-start(), calls=%async_computation.21 | async-start | bytes 552960 | tf_op jit(solution)/shard_map/reduce_scatter | solution.py:262
  2335.7 313.0 %all-gather.22.cloned.1.call-start = ((), (), s32[]{:S(2)}) async-start(), calls=%async_computation.28 | async-start | bytes 2949120 | tf_op jit(solution)/shard_map/all_gather | solution.py:324
  2368.2 196.4 %copy-start.57 = (f32[200]{0:T(256)S(1)}, f32[200]{0:T(256)}, u32[]{:S(2)}) copy-start(f32[200]{0:T(256)} %copy-done.56) | copy-start | bytes 2404
  2368.2 196.8 %copy-start.50 = (f32[768]{0:T(1024)S(1)}, f32[768]{0:T(1024)}, u32[]{:S(2)}) copy-start(f32[768]{0:T(1024)} %get-tuple-element.16) | copy-start | bytes 9220
  2368.2 196.8 %copy-start.51 = (f32[768]{0:T(1024)S(1)}, f32[768]{0:T(1024)}, u32[]{:S(2)}) copy-start(f32[768]{0:T(1024)} %get-tuple-element.22) | copy-start | bytes 9220
  2368.3 286.7 %all-gather.20.cloned.1.call-start = ((), (), s32[]{:S(2)}) async-start(), calls=%async_computation.25 | async-start | bytes 2949120 | tf_op jit(solution)/shard_map/all_gather | solution.py:318
  2406.1 224.3 %copy-start.20 = (bf16[1,200,768]{2,1,0:T(8,128)(2,1)S(1)}, bf16[1,200,768]{2,1,0:T(8,128)(2,1)}, u32[]{:S(2)}) copy-start(bf16[1,200,768]{2,1,0:T(8,128)(2,1)} %param.19) | copy-start | bytes 921604
  2406.1 224.3 %copy-start.53 = (f32[200]{0:T(256)S(1)}, f32[200]{0:T(256)}, u32[]{:S(2)}) copy-start(f32[200]{0:T(256)} %copy-done.52) | copy-start | bytes 2404
  (29 other events, 101.2 us)
Sparse Core Ops, SparseCore 0:
  10.3 68.3 all-gather.11
  80.9 39.7 all-gather.13
  122.2 361.3 all-gather.15
  485.1 362.3 all-gather.17
  851.2 602.9 reduce-scatter.34
  1458.4 603.1 reduce-scatter.32
  2065.0 64.0 reduce-scatter.42
  2133.5 67.8 reduce-scatter.28
  2205.5 128.0 reduce-scatter.24
  2336.0 32.1 reduce-scatter.36
  2371.5 33.0 reduce-scatter.40
  2407.7 61.3 reduce-scatter.46
  2472.4 60.3 reduce-scatter.38
  2535.7 18.5 reduce-scatter.44
  2557.1 19.6 reduce-scatter.30
  2579.7 21.0 reduce-scatter.26
  2602.3 24.3 all-gather.21
  2628.7 26.2 all-gather.19
where the time goes:
time: 2670 us
  waiting for transfers between devices  2130 us (80%)
  blocking collectives  226 us (8%)
  local copies, waits for them, and re-layouts  109 us (4%)
  matrix products  109 us (4%)
  other arithmetic  57.7 us (2%)
    reduce_scatter x1, waiting for transfers between devices, per_device(): lax.psum_scatter(grad_inner_weight, 'fsdp', scatter_dimension=1, tiled=True)  603 us
    reduce_scatter x1, waiting for transfers between devices, per_device(): lax.psum_scatter(grad_outer_weight, 'fsdp', scatter_dimension=1, tiled=True)  450 us
    all_gather x1, waiting for transfers between devices, per_device(): lax.all_gather(w_out, 'fsdp', axis=1, tiled=True)  313 us
    all_gather x1, waiting for transfers between devices, per_device(): lax.all_gather(w_in, 'fsdp', axis=1, tiled=True)  261 us
    unnamed x23, waiting for transfers between devices  241 us
    reduce_scatter x1, waiting for transfers between devices, per_device(): lax.psum_scatter(grad_qkv_weight, 'fsdp', scatter_dimension=0, tiled=True)  131 us
    unnamed x4, blocking collectives  88.5 us
    reduce_scatter x1, waiting for transfers between devices, per_device(): lax.psum_scatter(grad_proj_weight, 'fsdp', scatter_dimension=0, tiled=True)  70.4 us
  transfers between devices with their start and end apart: 21, of which 16 were waited for; matrix products, arithmetic and copies ran while one was open for 10% of the time, Pallas kernels for 0%

commit v1 on v0

--- a/solution.py
+++ b/solution.py
@@ -34,7 +34,7 @@
     return (flat_ids, slot_pos)
 
 
-def per_device(
+def gather_weights_plan(
     tokens,
     key_mask,
     expert_ids,
@@ -346,7 +346,352 @@
     )
 
 
+def z_shift(planes, step):
+    return [(2 * z + x, 2 * ((z + step) % planes) + x) for z in range(planes) for x in range(2)]
+
+
+def x_swap(planes):
+    return [(2 * z + x, 2 * z + 1 - x) for z in range(planes) for x in range(2)]
+
+
+core_swap = [(0, 1), (1, 0), (2, 3), (3, 2)]
+y_swap = [(0, 2), (1, 3), (2, 0), (3, 1)]
+
+
+def gather_fsdp(block, planes):
+    column = jnp.stack(
+        [block] + [lax.ppermute(block, "fsdp", z_shift(planes, k)) for k in range(1, planes)]
+    )
+    across = lax.ppermute(column, "fsdp", x_swap(planes))
+    return jnp.stack([column, across], axis=1)
+
+
+def gather_plane(block, planes):
+    mine = gather_fsdp(block, planes)
+    return jnp.stack([mine, lax.ppermute(mine, "seq", core_swap)])
+
+
+def scatter_fsdp(parts, planes):
+    add = lambda a, b: a.astype(jnp.float32) + b.astype(jnp.float32)
+    column = add(parts[:, 0], lax.ppermute(parts[:, 1], "fsdp", x_swap(planes))).astype(
+        jnp.bfloat16
+    )
+    total = column[0].astype(jnp.float32)
+    for k in range(1, planes):
+        total = total + lax.ppermute(column[k], "fsdp", z_shift(planes, -k)).astype(jnp.float32)
+    return total
+
+
+def scatter_plane(parts, planes):
+    other = lax.ppermute(parts[1], "seq", core_swap)
+    mine = (parts[0].astype(jnp.float32) + other.astype(jnp.float32)).astype(jnp.bfloat16)
+    return scatter_fsdp(mine, planes)
+
+
+def shard_order(planes):
+    f = lax.axis_index("fsdp")
+    z, x = f // 2, f % 2
+    g = jnp.arange(2 * planes, dtype=jnp.int32)
+    return ((z - g // 2) % planes) * 2 + (x ^ (g % 2))
+
+
+def sum_everywhere(parts, planes):
+    order = shard_order(planes)
+    shards, rows, columns = parts.shape
+    s = lax.axis_index("seq")
+    y, c = s // 2, s % 2
+    half, quarter = columns // 2, columns // 4
+    keep = lax.dynamic_slice_in_dim(parts, c * half, half, 2)
+    give = lax.dynamic_slice_in_dim(parts, (1 - c) * half, half, 2)
+    got = lax.ppermute(give, "seq", core_swap)
+    keep = (keep.astype(jnp.float32) + got.astype(jnp.float32)).astype(jnp.bfloat16)
+    give = lax.dynamic_slice_in_dim(keep, (1 - y) * quarter, quarter, 2)
+    keep = lax.dynamic_slice_in_dim(keep, y * quarter, quarter, 2)
+    got = lax.ppermute(give, "seq", y_swap)
+    keep = (keep.astype(jnp.float32) + got.astype(jnp.float32)).astype(jnp.bfloat16)
+    place = jnp.take(keep, order, axis=0).reshape(planes, 2, rows, quarter)
+    total = scatter_fsdp(place, planes).astype(jnp.bfloat16)
+    other = lax.ppermute(total, "seq", y_swap)
+    first, second = jnp.where(y == 0, total, other), jnp.where(y == 0, other, total)
+    total = jnp.concatenate([first, second], axis=1)
+    other = lax.ppermute(total, "seq", core_swap)
+    first, second = jnp.where(c == 0, total, other), jnp.where(c == 0, other, total)
+    return jnp.concatenate([first, second], axis=1).astype(jnp.float32)
+
+
+def norm_parts(values):
+    center = values - jnp.mean(values, axis=-1, keepdims=True)
+    rstd = lax.rsqrt(jnp.mean(center * center, axis=-1, keepdims=True) + epsilon)
+    return center * rstd, rstd
+
+
+def norm_back(grad, normal, rstd, gain):
+    scaled = grad * gain
+    return rstd * (
+        scaled
+        - jnp.mean(scaled, axis=-1, keepdims=True)
+        - normal * jnp.mean(scaled * normal, axis=-1, keepdims=True)
+    )
+
+
+def move_tokens_plan(
+    tokens,
+    key_mask,
+    expert_ids,
+    cotangent,
+    norm1_gain,
+    norm1_bias,
+    w_qkv,
+    w_proj,
+    proj_bias,
+    norm2_gain,
+    norm2_bias,
+    w_router,
+    w_in,
+    b_in,
+    w_out,
+    b_out,
+):
+    f32, bf16 = jnp.float32, jnp.bfloat16
+    _, rows, width = tokens.shape
+    experts, depth, hidden = w_in.shape
+    slice_width = w_out.shape[1]
+    planes = hidden // slice_width // 2
+    own = experts // 2
+    head_dim = width // HEADS
+    scaling = head_dim ** (-0.5)
+    s = lax.axis_index("seq")
+    f = lax.axis_index("fsdp")
+    core = s % 2
+    z, x = f // 2, f % 2
+    order = shard_order(planes)
+
+    small = jnp.concatenate(
+        [
+            jnp.stack([norm1_gain, norm1_bias, proj_bias, norm2_gain, norm2_bias], axis=1),
+            w_router,
+            b_out.T,
+        ],
+        axis=1,
+    )
+    small = jnp.pad(small, ((0, 0), (0, 128 - small.shape[1])))
+    dense = jnp.concatenate([small, w_qkv, w_proj], axis=1)
+    dense = gather_fsdp(dense, planes).reshape(2 * planes, depth, dense.shape[1])
+    dense = jnp.take(dense, order, axis=0).reshape(width, dense.shape[2])
+    small, full_qkv, full_proj = jnp.split(dense, [128, 128 + w_qkv.shape[1]], axis=1)
+    vectors = small[:, :5].T.astype(f32)
+    gain_first, bias_first, bias_proj, gain_second, bias_second = [vectors[i] for i in range(5)]
+    full_router = small[:, 5 : 5 + experts]
+    full_b_out = small[:, 5 + experts : 5 + 2 * experts].T.astype(f32)
+
+    own_mask = lax.dynamic_slice_in_dim(key_mask, s, 1, 0)
+    keep_rows = own_mask.reshape(rows, 1).astype(f32)
+    usable = (own_mask > 0)[:, None, :]
+    chosen = expert_ids.reshape(rows, 2)
+    selected = jnp.sum(
+        (chosen[:, :, None] == jnp.arange(experts, dtype=jnp.int32)).astype(f32), axis=1
+    )
+    grad_out = cotangent.astype(f32).reshape(rows, width) * keep_rows
+    packed = jnp.concatenate(
+        [grad_out.astype(bf16), jnp.pad(selected, ((0, 0), (0, 128 - experts))).astype(bf16)],
+        axis=1,
+    )
+    packed = gather_plane(packed, planes).reshape(-1, width + 128)
+    all_grad_out, all_selected = packed[:, :width], packed[:, width : width + experts].astype(f32)
+
+    mine_in = lax.dynamic_slice_in_dim(w_in, core * own, own, 0)
+    mine_in = mine_in.reshape(own, depth, 2 * planes, slice_width).transpose(2, 0, 1, 3)
+    mine_in = jnp.take(mine_in, order, axis=0).reshape(planes, 2, own, depth, slice_width)
+    across = lax.ppermute(mine_in[:, 1], "fsdp", x_swap(planes))
+    pairs = jnp.stack([mine_in[:, 0], across], axis=1)
+    got = [pairs[0]] + [
+        lax.ppermute(pairs[k], "fsdp", z_shift(planes, -k)) for k in range(1, planes)
+    ]
+    got = jnp.stack(got).reshape(2 * planes, own, depth, slice_width)
+    up_order = ((jnp.arange(2 * planes, dtype=jnp.int32) // 2 - z) % planes) * 2 + (
+        x ^ (jnp.arange(2 * planes, dtype=jnp.int32) % 2)
+    )
+    inner = jnp.take(got, up_order, axis=0).transpose(0, 2, 1, 3).reshape(width, own * slice_width)
+    outer = lax.dynamic_slice_in_dim(w_out, core * own, own, 0).reshape(own * slice_width, width)
+    inner_bias = lax.dynamic_slice_in_dim(b_in_slice(b_in), core * own, own, 0)
+    inner_bias = inner_bias.reshape(1, own * slice_width).astype(f32)
+
+    flat_tokens = tokens.astype(f32).reshape(rows, width)
+    normal_first, rstd_first = norm_parts(flat_tokens)
+    normed_in = (normal_first * gain_first + bias_first).astype(bf16)
+    qkv = jnp.dot(normed_in, full_qkv, preferred_element_type=f32).astype(bf16)
+    qkv = qkv.reshape(rows, 3, HEADS, head_dim).transpose(1, 2, 0, 3)
+    queries, key_rows, value_rows = qkv[0], qkv[1], qkv[2]
+    raw = jnp.einsum("had,hbd->hab", queries, key_rows, preferred_element_type=f32) * scaling
+    scores = jnp.where(usable, raw, masked_score)
+    shifted = jnp.exp(scores - jnp.max(scores, axis=-1, keepdims=True))
+    probs = shifted / jnp.sum(shifted, axis=-1, keepdims=True)
+    attended = jnp.einsum("hab,hbd->ahd", probs.astype(bf16), value_rows, preferred_element_type=f32)
+    attended = attended.astype(bf16).reshape(rows, width)
+    middle = flat_tokens + jnp.dot(attended, full_proj, preferred_element_type=f32) + bias_proj
+    normal_mid, rstd_mid = norm_parts(middle)
+    normed_mid = (normal_mid * gain_second + bias_second).astype(bf16)
+
+    everyone = gather_plane(normed_mid, planes).reshape(-1, width)
+    own_experts = core * own + jnp.arange(own, dtype=jnp.int32)
+    pick = (own_experts[:, None] == jnp.arange(experts, dtype=jnp.int32)).astype(f32)
+    routing = softmax_rows(jnp.dot(everyone, full_router, preferred_element_type=f32))
+    gates = jnp.dot(routing * all_selected, pick.T, precision=lax.Precision.HIGHEST)
+    spread_gates = jnp.repeat(gates, slice_width, axis=1)
+    pre = jnp.dot(everyone, inner, preferred_element_type=f32) + inner_bias
+    cdf = 0.5 * (1.0 + lax.erf(pre * (0.5**0.5)))
+    slope = cdf + pre * jnp.exp(-0.5 * pre * pre) * 0.3989422804014327
+    act = pre * cdf
+    gated = (spread_gates * act).astype(bf16)
+    mix_parts = jnp.dot(gated, outer, preferred_element_type=f32).astype(bf16)
+    grad_act = jnp.einsum("nd,fd->nf", all_grad_out, outer, preferred_element_type=f32)
+    grad_gate = jnp.sum((act * grad_act).reshape(-1, own, slice_width), axis=2)
+    grad_pre32 = spread_gates * grad_act * slope
+    grad_pre = grad_pre32.astype(bf16)
+    outer_grad = jnp.einsum("nf,nd->fd", gated, all_grad_out, preferred_element_type=f32)
+    inner_bias_grad = jnp.sum(grad_pre32, axis=0)
+    inner_grad = jnp.einsum("nd,nf->df", everyone, grad_pre, preferred_element_type=f32)
+    grad_gate = jnp.dot(grad_gate * all_select(all_selected, pick), pick, precision=lax.Precision.HIGHEST)
+    grad_logits = (
+        routing * (grad_gate - jnp.sum(routing * grad_gate, axis=-1, keepdims=True))
+    ).astype(bf16)
+    router_grad = jnp.einsum("nd,ne->de", everyone, grad_logits, preferred_element_type=f32)
+    row_parts = jnp.einsum("nf,df->nd", grad_pre, inner, preferred_element_type=f32)
+    row_parts = row_parts + jnp.einsum(
+        "ne,de->nd", grad_logits, full_router, preferred_element_type=f32
+    )
+    row_parts = row_parts.astype(bf16)
+    grad_rows = scatter_plane(row_parts.reshape(2, planes, 2, rows, width), planes)
+    mixture = scatter_plane(mix_parts.reshape(2, planes, 2, rows, width), planes)
+
+    own_routing = softmax_rows(jnp.dot(normed_mid, full_router, preferred_element_type=f32))
+    own_gates = own_routing * selected
+    mixture = mixture + jnp.dot(own_gates, full_b_out, precision=lax.Precision.HIGHEST)
+    mixed = (keep_rows * (middle + mixture)).astype(bf16).reshape(1, rows, width)
+    bias_gate = selected * jnp.einsum(
+        "nd,ed->ne", grad_out, full_b_out, precision=lax.Precision.HIGHEST
+    )
+    bias_logits = (
+        own_routing * (bias_gate - jnp.sum(own_routing * bias_gate, axis=-1, keepdims=True))
+    ).astype(bf16)
+    router_grad = router_grad + jnp.einsum(
+        "nd,ne->de", normed_mid, bias_logits, preferred_element_type=f32
+    )
+    outer_bias_grad = jnp.einsum(
+        "ne,nd->de", own_gates, grad_out, precision=lax.Precision.HIGHEST
+    )
+    grad_normed_mid = grad_rows + jnp.einsum(
+        "ne,de->nd", bias_logits, full_router, preferred_element_type=f32
+    )
+    grad_gain_second = jnp.sum(grad_normed_mid * normal_mid, axis=0)
+    grad_bias_second = jnp.sum(grad_normed_mid, axis=0)
+    grad_middle = grad_out + norm_back(grad_normed_mid, normal_mid, rstd_mid, gain_second)
+    grad_proj = grad_middle.astype(bf16)
+    grad_bias_proj = jnp.sum(grad_proj, axis=0, dtype=f32)
+    grad_proj_weight = jnp.einsum("nd,ne->de", attended, grad_proj, preferred_element_type=f32)
+    vectors = jnp.concatenate(
+        [
+            jnp.stack([grad_gain_second, grad_bias_second, grad_bias_proj], axis=1),
+            router_grad,
+            outer_bias_grad,
+        ],
+        axis=1,
+    )
+    early = jnp.concatenate(
+        [grad_proj_weight, jnp.pad(vectors, ((0, 0), (0, 256 - vectors.shape[1])))], axis=1
+    ).astype(bf16)
+    early = sum_everywhere(early.reshape(2 * planes, depth, width + 256), planes)
+    grad_attended = jnp.einsum("ne,de->nd", grad_proj, full_proj, preferred_element_type=f32)
+    grad_attended = grad_attended.astype(bf16).reshape(rows, HEADS, head_dim)
+    grad_values = jnp.einsum(
+        "hab,ahd->bhd", probs.astype(bf16), grad_attended, preferred_element_type=f32
+    )
+    grad_probs = jnp.einsum("ahd,hbd->hab", grad_attended, value_rows, preferred_element_type=f32)
+    grad_scores = (
+        probs * (grad_probs - jnp.sum(probs * grad_probs, axis=-1, keepdims=True))
+    ).astype(bf16)
+    grad_queries = (
+        jnp.einsum("hab,hbd->ahd", grad_scores, key_rows, preferred_element_type=f32) * scaling
+    )
+    grad_keys = (
+        jnp.einsum("hab,had->bhd", grad_scores, queries, preferred_element_type=f32) * scaling
+    )
+    grad_qkv = jnp.stack([grad_queries, grad_keys, grad_values], axis=1).astype(bf16)
+    grad_qkv = grad_qkv.reshape(rows, 3 * width)
+    grad_qkv_weight = jnp.einsum("nd,ne->de", normed_in, grad_qkv, preferred_element_type=f32)
+    grad_normed_in = jnp.einsum("ne,de->nd", grad_qkv, full_qkv, preferred_element_type=f32)
+    grad_gain_first = jnp.sum(grad_normed_in * normal_first, axis=0)
+    grad_bias_first = jnp.sum(grad_normed_in, axis=0)
+    token_grad = grad_middle + norm_back(grad_normed_in, normal_first, rstd_first, gain_first)
+    token_grad = token_grad.astype(bf16).reshape(1, rows, width)
+    vectors = jnp.stack([grad_gain_first, grad_bias_first], axis=1)
+    late = jnp.concatenate(
+        [grad_qkv_weight, jnp.pad(vectors, ((0, 0), (0, 256 - vectors.shape[1])))], axis=1
+    ).astype(bf16)
+    late = sum_everywhere(late.reshape(2 * planes, depth, 3 * width + 256), planes)
+
+    def both_cores(mine):
+        mine = mine.astype(bf16)
+        other = lax.ppermute(mine, "seq", core_swap)
+        first, second = jnp.where(core == 0, mine, other), jnp.where(core == 0, other, mine)
+        return jnp.concatenate([first, second], axis=0).astype(f32)
+
+    bias_row = jnp.pad(
+        inner_bias_grad.reshape(own, 1, slice_width), ((0, 0), (0, 15), (0, width - slice_width))
+    )
+    outer_grad = jnp.concatenate([outer_grad.reshape(own, slice_width, width), bias_row], axis=1)
+    outer_grad = outer_grad.astype(bf16)
+    outer_grad = outer_grad.astype(f32) + lax.ppermute(outer_grad, "seq", y_swap).astype(f32)
+    outer_grad = both_cores(outer_grad)
+    inner_grad = inner_grad.astype(bf16).reshape(2 * planes, depth, own, slice_width)
+    inner_grad = jnp.take(inner_grad, order, axis=0).reshape(planes, 2, depth, own, slice_width)
+    across = lax.ppermute(inner_grad[:, 1], "fsdp", x_swap(planes))
+    pairs = jnp.stack([inner_grad[:, 0], across], axis=1)
+    got = [pairs[0]] + [
+        lax.ppermute(pairs[k], "fsdp", z_shift(planes, -k)) for k in range(1, planes)
+    ]
+    got = jnp.stack(got).reshape(2 * planes, depth, own, slice_width)
+    inner_grad = jnp.take(got, up_order, axis=0).transpose(2, 1, 0, 3).reshape(own, depth, hidden)
+    inner_grad = inner_grad.astype(f32) + lax.ppermute(inner_grad, "seq", y_swap).astype(f32)
+    inner_grad = both_cores(inner_grad)
+    return (
+        mixed,
+        token_grad,
+        late[:, 3 * width],
+        late[:, 3 * width + 1],
+        late[:, : 3 * width],
+        early[:, :width],
+        early[:, width + 2],
+        early[:, width],
+        early[:, width + 1],
+        early[:, width + 3 : width + 3 + experts],
+        inner_grad,
+        outer_grad[:, slice_width, :slice_width],
+        outer_grad[:, :slice_width],
+        early[:, width + 3 + experts : width + 3 + 2 * experts].T,
+    )
+
+
+def b_in_slice(b_in):
+    return b_in
+
+
+def all_select(selected, pick):
+    return jnp.dot(selected, pick.T, precision=lax.Precision.HIGHEST)
+
+
 def solution(mesh):
+    n_seq, n_fsdp = mesh.shape["seq"], mesh.shape["fsdp"]
+
+    def per_device(*args):
+        tokens, w_in, w_out = args[0], args[12], args[14]
+        experts, _, hidden = w_in.shape
+        lanes = hidden // n_fsdp
+        whole_tiles = lanes % 128 == 0 and w_in.shape[1] % 16 == 0
+        if n_seq == 4 and experts == n_seq and tokens.shape[0] == 1 and whole_tiles:
+            return move_tokens_plan(*args)
+        return gather_weights_plan(*args)
+
     return jax.shard_map(
         per_device,
         mesh=mesh,

time: 2670 us -> 593 us (0.22)
  waiting for transfers between devices: 2130 us -> 244 us
  blocking collectives: 226 us -> 0 us
  starting transfers between devices: 12.1 us -> 101 us
  local copies, waits for them, and re-layouts: 109 us -> 61.1 us
  other arithmetic: 57.7 us -> 86.7 us
    reduce_scatter x7 -> x0, waiting for transfers between devices: 1290 us -> none  [the longest x1 603 us: per_device(): lax.psum_scatter(grad_inner_weight, 'fsdp', scatter_dimension=1, tiled=True)]
    all_gather x6 -> x0, waiting for transfers between devices: 584 us -> none  [the longest x1 313 us: per_device(): lax.all_gather(w_out, 'fsdp', axis=1, tiled=True)]
    ppermute x0 -> x52, waiting for transfers between devices: none -> 244 us  [the longest x9 71.2 us: gather_fsdp(): lax.ppermute(block, 'fsdp', z_shift(planes, k))]
    unnamed x23 -> x0, waiting for transfers between devices: 241 us -> none
    all_gather x8 -> x0, blocking collectives: 119 us -> none  [the longest x1 51.7 us: per_device(): lax.all_gather(b_in, 'fsdp', axis=1, tiled=True)]
    ppermute x0 -> x52, starting transfers between devices: none -> 101 us  [the longest x9 51.5 us: gather_fsdp(): lax.ppermute(block, 'fsdp', z_shift(planes, k))]
    unnamed x4 -> x0, blocking collectives: 88.5 us -> none
    scatter x2 -> x0, local copies, waits for them, and re-layouts: 47.1 us -> none  [the longest x1 23.6 us: per_device(): buffer = jnp.zeros((experts, CAP, width), jnp.bfloat16).at[flat_ids, slot...]
  transfers between devices with their start and end apart: 21 -> 52, of which waited for: 16 -> 26; matrix products, arithmetic and copies ran while one was open for 10% -> 24% of each run, Pallas kernels for 0% -> 0%
where the time goes in v1:
time: 593 us; the launch traced here: 584 us
  waiting for transfers between devices  244 us (41%)
  starting transfers between devices  101 us (17%)
  matrix products  87.9 us (15%)
  other arithmetic  86.7 us (15%)
  local copies, waits for them, and re-layouts  61.1 us (10%)
    ppermute x9, waiting for transfers between devices, gather_fsdp(): lax.ppermute(block, 'fsdp', z_shift(planes, k))  71.2 us
    ppermute x9, starting transfers between devices, gather_fsdp(): lax.ppermute(block, 'fsdp', z_shift(planes, k))  51.5 us
    ppermute x4, waiting for transfers between devices, scatter_fsdp(): lax.ppermute(parts[:, 1], 'fsdp', x_swap(planes))  44.1 us
    ppermute x6, waiting for transfers between devices, move_tokens_plan(): lax.ppermute(pairs[k], 'fsdp', z_shift(planes, -k))  34.5 us
    ppermute x12, waiting for transfers between devices, scatter_fsdp(): lax.ppermute(column[k], 'fsdp', z_shift(planes, -k)).astype(jnp.float32)  27.7 us
    ppermute x3, waiting for transfers between devices, gather_fsdp(): across = lax.ppermute(column, 'fsdp', x_swap(planes))  26.8 us
    ppermute x6, starting transfers between devices, move_tokens_plan(): lax.ppermute(pairs[k], 'fsdp', z_shift(planes, -k))  17.2 us
    ppermute x1, waiting for transfers between devices, move_tokens_plan(): lax.ppermute(inner_grad, 'seq', y_swap).astype(f32)  17.2 us
  transfers between devices with their start and end apart: 52, of which 26 were waited for; matrix products, arithmetic and copies ran while one was open for 24% of the time, Pallas kernels for 0%

profile of v1, /device:TPU:0, one launch (start us, length us, event | category | flops | bytes accessed | tf_op | source)
XLA Modules:
  0.0 583.5 jit_solution(16587453792611969115)
XLA Ops:
  4.4 4.1 collective-permute-start.1
  10.5 26.7 %collective-permute-done.1 = bf16[96,3200]{1,0:T(8,128)(2,1)S(1)} collective-permute-done((bf16[96,3200]{1,0:T(8,128)(2,1)S(1)}, bf16[96,3200]{1,0:T(8,128)(2,1)S(1)}, u32[]{:S(2)}, u32[]{:S(2)}) %collective-permute-start.1) | collective-permute-done | bytes 614432 | tf_op jit(solution)/shard_map/ppermute | solution.py:363
  37.2 12.6 %collective-permute-done = bf16[96,3200]{1,0:T(8,128)(2,1)S(1)} collective-permute-done((bf16[96,3200]{1,0:T(8,128)(2,1)S(1)}, bf16[96,3200]{1,0:T(8,128)(2,1)S(1)}, u32[]{:S(2)}, u32[]{:S(2)}) %collective-permute-start) | collective-permute-done | bytes 614432 | tf_op jit(solution)/shard_map/ppermute | solution.py:363
  49.9 2.5 fusion.176
  55.0 20.3 %collective-permute-start.9 = (bf16[200,896]{1,0:T(8,128)(2,1)}, bf16[200,896]{1,0:T(8,128)(2,1)}, u32[]{:S(2)}, u32[]{:S(2)}) collective-permute-start(bf16[200,896]{1,0:T(8,128)(2,1)} %get-tuple-element.172), channel_id=1, source_target_pairs={{0,2},{1,3},{2,4},{3,5},{4,6},{5,7},{6,0},{7,1},{8,10},{9,11},{10,... | collective-permute-start | bytes 1075208 | tf_op jit(solution)/shard_map/ppermute | solution.py:363
  78.4 6.1 %collective-permute-done.9 = bf16[200,896]{1,0:T(8,128)(2,1)} collective-permute-done((bf16[200,896]{1,0:T(8,128)(2,1)}, bf16[200,896]{1,0:T(8,128)(2,1)}, u32[]{:S(2)}, u32[]{:S(2)}) %collective-permute-start.9) | collective-permute-done | bytes 358432 | tf_op jit(solution)/shard_map/ppermute | solution.py:363
  84.4 8.3 %collective-permute-done.10 = bf16[200,896]{1,0:T(8,128)(2,1)} collective-permute-done((bf16[200,896]{1,0:T(8,128)(2,1)}, bf16[200,896]{1,0:T(8,128)(2,1)}, u32[]{:S(2)}, u32[]{:S(2)}) %collective-permute-start.10) | collective-permute-done | bytes 358432 | tf_op jit(solution)/shard_map/ppermute | solution.py:363
  92.7 4.8 collective-permute-done.11
  97.5 3.1 fusion.175
  101.4 7.6 %collective-permute-done.3 = bf16[4,96,3200]{2,1,0:T(8,128)(2,1)} collective-permute-done((bf16[4,96,3200]{2,1,0:T(8,128)(2,1)}, bf16[4,96,3200]{2,1,0:T(8,128)(2,1)}, u32[]{:S(2)}, u32[]{:S(2)}) %collective-permute-start.3) | collective-permute-done | bytes 2457632 | tf_op jit(solution)/shard_map/ppermute | solution.py:365
  109.0 4.4 pad_maximum_fusion.1
  113.4 5.7 gather_fusion
  119.1 7.5 %copy.194 = bf16[768,3200]{0,1:T(8,128)(2,1)} copy(bf16[768,3200]{1,0:T(8,128)(2,1)} %bitcast.362) | data formatting | bytes 9830400 | tf_op jit(solution)/shard_map/jit(_take)/gather | solution.py:480
  126.6 2.9 broadcast_select_fusion
  136.2 3.6 fusion.186
  144.6 20.3 %collective-permute-start.4 = (bf16[200,768]{1,0:T(8,128)(2,1)S(1)}, bf16[200,768]{1,0:T(8,128)(2,1)S(1)}, u32[]{:S(2)}, u32[]{:S(2)}) collective-permute-start(bf16[200,768]{1,0:T(8,128)(2,1)S(1)} %add_convert_fusion.7), channel_id=1, source_target_pairs={{0,2},{1,3},{2,4},{3,5},{4,6},{5,7},{6,0},{7,1},{8,10},{9,11},{10,... | collective-permute-start | bytes 921608 | tf_op jit(solution)/shard_map/ppermute | solution.py:363
  164.9 2.4 collective-permute-start.6
  168.8 3.8 collective-permute-done.4
  172.6 6.5 %collective-permute-done.5 = bf16[200,768]{1,0:T(8,128)(2,1)S(1)} collective-permute-done((bf16[200,768]{1,0:T(8,128)(2,1)S(1)}, bf16[200,768]{1,0:T(8,128)(2,1)S(1)}, u32[]{:S(2)}, u32[]{:S(2)}) %collective-permute-start.5) | collective-permute-done | bytes 307232 | tf_op jit(solution)/shard_map/ppermute | solution.py:363
  184.0 3.0 gather_fusion.3
  188.5 4.3 fusion.174
  194.1 19.2 %collective-permute-done.7 = bf16[4,200,768]{2,1,0:T(8,128)(2,1)} collective-permute-done((bf16[4,200,768]{2,1,0:T(8,128)(2,1)}, bf16[4,200,768]{2,1,0:T(8,128)(2,1)}, u32[]{:S(2)}, u32[]{:S(2)}) %collective-permute-start.7) | collective-permute-done | bytes 1228832 | tf_op jit(solution)/shard_map/ppermute | solution.py:365
  213.3 3.9 fusion.172
  217.2 3.4 collective-permute-done.14
  220.7 9.6 %collective-permute-start.15 = (bf16[2,2,96,384]{3,2,1,0:T(8,128)(2,1)S(1)}, bf16[2,2,96,384]{3,2,1,0:T(8,128)(2,1)S(1)}, u32[]{:S(2)}, u32[]{:S(2)}) collective-permute-start(bf16[2,2,96,384]{3,2,1,0:T(8,128)(2,1)S(1)} %get-tuple-element.158), channel_id=1, source_target_pairs={{0,6},{1,7},{2,0},{3,1},{4,2},{5,3},{6,4},{7,5},{8,14},{9,15},{10,... | collective-permute-start | bytes 884744 | tf_op jit(solution)/shard_map/ppermute | solution.py:508
  234.1 3.7 collective-permute-done.15
  237.8 15.1 %collective-permute-done.16 = bf16[2,2,96,384]{3,2,1,0:T(8,128)(2,1)S(1)} collective-permute-done((bf16[2,2,96,384]{3,2,1,0:T(8,128)(2,1)S(1)}, bf16[2,2,96,384]{3,2,1,0:T(8,128)(2,1)S(1)}, u32[]{:S(2)}, u32[]{:S(2)}) %collective-permute-start.16) | collective-permute-done | bytes 294944 | tf_op jit(solution)/shard_map/ppermute | solution.py:508
  266.4 2.4 copy-done.4
  269.2 2.9 pad_maximum_fusion.2
  274.8 4.5 fusion.191
  279.3 13.3 %fusion.33 = (f32[3200,768]{0,1:T(8,128)}, f32[3200,768]{0,1:T(8,128)}) fusion(f32[3200,768]{0,1:T(8,128)S(1)} %fusion.191, f32[768]{0:T(1024)S(1)} %reshape.410, bf16[768,768]{1,0:T(8,128)(2,1)S(1)} %bitcast.380, bf16[3200,896]{1,0:T(8,128)(2,1)} %bitcast.356), kind=kOutput, calls=%fused_computation.93 | convolution fusion | flops 3789619200 | bytes 35589120 | tf_op jit(solution)/shard_map/nd,fd->nf/dot_general | solution.py:547
  292.5 4.3 reduce_sum.206
  301.1 11.1 %fusion.177 = (bf16[768]{0:T(1024)(128)(2,1)S(1)}, bf16[3200,768]{0,1:T(8,128)(2,1)S(1)}, bf16[3200,768]{0,1:T(8,128)(2,1)S(1)}) fusion(f32[3200,768]{0,1:T(8,128)} %copy-done.2, f32[768]{0:T(1024)S(1)} %reshape.410, f32[3200,768]{0,1:T(8,128)} %get-tuple-element.196, f32[3200,2]{0,1:T(2,128)S(1)} %fusion.120), kind=kLoop, calls=%fused_computation.396 | loop fusion | flops 39320832 | bytes 29521408 | tf_op jit(solution)/shard_map/reduce_sum | solution.py:552
  312.2 5.1 fusion.30
  317.4 6.0 %convolution_convert_fusion = bf16[3200,768]{1,0:T(8,128)(2,1)} fusion(bf16[3200,768]{0,1:T(8,128)(2,1)S(1)} %get-tuple-element.126, bf16[768,768]{1,0:T(8,128)(2,1)S(1)} %bitcast.381), kind=kOutput, calls=%fused_computation.20 | convolution fusion | flops 3777331200 | bytes 11010048 | tf_op jit(solution)/shard_map/dot_general | solution.py:546
  323.4 5.2 fusion.27
  328.6 6.7 %fusion.20 = f32[3200,768]{1,0:T(8,128)} fusion(bf16[768,768]{1,0:T(8,128)(2,1)S(1)} %bitcast.395, bf16[3200,768]{0,1:T(8,128)(2,1)S(1)} %get-tuple-element.116), kind=kOutput, calls=%fused_computation.57 | convolution fusion | flops 3774873600 | bytes 15925248 | tf_op jit(solution)/shard_map/nf,df->nd/dot_general | solution.py:559
  335.4 3.0 reshape.402
  338.4 3.4 gather_fusion.5
  344.5 4.2 fusion.183
  350.3 5.3 add_convert_fusion
  365.8 3.0 collective-permute-start.46
  371.2 3.7 collective-permute-start.47
  374.9 3.1 fusion.42
  378.0 13.4 %collective-permute-done.46 = bf16[2,96,2,384]{3,1,2,0:T(8,128)(2,1)S(1)} collective-permute-done((bf16[2,96,2,384]{3,1,2,0:T(8,128)(2,1)S(1)}, bf16[2,96,2,384]{3,1,2,0:T(8,128)(2,1)S(1)}, u32[]{:S(2)}, u32[]{:S(2)}) %collective-permute-start.46) | collective-permute-done | bytes 294944 | tf_op jit(solution)/shard_map/ppermute | solution.py:651
  403.0 17.2 %collective-permute-done.48 = bf16[2,96,3072]{2,1,0:T(8,128)(2,1)S(1)} collective-permute-done((bf16[2,96,3072]{2,1,0:T(8,128)(2,1)S(1)}, bf16[2,96,3072]{2,1,0:T(8,128)(2,1)S(1)}, u32[]{:S(2)}, u32[]{:S(2)}) %collective-permute-start.48) | collective-permute-done | bytes 1179680 | tf_op jit(solution)/shard_map/ppermute | solution.py:655
  421.9 6.0 %collective-permute-done.19 = bf16[4,200,768]{2,1,0:T(8,128)(2,1)S(1)} collective-permute-done((bf16[4,200,768]{2,1,0:T(8,128)(2,1)S(1)}, bf16[4,200,768]{2,1,0:T(8,128)(2,1)S(1)}, u32[]{:S(2)}, u32[]{:S(2)}) %collective-permute-start.19) | collective-permute-done | bytes 1228832 | tf_op jit(solution)/shard_map/ppermute | solution.py:376
  430.5 23.4 %collective-permute-done.24 = bf16[4,200,768]{2,1,0:T(8,128)(2,1)S(1)} collective-permute-done((bf16[4,200,768]{2,1,0:T(8,128)(2,1)S(1)}, bf16[4,200,768]{2,1,0:T(8,128)(2,1)S(1)}, u32[]{:S(2)}, u32[]{:S(2)}) %collective-permute-start.24) | collective-permute-done | bytes 1228832 | tf_op jit(solution)/shard_map/ppermute | solution.py:376
  457.2 2.6 fusion.23
  459.8 4.6 collective-permute-done.25
  464.4 16.6 %collective-permute-done.26 = bf16[200,768]{1,0:T(8,128)(2,1)S(1)} collective-permute-done((bf16[200,768]{1,0:T(8,128)(2,1)S(1)}, bf16[200,768]{1,0:T(8,128)(2,1)S(1)}, u32[]{:S(2)}, u32[]{:S(2)}) %collective-permute-start.26) | collective-permute-done | bytes 307232 | tf_op jit(solution)/shard_map/ppermute | solution.py:381
  484.6 2.5 multiply_reduce_fusion
  494.8 4.2 fusion.63
  499.4 2.5 convolution_convert_fusion.1
  509.6 2.5 maximum_convert_fusion.1
  512.1 7.2 %collective-permute-done.37 = bf16[8,96,256]{2,1,0:T(8,128)(2,1)S(1)} collective-permute-done((bf16[8,96,256]{2,1,0:T(8,128)(2,1)S(1)}, bf16[8,96,256]{2,1,0:T(8,128)(2,1)S(1)}, u32[]{:S(2)}, u32[]{:S(2)}) %collective-permute-start.37) | collective-permute-done | bytes 393248 | tf_op jit(solution)/shard_map/ppermute | solution.py:410
  520.4 3.0 add_convert_fusion.1
  525.7 6.5 %collective-permute-done.38 = bf16[4,96,256]{1,2,0:T(8,128)(2,1)S(1)} collective-permute-done((bf16[4,96,256]{1,2,0:T(8,128)(2,1)S(1)}, bf16[4,96,256]{1,2,0:T(8,128)(2,1)S(1)}, u32[]{:S(2)}, u32[]{:S(2)}) %collective-permute-start.38) | collective-permute-done | bytes 196640 | tf_op jit(solution)/shard_map/ppermute | solution.py:376
  532.4 3.1 collective-permute-start.40
  537.7 8.6 %collective-permute-done.29 = bf16[8,96,640]{2,1,0:T(8,128)(2,1)S(1)} collective-permute-done((bf16[8,96,640]{2,1,0:T(8,128)(2,1)S(1)}, bf16[8,96,640]{2,1,0:T(8,128)(2,1)S(1)}, u32[]{:S(2)}, u32[]{:S(2)}) %collective-permute-start.29) | collective-permute-done | bytes 983072 | tf_op jit(solution)/shard_map/ppermute | solution.py:410
  553.1 8.2 %collective-permute-done.30 = bf16[4,96,640]{2,1,0:T(8,128)(2,1)S(1)} collective-permute-done((bf16[4,96,640]{2,1,0:T(8,128)(2,1)S(1)}, bf16[4,96,640]{2,1,0:T(8,128)(2,1)S(1)}, u32[]{:S(2)}, u32[]{:S(2)}) %collective-permute-start.30) | collective-permute-done | bytes 491552 | tf_op jit(solution)/shard_map/ppermute | solution.py:376
  561.5 3.3 collective-permute-start.32
  566.9 6.5 %collective-permute-done.32 = bf16[96,640]{1,0:T(8,128)(2,1)S(1)} collective-permute-done((bf16[96,640]{1,0:T(8,128)(2,1)S(1)}, bf16[96,640]{1,0:T(8,128)(2,1)S(1)}, u32[]{:S(2)}, u32[]{:S(2)}) %collective-permute-start.32) | collective-permute-done | bytes 122912 | tf_op jit(solution)/shard_map/ppermute | solution.py:381
  574.9 3.5 collective-permute-done.34
  (363 shorter events, 132.9 us)
Async XLA Ops:
  0.6 166.7 %copy-start = (bf16[4,96,3072]{2,1,0:T(8,128)(2,1)S(1)}, bf16[4,96,3072]{2,1,0:T(8,128)(2,1)}, u32[]{:S(2)}) copy-start(bf16[4,96,3072]{2,1,0:T(8,128)(2,1)} %param.32) | copy-start | bytes 7077892
  4.4 32.9 %collective-permute-start.1 = (bf16[96,3200]{1,0:T(8,128)(2,1)S(1)}, bf16[96,3200]{1,0:T(8,128)(2,1)S(1)}, u32[]{:S(2)}, u32[]{:S(2)}) collective-permute-start(bf16[96,3200]{1,0:T(8,128)(2,1)S(1)} %get-tuple-element.165), channel_id=1, source_target_pairs={{0,4},{1,5},{2,6},{3,7},{4,0},{5,1},{6,2},{7,3},{8,12},{9,13},{10,... | collective-permute-start | bytes 1843208 | tf_op jit(solution)/shard_map/ppermute | solution.py:363
  8.5 28.8 %collective-permute-start.2 = (bf16[96,3200]{1,0:T(8,128)(2,1)S(1)}, bf16[96,3200]{1,0:T(8,128)(2,1)S(1)}, u32[]{:S(2)}, u32[]{:S(2)}) collective-permute-start(bf16[96,3200]{1,0:T(8,128)(2,1)S(1)} %get-tuple-element.165), channel_id=1, source_target_pairs={{0,6},{1,7},{2,0},{3,1},{4,2},{5,3},{6,4},{7,5},{8,14},{9,15},{10,... | collective-permute-start | bytes 1843208 | tf_op jit(solution)/shard_map/ppermute | solution.py:363
  9.8 40.1 %collective-permute-start = (bf16[96,3200]{1,0:T(8,128)(2,1)S(1)}, bf16[96,3200]{1,0:T(8,128)(2,1)S(1)}, u32[]{:S(2)}, u32[]{:S(2)}) collective-permute-start(bf16[96,3200]{1,0:T(8,128)(2,1)S(1)} %get-tuple-element.165), channel_id=1, source_target_pairs={{0,2},{1,3},{2,4},{3,5},{4,6},{5,7},{6,0},{7,1},{8,10},{9,11},{10,... | collective-permute-start | bytes 1843208 | tf_op jit(solution)/shard_map/ppermute | solution.py:363
  49.9 28.1 %copy-start.13 = (bf16[1,200,768]{2,1,0:T(8,128)(2,1)S(1)}, bf16[1,200,768]{2,1,0:T(8,128)(2,1)}, u32[]{:S(2)}) copy-start(bf16[1,200,768]{2,1,0:T(8,128)(2,1)} %param.20) | copy-start | bytes 921604
  52.4 56.6 %collective-permute-start.3 = (bf16[4,96,3200]{2,1,0:T(8,128)(2,1)}, bf16[4,96,3200]{2,1,0:T(8,128)(2,1)}, u32[]{:S(2)}, u32[]{:S(2)}) collective-permute-start(bf16[4,96,3200]{2,1,0:T(8,128)(2,1)} %get-tuple-element.138), channel_id=1, source_target_pairs={{0,1},{1,0},{2,3},{3,2},{4,5},{5,4},{6,7},{7,6},{8,9},{9,8},{10,11... | collective-permute-start | bytes 7372808 | tf_op jit(solution)/shard_map/ppermute | solution.py:365
  54.1 205.0 %copy-start.46 = (f32[1,200]{1,0:T(1,128)}, f32[1,200]{1,0:T(1,128)S(1)}, u32[]{:S(2)}) copy-start(f32[1,200]{1,0:T(1,128)S(1)} %fusion.162) | copy-start | bytes 2404
  55.0 29.4 %collective-permute-start.9 = (bf16[200,896]{1,0:T(8,128)(2,1)}, bf16[200,896]{1,0:T(8,128)(2,1)}, u32[]{:S(2)}, u32[]{:S(2)}) collective-permute-start(bf16[200,896]{1,0:T(8,128)(2,1)} %get-tuple-element.172), channel_id=1, source_target_pairs={{0,2},{1,3},{2,4},{3,5},{4,6},{5,7},{6,0},{7,1},{8,10},{9,11},{10,... | collective-permute-start | bytes 1075208 | tf_op jit(solution)/shard_map/ppermute | solution.py:363
  75.3 17.4 %collective-permute-start.10 = (bf16[200,896]{1,0:T(8,128)(2,1)}, bf16[200,896]{1,0:T(8,128)(2,1)}, u32[]{:S(2)}, u32[]{:S(2)}) collective-permute-start(bf16[200,896]{1,0:T(8,128)(2,1)} %get-tuple-element.172), channel_id=1, source_target_pairs={{0,4},{1,5},{2,6},{3,7},{4,0},{5,1},{6,2},{7,3},{8,12},{9,13},{10,... | collective-permute-start | bytes 1075208 | tf_op jit(solution)/shard_map/ppermute | solution.py:363
  75.3 22.2 %collective-permute-start.11 = (bf16[200,896]{1,0:T(8,128)(2,1)}, bf16[200,896]{1,0:T(8,128)(2,1)}, u32[]{:S(2)}, u32[]{:S(2)}) collective-permute-start(bf16[200,896]{1,0:T(8,128)(2,1)} %get-tuple-element.172), channel_id=1, source_target_pairs={{0,6},{1,7},{2,0},{3,1},{4,2},{5,3},{6,4},{7,5},{8,14},{9,15},{10,... | collective-permute-start | bytes 1075208 | tf_op jit(solution)/shard_map/ppermute | solution.py:363
  77.7 109.3 %copy-start.55 = (pred[8]{0:T(512)(128)(4,1)}, pred[8]{0:T(512)(128)(4,1)S(1)}, u32[]{:S(2)}) copy-start(pred[8]{0:T(512)(128)(4,1)S(1)} %get-tuple-element.203) | copy-start | bytes 28
  77.7 177.9 %copy-start.53 = (pred[8]{0:T(512)(128)(4,1)}, pred[8]{0:T(512)(128)(4,1)S(1)}, u32[]{:S(2)}) copy-start(pred[8]{0:T(512)(128)(4,1)S(1)} %get-tuple-element.122) | copy-start | bytes 28
  77.9 35.4 %copy-start.50 = (s32[1024]{0:T(1024)}, s32[1024]{0:T(1024)S(1)}, u32[]{:S(2)}) copy-start(s32[1024]{0:T(1024)S(1)} %pad_clamp_fusion.2) | copy-start | bytes 12292
  78.0 31.0 %copy-start.7 = (bf16[4,1,96,3200]{3,2,1,0:T(8,128)(2,1)S(1)}, bf16[4,1,96,3200]{3,2,1,0:T(8,128)(2,1)}, u32[]{:S(2)}) copy-start(bf16[4,1,96,3200]{3,2,1,0:T(8,128)(2,1)} %get-tuple-element.137) | copy-start | bytes 7372804
  78.1 182.4 %copy-start.37 = (f32[200]{0:T(256)}, f32[200]{0:T(256)S(1)}, u32[]{:S(2)}) copy-start(f32[200]{0:T(256)S(1)} %broadcast_multiply_fusion.5) | copy-start | bytes 2404
  78.4 182.2 %copy-start.48 = (f32[200]{0:T(256)}, f32[200]{0:T(256)S(1)}, u32[]{:S(2)}) copy-start(f32[200]{0:T(256)S(1)} %add_rsqrt_fusion.1) | copy-start | bytes 2404
  100.6 87.9 %collective-permute-start.12 = (bf16[4,200,896]{2,1,0:T(8,128)(2,1)}, bf16[4,200,896]{2,1,0:T(8,128)(2,1)}, u32[]{:S(2)}, u32[]{:S(2)}) collective-permute-start(bf16[4,200,896]{2,1,0:T(8,128)(2,1)} %get-tuple-element.142), channel_id=1, source_target_pairs={{0,1},{1,0},{2,3},{3,2},{4,5},{5,4},{6,7},{7,6},{8,9},{9,8},{10,11... | collective-permute-start | bytes 4300808 | tf_op jit(solution)/shard_map/ppermute | solution.py:365
  144.3 24.2 %copy-start.35 = (f32[200]{0:T(256)}, f32[200]{0:T(256)S(1)}, u32[]{:S(2)}) copy-start(f32[200]{0:T(256)S(1)} %add_rsqrt_fusion) | copy-start | bytes 2404
  144.5 24.2 %copy-start.19 = (bf16[200,768]{1,0:T(8,128)(2,1)}, bf16[200,768]{1,0:T(8,128)(2,1)S(1)}, u32[]{:S(2)}) copy-start(bf16[200,768]{1,0:T(8,128)(2,1)S(1)} %add_convert_fusion.7) | copy-start | bytes 921604
  144.6 28.0 %collective-permute-start.4 = (bf16[200,768]{1,0:T(8,128)(2,1)S(1)}, bf16[200,768]{1,0:T(8,128)(2,1)S(1)}, u32[]{:S(2)}, u32[]{:S(2)}) collective-permute-start(bf16[200,768]{1,0:T(8,128)(2,1)S(1)} %add_convert_fusion.7), channel_id=1, source_target_pairs={{0,2},{1,3},{2,4},{3,5},{4,6},{5,7},{6,0},{7,1},{8,10},{9,11},{10,... | collective-permute-start | bytes 921608 | tf_op jit(solution)/shard_map/ppermute | solution.py:363
  164.9 14.2 %collective-permute-start.5 = (bf16[200,768]{1,0:T(8,128)(2,1)S(1)}, bf16[200,768]{1,0:T(8,128)(2,1)S(1)}, u32[]{:S(2)}, u32[]{:S(2)}) collective-permute-start(bf16[200,768]{1,0:T(8,128)(2,1)S(1)} %add_convert_fusion.7), channel_id=1, source_target_pairs={{0,4},{1,5},{2,6},{3,7},{4,0},{5,1},{6,2},{7,3},{8,12},{9,13},{10,... | collective-permute-start | bytes 921608 | tf_op jit(solution)/shard_map/ppermute | solution.py:363
  164.9 16.5 %collective-permute-start.6 = (bf16[200,768]{1,0:T(8,128)(2,1)S(1)}, bf16[200,768]{1,0:T(8,128)(2,1)S(1)}, u32[]{:S(2)}, u32[]{:S(2)}) collective-permute-start(bf16[200,768]{1,0:T(8,128)(2,1)S(1)} %add_convert_fusion.7), channel_id=1, source_target_pairs={{0,6},{1,7},{2,0},{3,1},{4,2},{5,3},{6,4},{7,5},{8,14},{9,15},{10,... | collective-permute-start | bytes 921608 | tf_op jit(solution)/shard_map/ppermute | solution.py:363
  183.0 30.3 %collective-permute-start.7 = (bf16[4,200,768]{2,1,0:T(8,128)(2,1)}, bf16[4,200,768]{2,1,0:T(8,128)(2,1)}, u32[]{:S(2)}, u32[]{:S(2)}) collective-permute-start(bf16[4,200,768]{2,1,0:T(8,128)(2,1)} %get-tuple-element.150), channel_id=1, source_target_pairs={{0,1},{1,0},{2,3},{3,2},{4,5},{5,4},{6,7},{7,6},{8,9},{9,8},{10,11... | collective-permute-start | bytes 3686408 | tf_op jit(solution)/shard_map/ppermute | solution.py:365
  192.8 70.7 %collective-permute-start.13 = (bf16[4,2,200,896]{3,2,0,1:T(8,128)(2,1)}, bf16[4,2,200,896]{3,2,0,1:T(8,128)(2,1)}, u32[]{:S(2)}, u32[]{:S(2)}) collective-permute-start(bf16[4,2,200,896]{3,2,0,1:T(8,128)(2,1)} %get-tuple-element.132), channel_id=1, source_target_pairs={{0,8},{8,0},{16,24},{24,16},{1,9},{9,1},{17,25},{25,17},{2,10},{10... | collective-permute-start | bytes 8601608 | tf_op jit(solution)/shard_map/ppermute | solution.py:371
  192.9 27.6 %collective-permute-start.14 = (bf16[4,2,96,384]{3,2,1,0:T(8,128)(2,1)S(1)}, bf16[4,2,96,384]{3,2,1,0:T(8,128)(2,1)S(1)}, u32[]{:S(2)}, u32[]{:S(2)}) collective-permute-start(bf16[4,2,96,384]{3,2,1,0:T(8,128)(2,1)S(1)} %get-tuple-element.162), channel_id=1, source_target_pairs={{0,1},{1,0},{2,3},{3,2},{4,5},{5,4},{6,7},{7,6},{8,9},{9,8},{10,11... | collective-permute-start | bytes 1769480 | tf_op jit(solution)/shard_map/ppermute | solution.py:505
  194.1 102.7 %copy-start.63 = (s32[2]{0:T(128)}, s32[2]{0:T(128)S(1)}, u32[]{:S(2)}) copy-start(s32[2]{0:T(128)S(1)} %iota_add_fusion) | copy-start | bytes 28
  217.2 52.1 %collective-permute-start.8 = (bf16[4,2,200,768]{3,2,0,1:T(8,128)(2,1)}, bf16[4,2,200,768]{3,2,0,1:T(8,128)(2,1)}, u32[]{:S(2)}, u32[]{:S(2)}) collective-permute-start(bf16[4,2,200,768]{3,2,0,1:T(8,128)(2,1)} %get-tuple-element.136), channel_id=1, source_target_pairs={{0,8},{8,0},{16,24},{24,16},{1,9},{9,1},{17,25},{25,17},{2,10},{10... | collective-permute-start | bytes 7372808 | tf_op jit(solution)/shard_map/ppermute | solution.py:371
  220.7 17.1 %collective-permute-start.15 = (bf16[2,2,96,384]{3,2,1,0:T(8,128)(2,1)S(1)}, bf16[2,2,96,384]{3,2,1,0:T(8,128)(2,1)S(1)}, u32[]{:S(2)}, u32[]{:S(2)}) collective-permute-start(bf16[2,2,96,384]{3,2,1,0:T(8,128)(2,1)S(1)} %get-tuple-element.158), channel_id=1, source_target_pairs={{0,6},{1,7},{2,0},{3,1},{4,2},{5,3},{6,4},{7,5},{8,14},{9,15},{10,... | collective-permute-start | bytes 884744 | tf_op jit(solution)/shard_map/ppermute | solution.py:508
  230.3 22.5 %collective-permute-start.16 = (bf16[2,2,96,384]{3,2,1,0:T(8,128)(2,1)S(1)}, bf16[2,2,96,384]{3,2,1,0:T(8,128)(2,1)S(1)}, u32[]{:S(2)}, u32[]{:S(2)}) collective-permute-start(bf16[2,2,96,384]{3,2,1,0:T(8,128)(2,1)S(1)} %get-tuple-element.160), channel_id=1, source_target_pairs={{0,4},{1,5},{2,6},{3,7},{4,0},{5,1},{6,2},{7,3},{8,12},{9,13},{10,... | collective-permute-start | bytes 884744 | tf_op jit(solution)/shard_map/ppermute | solution.py:508
  230.3 22.5 %collective-permute-start.17 = (bf16[2,2,96,384]{3,2,1,0:T(8,128)(2,1)S(1)}, bf16[2,2,96,384]{3,2,1,0:T(8,128)(2,1)S(1)}, u32[]{:S(2)}, u32[]{:S(2)}) collective-permute-start(bf16[2,2,96,384]{3,2,1,0:T(8,128)(2,1)S(1)} %get-tuple-element.159), channel_id=1, source_target_pairs={{0,2},{1,3},{2,4},{3,5},{4,6},{5,7},{6,0},{7,1},{8,10},{9,11},{10,... | collective-permute-start | bytes 884744 | tf_op jit(solution)/shard_map/ppermute | solution.py:508
  343.8 18.4 %collective-permute-start.44 = (bf16[4,96,2,384]{3,1,2,0:T(8,128)(2,1)S(1)}, bf16[4,96,2,384]{3,1,2,0:T(8,128)(2,1)S(1)}, u32[]{:S(2)}, u32[]{:S(2)}) collective-permute-start(bf16[4,96,2,384]{3,1,2,0:T(8,128)(2,1)S(1)} %bitcast.399), channel_id=1, source_target_pairs={{0,1},{1,0},{2,3},{3,2},{4,5},{5,4},{6,7},{7,6},{8,9},{9,8},{10,11... | collective-permute-start | bytes 1769480 | tf_op jit(solution)/shard_map/ppermute | solution.py:648
  350.3 45.2 %collective-permute-start.18 = (bf16[4,2,200,768]{3,2,0,1:T(8,128)(2,1)}, bf16[4,2,200,768]{3,2,0,1:T(8,128)(2,1)}, u32[]{:S(2)}, u32[]{:S(2)}) collective-permute-start(bf16[4,2,200,768]{3,2,0,1:T(8,128)(2,1)} %copy.204), channel_id=1, source_target_pairs={{0,8},{8,0},{16,24},{24,16},{1,9},{9,1},{17,25},{25,17},{2,10},{10... | collective-permute-start | bytes 7372808 | tf_op jit(solution)/shard_map/ppermute | solution.py:386
  359.0 39.9 %collective-permute-start.23 = (bf16[4,2,200,768]{3,2,0,1:T(8,128)(2,1)}, bf16[4,2,200,768]{3,2,0,1:T(8,128)(2,1)}, u32[]{:S(2)}, u32[]{:S(2)}) collective-permute-start(bf16[4,2,200,768]{3,2,0,1:T(8,128)(2,1)} %copy.206), channel_id=1, source_target_pairs={{0,8},{8,0},{16,24},{24,16},{1,9},{9,1},{17,25},{25,17},{2,10},{10... | collective-permute-start | bytes 7372808 | tf_op jit(solution)/shard_map/ppermute | solution.py:386
  360.6 32.9 %collective-permute-start.50 = (bf16[2,400,768]{2,1,0:T(8,128)(2,1)}, bf16[2,400,768]{2,1,0:T(8,128)(2,1)}, u32[]{:S(2)}, u32[]{:S(2)}) collective-permute-start(bf16[2,400,768]{2,1,0:T(8,128)(2,1)} %fusion.37), channel_id=1, source_target_pairs={{0,16},{8,24},{16,0},{24,8},{1,17},{9,25},{17,1},{25,9},{2,18},{10... | collective-permute-start | bytes 3686408 | tf_op jit(solution)/shard_map/ppermute | solution.py:644
  362.4 8.8 %collective-permute-start.45 = (bf16[2,96,2,384]{3,1,2,0:T(8,128)(2,1)S(1)}, bf16[2,96,2,384]{3,1,2,0:T(8,128)(2,1)S(1)}, u32[]{:S(2)}, u32[]{:S(2)}) collective-permute-start(bf16[2,96,2,384]{3,1,2,0:T(8,128)(2,1)S(1)} %get-tuple-element.152), channel_id=1, source_target_pairs={{0,6},{1,7},{2,0},{3,1},{4,2},{5,3},{6,4},{7,5},{8,14},{9,15},{10,... | collective-permute-start | bytes 884744 | tf_op jit(solution)/shard_map/ppermute | solution.py:651
  365.8 25.6 %collective-permute-start.46 = (bf16[2,96,2,384]{3,1,2,0:T(8,128)(2,1)S(1)}, bf16[2,96,2,384]{3,1,2,0:T(8,128)(2,1)S(1)}, u32[]{:S(2)}, u32[]{:S(2)}) collective-permute-start(bf16[2,96,2,384]{3,1,2,0:T(8,128)(2,1)S(1)} %get-tuple-element.154), channel_id=1, source_target_pairs={{0,4},{1,5},{2,6},{3,7},{4,0},{5,1},{6,2},{7,3},{8,12},{9,13},{10,... | collective-permute-start | bytes 884744 | tf_op jit(solution)/shard_map/ppermute | solution.py:651
  371.2 20.2 %collective-permute-start.47 = (bf16[2,96,2,384]{3,1,2,0:T(8,128)(2,1)S(1)}, bf16[2,96,2,384]{3,1,2,0:T(8,128)(2,1)S(1)}, u32[]{:S(2)}, u32[]{:S(2)}) collective-permute-start(bf16[2,96,2,384]{3,1,2,0:T(8,128)(2,1)S(1)} %get-tuple-element.153), channel_id=1, source_target_pairs={{0,2},{1,3},{2,4},{3,5},{4,6},{5,7},{6,0},{7,1},{8,10},{9,11},{10,... | collective-permute-start | bytes 884744 | tf_op jit(solution)/shard_map/ppermute | solution.py:651
  393.0 27.2 %collective-permute-start.48 = (bf16[2,96,3072]{2,1,0:T(8,128)(2,1)S(1)}, bf16[2,96,3072]{2,1,0:T(8,128)(2,1)S(1)}, u32[]{:S(2)}, u32[]{:S(2)}) collective-permute-start(bf16[2,96,3072]{2,1,0:T(8,128)(2,1)S(1)} %bitcast.367), channel_id=1, source_target_pairs={{0,16},{8,24},{16,0},{24,8},{1,17},{9,25},{17,1},{25,9},{2,18},{10... | collective-permute-start | bytes 3538952 | tf_op jit(solution)/shard_map/ppermute | solution.py:655
  395.4 26.3 %collective-permute-start.51 = (bf16[2,400,768]{2,1,0:T(8,128)(2,1)S(1)}, bf16[2,400,768]{2,1,0:T(8,128)(2,1)S(1)}, u32[]{:S(2)}, u32[]{:S(2)}) collective-permute-start(bf16[2,400,768]{2,1,0:T(8,128)(2,1)S(1)} %add_convert_fusion.2), channel_id=1, source_target_pairs={{0,8},{8,0},{16,24},{24,16},{1,9},{9,1},{17,25},{25,17},{2,10},{10... | collective-permute-start | bytes 3686408 | tf_op jit(solution)/shard_map/ppermute | solution.py:635
  398.0 29.9 %collective-permute-start.19 = (bf16[4,200,768]{2,1,0:T(8,128)(2,1)S(1)}, bf16[4,200,768]{2,1,0:T(8,128)(2,1)S(1)}, u32[]{:S(2)}, u32[]{:S(2)}) collective-permute-start(bf16[4,200,768]{2,1,0:T(8,128)(2,1)S(1)} %slice_bitcast_fusion.2), channel_id=1, source_target_pairs={{0,1},{1,0},{2,3},{3,2},{4,5},{5,4},{6,7},{7,6},{8,9},{9,8},{10,11... | collective-permute-start | bytes 3686408 | tf_op jit(solution)/shard_map/ppermute | solution.py:376
  402.1 51.7 %collective-permute-start.24 = (bf16[4,200,768]{2,1,0:T(8,128)(2,1)S(1)}, bf16[4,200,768]{2,1,0:T(8,128)(2,1)S(1)}, u32[]{:S(2)}, u32[]{:S(2)}) collective-permute-start(bf16[4,200,768]{2,1,0:T(8,128)(2,1)S(1)} %slice_bitcast_fusion), channel_id=1, source_target_pairs={{0,1},{1,0},{2,3},{3,2},{4,5},{5,4},{6,7},{7,6},{8,9},{9,8},{10,11... | collective-permute-start | bytes 3686408 | tf_op jit(solution)/shard_map/ppermute | solution.py:376
  428.3 26.1 %collective-permute-start.20 = (bf16[200,768]{1,0:T(8,128)(2,1)S(1)}, bf16[200,768]{1,0:T(8,128)(2,1)S(1)}, u32[]{:S(2)}, u32[]{:S(2)}) collective-permute-start(bf16[200,768]{1,0:T(8,128)(2,1)S(1)} %get-tuple-element.146), channel_id=1, source_target_pairs={{0,6},{1,7},{2,0},{3,1},{4,2},{5,3},{6,4},{7,5},{8,14},{9,15},{10,... | collective-permute-start | bytes 921608 | tf_op jit(solution)/shard_map/ppermute | solution.py:381
  428.4 31.4 %collective-permute-start.21 = (bf16[200,768]{1,0:T(8,128)(2,1)S(1)}, bf16[200,768]{1,0:T(8,128)(2,1)S(1)}, u32[]{:S(2)}, u32[]{:S(2)}) collective-permute-start(bf16[200,768]{1,0:T(8,128)(2,1)S(1)} %get-tuple-element.148), channel_id=1, source_target_pairs={{0,4},{1,5},{2,6},{3,7},{4,0},{5,1},{6,2},{7,3},{8,12},{9,13},{10,... | collective-permute-start | bytes 921608 | tf_op jit(solution)/shard_map/ppermute | solution.py:381
  428.5 31.3 %collective-permute-start.22 = (bf16[200,768]{1,0:T(8,128)(2,1)S(1)}, bf16[200,768]{1,0:T(8,128)(2,1)S(1)}, u32[]{:S(2)}, u32[]{:S(2)}) collective-permute-start(bf16[200,768]{1,0:T(8,128)(2,1)S(1)} %get-tuple-element.147), channel_id=1, source_target_pairs={{0,2},{1,3},{2,4},{3,5},{4,6},{5,7},{6,0},{7,1},{8,10},{9,11},{10,... | collective-permute-start | bytes 921608 | tf_op jit(solution)/shard_map/ppermute | solution.py:381
  454.2 10.2 %collective-permute-start.25 = (bf16[200,768]{1,0:T(8,128)(2,1)S(1)}, bf16[200,768]{1,0:T(8,128)(2,1)S(1)}, u32[]{:S(2)}, u32[]{:S(2)}) collective-permute-start(bf16[200,768]{1,0:T(8,128)(2,1)S(1)} %get-tuple-element.143), channel_id=1, source_target_pairs={{0,6},{1,7},{2,0},{3,1},{4,2},{5,3},{6,4},{7,5},{8,14},{9,15},{10,... | collective-permute-start | bytes 921608 | tf_op jit(solution)/shard_map/ppermute | solution.py:381
  454.3 26.7 %collective-permute-start.26 = (bf16[200,768]{1,0:T(8,128)(2,1)S(1)}, bf16[200,768]{1,0:T(8,128)(2,1)S(1)}, u32[]{:S(2)}, u32[]{:S(2)}) collective-permute-start(bf16[200,768]{1,0:T(8,128)(2,1)S(1)} %get-tuple-element.145), channel_id=1, source_target_pairs={{0,4},{1,5},{2,6},{3,7},{4,0},{5,1},{6,2},{7,3},{8,12},{9,13},{10,... | collective-permute-start | bytes 921608 | tf_op jit(solution)/shard_map/ppermute | solution.py:381
  454.4 26.6 %collective-permute-start.27 = (bf16[200,768]{1,0:T(8,128)(2,1)S(1)}, bf16[200,768]{1,0:T(8,128)(2,1)S(1)}, u32[]{:S(2)}, u32[]{:S(2)}) collective-permute-start(bf16[200,768]{1,0:T(8,128)(2,1)S(1)} %get-tuple-element.144), channel_id=1, source_target_pairs={{0,2},{1,3},{2,4},{3,5},{4,6},{5,7},{6,0},{7,1},{8,10},{9,11},{10,... | collective-permute-start | bytes 921608 | tf_op jit(solution)/shard_map/ppermute | solution.py:381
  459.8 45.0 %collective-permute-start.49 = (bf16[2,96,3072]{2,1,0:T(8,128)(2,1)}, bf16[2,96,3072]{2,1,0:T(8,128)(2,1)}, u32[]{:S(2)}, u32[]{:S(2)}) collective-permute-start(bf16[2,96,3072]{2,1,0:T(8,128)(2,1)} %add_convert_fusion.3), channel_id=1, source_target_pairs={{0,8},{8,0},{16,24},{24,16},{1,9},{9,1},{17,25},{25,17},{2,10},{10... | collective-permute-start | bytes 3538952 | tf_op jit(solution)/shard_map/ppermute | solution.py:635
  494.5 12.1 %collective-permute-start.36 = (bf16[8,96,512]{2,1,0:T(8,128)(2,1)}, bf16[8,96,512]{2,1,0:T(8,128)(2,1)}, u32[]{:S(2)}, u32[]{:S(2)}) collective-permute-start(bf16[8,96,512]{2,1,0:T(8,128)(2,1)} %fusion.46), channel_id=1, source_target_pairs={{0,8},{8,0},{16,24},{24,16},{1,9},{9,1},{17,25},{25,17},{2,10},{10... | collective-permute-start | bytes 2359304 | tf_op jit(solution)/shard_map/ppermute | solution.py:406
  504.3 16.1 %collective-permute-start.28 = (bf16[8,96,1280]{2,1,0:T(8,128)(2,1)}, bf16[8,96,1280]{2,1,0:T(8,128)(2,1)}, u32[]{:S(2)}, u32[]{:S(2)}) collective-permute-start(bf16[8,96,1280]{2,1,0:T(8,128)(2,1)} %fusion.25), channel_id=1, source_target_pairs={{0,8},{8,0},{16,24},{24,16},{1,9},{9,1},{17,25},{25,17},{2,10},{10... | collective-permute-start | bytes 5898248 | tf_op jit(solution)/shard_map/ppermute | solution.py:406
  508.1 11.1 %collective-permute-start.37 = (bf16[8,96,256]{2,1,0:T(8,128)(2,1)S(1)}, bf16[8,96,256]{2,1,0:T(8,128)(2,1)S(1)}, u32[]{:S(2)}, u32[]{:S(2)}) collective-permute-start(bf16[8,96,256]{2,1,0:T(8,128)(2,1)S(1)} %constant_dynamic-slice_fusion), channel_id=1, source_target_pairs={{0,16},{8,24},{16,0},{24,8},{1,17},{9,25},{17,1},{25,9},{2,18},{10... | collective-permute-start | bytes 1179656 | tf_op jit(solution)/shard_map/ppermute | solution.py:410
  523.5 22.8 %collective-permute-start.29 = (bf16[8,96,640]{2,1,0:T(8,128)(2,1)S(1)}, bf16[8,96,640]{2,1,0:T(8,128)(2,1)S(1)}, u32[]{:S(2)}, u32[]{:S(2)}) collective-permute-start(bf16[8,96,640]{2,1,0:T(8,128)(2,1)S(1)} %constant_dynamic-slice_fusion.1), channel_id=1, source_target_pairs={{0,16},{8,24},{16,0},{24,8},{1,17},{9,25},{17,1},{25,9},{2,18},{10... | collective-permute-start | bytes 2949128 | tf_op jit(solution)/shard_map/ppermute | solution.py:410
  525.1 7.1 %collective-permute-start.38 = (bf16[4,96,256]{1,2,0:T(8,128)(2,1)S(1)}, bf16[4,96,256]{1,2,0:T(8,128)(2,1)S(1)}, u32[]{:S(2)}, u32[]{:S(2)}) collective-permute-start(bf16[4,96,256]{1,2,0:T(8,128)(2,1)S(1)} %slice_bitcast_fusion.24), channel_id=1, source_target_pairs={{0,1},{1,0},{2,3},{3,2},{4,5},{5,4},{6,7},{7,6},{8,9},{9,8},{10,11... | collective-permute-start | bytes 589832 | tf_op jit(solution)/shard_map/ppermute | solution.py:376
  532.3 20.0 %collective-permute-start.39 = (bf16[96,256]{0,1:T(8,128)(2,1)S(1)}, bf16[96,256]{0,1:T(8,128)(2,1)S(1)}, u32[]{:S(2)}, u32[]{:S(2)}) collective-permute-start(bf16[96,256]{0,1:T(8,128)(2,1)S(1)} %get-tuple-element.180), channel_id=1, source_target_pairs={{0,6},{1,7},{2,0},{3,1},{4,2},{5,3},{6,4},{7,5},{8,14},{9,15},{10,... | collective-permute-start | bytes 147464 | tf_op jit(solution)/shard_map/ppermute | solution.py:381
  532.4 19.9 %collective-permute-start.40 = (bf16[96,256]{0,1:T(8,128)(2,1)S(1)}, bf16[96,256]{0,1:T(8,128)(2,1)S(1)}, u32[]{:S(2)}, u32[]{:S(2)}) collective-permute-start(bf16[96,256]{0,1:T(8,128)(2,1)S(1)} %get-tuple-element.182), channel_id=1, source_target_pairs={{0,4},{1,5},{2,6},{3,7},{4,0},{5,1},{6,2},{7,3},{8,12},{9,13},{10,... | collective-permute-start | bytes 147464 | tf_op jit(solution)/shard_map/ppermute | solution.py:381
  535.5 16.8 %collective-permute-start.41 = (bf16[96,256]{0,1:T(8,128)(2,1)S(1)}, bf16[96,256]{0,1:T(8,128)(2,1)S(1)}, u32[]{:S(2)}, u32[]{:S(2)}) collective-permute-start(bf16[96,256]{0,1:T(8,128)(2,1)S(1)} %get-tuple-element.181), channel_id=1, source_target_pairs={{0,2},{1,3},{2,4},{3,5},{4,6},{5,7},{6,0},{7,1},{8,10},{9,11},{10,... | collective-permute-start | bytes 147464 | tf_op jit(solution)/shard_map/ppermute | solution.py:381
  549.9 11.3 %collective-permute-start.30 = (bf16[4,96,640]{2,1,0:T(8,128)(2,1)S(1)}, bf16[4,96,640]{2,1,0:T(8,128)(2,1)S(1)}, u32[]{:S(2)}, u32[]{:S(2)}) collective-permute-start(bf16[4,96,640]{2,1,0:T(8,128)(2,1)S(1)} %slice_bitcast_fusion.5), channel_id=1, source_target_pairs={{0,1},{1,0},{2,3},{3,2},{4,5},{5,4},{6,7},{7,6},{8,9},{9,8},{10,11... | collective-permute-start | bytes 1474568 | tf_op jit(solution)/shard_map/ppermute | solution.py:376
  552.3 14.4 %collective-permute-start.42 = (bf16[96,256]{0,1:T(8,128)(2,1)S(1)}, bf16[96,256]{0,1:T(8,128)(2,1)S(1)}, u32[]{:S(2)}, u32[]{:S(2)}) collective-permute-start(bf16[96,256]{0,1:T(8,128)(2,1)S(1)} %fusion.119), channel_id=1, source_target_pairs={{0,16},{8,24},{16,0},{24,8},{1,17},{9,25},{17,1},{25,9},{2,18},{10... | collective-permute-start | bytes 147464 | tf_op jit(solution)/shard_map/ppermute | solution.py:414
  561.4 5.4 collective-permute-start.31
  561.5 11.8 %collective-permute-start.32 = (bf16[96,640]{1,0:T(8,128)(2,1)S(1)}, bf16[96,640]{1,0:T(8,128)(2,1)S(1)}, u32[]{:S(2)}, u32[]{:S(2)}) collective-permute-start(bf16[96,640]{1,0:T(8,128)(2,1)S(1)} %get-tuple-element.170), channel_id=1, source_target_pairs={{0,4},{1,5},{2,6},{3,7},{4,0},{5,1},{6,2},{7,3},{8,12},{9,13},{10,... | collective-permute-start | bytes 368648 | tf_op jit(solution)/shard_map/ppermute | solution.py:381
  564.8 8.6 %collective-permute-start.33 = (bf16[96,640]{1,0:T(8,128)(2,1)S(1)}, bf16[96,640]{1,0:T(8,128)(2,1)S(1)}, u32[]{:S(2)}, u32[]{:S(2)}) collective-permute-start(bf16[96,640]{1,0:T(8,128)(2,1)S(1)} %get-tuple-element.169), channel_id=1, source_target_pairs={{0,2},{1,3},{2,4},{3,5},{4,6},{5,7},{6,0},{7,1},{8,10},{9,11},{10,... | collective-permute-start | bytes 368648 | tf_op jit(solution)/shard_map/ppermute | solution.py:381
  566.8 8.0 %collective-permute-start.43 = (bf16[96,512]{0,1:T(8,128)(2,1)S(1)}, bf16[96,512]{0,1:T(8,128)(2,1)S(1)}, u32[]{:S(2)}, u32[]{:S(2)}) collective-permute-start(bf16[96,512]{0,1:T(8,128)(2,1)S(1)} %pad_maximum_fusion.15), channel_id=1, source_target_pairs={{0,8},{8,0},{16,24},{24,16},{1,9},{9,1},{17,25},{25,17},{2,10},{10... | collective-permute-start | bytes 294920 | tf_op jit(solution)/shard_map/ppermute | solution.py:417
  573.4 4.9 collective-permute-start.34
  579.1 2.1 collective-permute-start.35
  (56 other events, 396.6 us)

commit v2 on v1

--- a/solution.py
+++ b/solution.py
@@ -1,6 +1,10 @@
+import functools
+
 import jax
 import jax.numpy as jnp
 from jax import lax
+from jax.experimental import pallas as pl
+from jax.experimental.pallas import tpu as pltpu
 from jax.sharding import PartitionSpec as P
 
 HEADS = 12
@@ -368,7 +372,7 @@
 
 def gather_plane(block, planes):
     mine = gather_fsdp(block, planes)
-    return jnp.stack([mine, lax.ppermute(mine, "seq", core_swap)])
+    return jnp.stack([mine, lax.ppermute(mine, "seq", core_swap)], axis=1)
 
 
 def scatter_fsdp(parts, planes):
@@ -383,8 +387,8 @@
 
 
 def scatter_plane(parts, planes):
-    other = lax.ppermute(parts[1], "seq", core_swap)
-    mine = (parts[0].astype(jnp.float32) + other.astype(jnp.float32)).astype(jnp.bfloat16)
+    other = lax.ppermute(parts[:, 1], "seq", core_swap)
+    mine = (parts[:, 0].astype(jnp.float32) + other.astype(jnp.float32)).astype(jnp.bfloat16)
     return scatter_fsdp(mine, planes)
 
 
@@ -417,6 +421,287 @@
     other = lax.ppermute(total, "seq", core_swap)
     first, second = jnp.where(c == 0, total, other), jnp.where(c == 0, other, total)
     return jnp.concatenate([first, second], axis=1).astype(jnp.float32)
+
+
+MESH = pl.DeviceIdType.MESH
+NT = (((1,), (1,)), ((), ()))
+TN = (((0,), (0,)), ((), ()))
+
+
+def dot(a, b):
+    return jnp.dot(a, b, preferred_element_type=jnp.float32)
+
+
+class Place:
+    def __init__(self, planes):
+        self.planes = planes
+        s, f = lax.axis_index("seq"), lax.axis_index("fsdp")
+        self.y, self.c, self.z, self.x = s // 2, s % 2, f // 2, f % 2
+
+    def at(self, y, c, z, x):
+        return (y * 2 + c, z * 2 + x)
+
+    def other_core(self):
+        return self.at(self.y, 1 - self.c, self.z, self.x)
+
+    def other_x(self):
+        return self.at(self.y, self.c, self.z, 1 - self.x)
+
+    def other_y(self):
+        return self.at(1 - self.y, self.c, self.z, self.x)
+
+    def level(self, k):
+        return self.at(self.y, self.c, lax.rem(self.z + k + self.planes, self.planes), self.x)
+
+
+def greet(partners):
+    barrier = pltpu.get_barrier_semaphore()
+    for partner in partners:
+        pl.semaphore_signal(barrier, inc=1, device_id=partner, device_id_type=MESH)
+    pl.semaphore_wait(barrier, len(partners))
+
+
+def expert_kernel(
+    planes,
+    own,
+    rows,
+    normed_ref,
+    grads_ref,
+    select_ref,
+    inner_ref,
+    inner_t_ref,
+    outer_ref,
+    outer_t_ref,
+    bias_ref,
+    router_ref,
+    router_t_ref,
+    mix_ref,
+    out_ref,
+    inner_grad_ref,
+    outer_grad_ref,
+    bias_grad_ref,
+    router_grad_ref,
+    tokens,
+    part,
+    from_core,
+    from_x,
+    from_z,
+    hidden,
+    hidden_grad,
+    logit_grad,
+    inner_acc,
+    outer_acc,
+    z_send,
+    z_recv,
+    x_send,
+    x_recv,
+    c_send,
+    c_recv,
+    sum_c_send,
+    sum_c_recv,
+    sum_x_send,
+    sum_x_recv,
+    sum_z_send,
+    sum_z_recv,
+):
+    f32, bf16 = jnp.float32, jnp.bfloat16
+    place = Place(planes)
+    width = normed_ref.shape[1]
+    lanes = inner_ref.shape[1] // own
+
+    def remote(src, dst, send, recv, device):
+        return pltpu.make_async_remote_copy(
+            src_ref=src, dst_ref=dst, send_sem=send, recv_sem=recv, device_id=device, device_id_type=MESH
+        )
+
+    def slot(buffer, k, at, count=1):
+        return buffer.at[k, pl.ds(at * rows, count * rows)]
+
+    def z_copy(k):
+        return remote(slot(tokens, 0, 0), slot(tokens, k, 0), z_send.at[k], z_recv.at[k], place.level(k))
+
+    def x_copy(k):
+        return remote(slot(tokens, k, 0), slot(tokens, k, 1), x_send.at[k], x_recv.at[k], place.other_x())
+
+    def c_copy(k, r):
+        return remote(
+            slot(tokens, k, r), slot(tokens, k, 2 + r), c_send.at[k, r], c_recv.at[k, r], place.other_core()
+        )
+
+    def sum_c_copy(k):
+        return remote(slot(part, k, 2, 2), from_core.at[k], sum_c_send.at[k], sum_c_recv.at[k], place.other_core())
+
+    def sum_x_copy(k):
+        return remote(slot(part, k, 1), from_x.at[k], sum_x_send.at[k], sum_x_recv.at[k], place.other_x())
+
+    def sum_z_copy(k):
+        return remote(slot(part, k, 0), from_z.at[k], sum_z_send.at[k], sum_z_recv.at[k], place.level(-k))
+
+    greet([place.other_core(), place.other_x()] + [place.level(k) for k in range(1, planes)])
+    tokens[0, 0:rows, :] = normed_ref[...]
+    c_copy(0, 0).start()
+    x_copy(0).start()
+    for k in range(1, planes):
+        z_copy(k).start()
+    inner_acc[...] = jnp.zeros_like(inner_acc)
+    outer_acc[...] = jnp.zeros_like(outer_acc)
+    bias_grad_ref[...] = jnp.zeros_like(bias_grad_ref)
+    router_grad_ref[...] = jnp.zeros_like(router_grad_ref)
+
+    def tile(k, t):
+        here = pl.ds(pl.multiple_of(t * rows, 16), rows)
+        normed, grad_out = tokens[k, here, :], grads_ref[k, here, :]
+        select = select_ref[k, here, :].astype(f32)
+        lane = lax.broadcasted_iota(jnp.int32, select.shape, 1)
+        logits = dot(normed, router_ref[...])
+        logits = jnp.where(lane < 2 * own, logits, -1e30)
+        routing = jnp.exp(logits - jnp.max(logits, axis=1, keepdims=True))
+        routing = routing / jnp.sum(routing, axis=1, keepdims=True)
+        gates = routing * select
+        gate_grads = jnp.zeros_like(gates)
+        for i in range(own):
+            mine = lane == place.c * own + i
+            units = slice(i * lanes, (i + 1) * lanes)
+            gate = jnp.sum(jnp.where(mine, gates, 0.0), axis=1, keepdims=True)
+            pre = dot(normed, inner_ref[:, units]) + bias_ref[:, units]
+            grad_act = dot(grad_out, outer_t_ref[:, units])
+            cdf = 0.5 * (1.0 + lax.erf(pre * (0.5**0.5)))
+            act = pre * cdf
+            hidden[here, units] = (gate * act).astype(bf16)
+            gate_grad = jnp.sum(act * grad_act, axis=1, keepdims=True)
+            gate_grads = gate_grads + jnp.where(mine, gate_grad * select, 0.0)
+            slope = cdf + pre * jnp.exp(-0.5 * pre * pre) * 0.3989422804014327
+            grad_pre = gate * grad_act * slope
+            bias_grad_ref[:, units] += jnp.sum(grad_pre, axis=0, keepdims=True)
+            hidden_grad[here, units] = grad_pre.astype(bf16)
+        grad_logits = routing * (gate_grads - jnp.sum(routing * gate_grads, axis=1, keepdims=True))
+        logit_grad[here, :] = grad_logits.astype(bf16)
+        mix_ref[k, here, :] = dot(hidden[here, :], outer_ref[...]).astype(bf16)
+        row_grad = dot(hidden_grad[here, :], inner_t_ref[...])
+        row_grad = row_grad + dot(logit_grad[here, :], router_t_ref[...])
+        part[k, here, :] = row_grad.astype(bf16)
+
+    def add_core(k):
+        sum_c_copy(k).wait_recv()
+        total = slot(part, k, 1)[...].astype(f32) + from_core[k, rows : 2 * rows, :].astype(f32)
+        part[k, rows : 2 * rows, :] = total.astype(bf16)
+        sum_x_copy(k).start()
+
+    def add_x(k):
+        sum_x_copy(k).wait_recv()
+        total = part[k, 0:rows, :].astype(f32) + from_core[k, 0:rows, :].astype(f32)
+        total = total + from_x[k].astype(f32)
+        part[k, 0:rows, :] = total.astype(bf16)
+
+        @pl.when(k > 0)
+        def _():
+            sum_z_copy(k).start()
+
+    def step(k, carry):
+        x_copy(k).wait_recv()
+        c_copy(k, 1).start()
+
+        @pl.when(k + 1 < planes)
+        def _():
+            z_copy(k + 1).wait_recv()
+            c_copy(k + 1, 0).start()
+            x_copy(k + 1).start()
+
+        c_copy(k, 0).wait_recv()
+        c_copy(k, 1).wait_recv()
+
+        def one(t, carry):
+            tile(k, t)
+            return carry
+
+        lax.fori_loop(0, 4, one, 0)
+        sum_c_copy(k).start()
+
+        @pl.when(k > 0)
+        def _():
+            add_core(k - 1)
+
+        @pl.when(k > 1)
+        def _():
+            add_x(k - 2)
+
+        def columns(j, carry):
+            some = pl.ds(pl.multiple_of(j * 256, 256), 256)
+            outer_acc[:, some] += lax.dot_general(
+                hidden[...], grads_ref[k, :, some], TN, preferred_element_type=f32
+            )
+            inner_acc[:, some] += lax.dot_general(
+                tokens[k], hidden_grad[:, some], TN, preferred_element_type=f32
+            )
+            return carry
+
+        lax.fori_loop(0, width // 256, columns, 0)
+        router_grad_ref[...] += lax.dot_general(tokens[k], logit_grad[...], TN, preferred_element_type=f32)
+        return carry
+
+    lax.fori_loop(0, planes, step, 0)
+    add_core(planes - 1)
+    add_x(planes - 2)
+    add_x(planes - 1)
+    inner_grad_ref[...] = inner_acc[...].astype(bf16)
+    outer_grad_ref[...] = outer_acc[...].astype(bf16)
+    total = part[0, 0:rows, :].astype(f32)
+    for k in range(1, planes):
+        sum_z_copy(k).wait_recv()
+        total = total + from_z[k].astype(f32)
+    out_ref[...] = total
+    for k in range(planes):
+        x_copy(k).wait_send()
+        c_copy(k, 0).wait_send()
+        c_copy(k, 1).wait_send()
+        sum_c_copy(k).wait_send()
+        sum_x_copy(k).wait_send()
+        if k > 0:
+            z_copy(k).wait_send()
+            sum_z_copy(k).wait_send()
+
+
+def experts_of_the_plane(planes, own, normed, grads, select, inner, outer, bias, router):
+    f32, bf16 = jnp.float32, jnp.bfloat16
+    rows, width = normed.shape
+    chunk = 4 * rows
+    units = inner.shape[1]
+    vmem = pl.BlockSpec(memory_space=pltpu.VMEM)
+    dma = pltpu.SemaphoreType.DMA
+    flops = 12 * planes * chunk * width * units
+    return pl.pallas_call(
+        functools.partial(expert_kernel, planes, own, rows),
+        out_shape=[
+            jax.ShapeDtypeStruct((planes, chunk, width), bf16),
+            jax.ShapeDtypeStruct((rows, width), f32),
+            jax.ShapeDtypeStruct((width, units), bf16),
+            jax.ShapeDtypeStruct((units, width), bf16),
+            jax.ShapeDtypeStruct((1, units), f32),
+            jax.ShapeDtypeStruct((width, 128), f32),
+        ],
+        in_specs=[vmem] * 10,
+        out_specs=[vmem] * 6,
+        scratch_shapes=[
+            pltpu.VMEM((planes, chunk, width), bf16),
+            pltpu.VMEM((planes, chunk, width), bf16),
+            pltpu.VMEM((planes, 2 * rows, width), bf16),
+            pltpu.VMEM((planes, rows, width), bf16),
+            pltpu.VMEM((planes, rows, width), bf16),
+            pltpu.VMEM((chunk, units), bf16),
+            pltpu.VMEM((chunk, units), bf16),
+            pltpu.VMEM((chunk, 128), bf16),
+            pltpu.VMEM((width, units), f32),
+            pltpu.VMEM((units, width), f32),
+        ]
+        + [dma((planes,))] * 4
+        + [dma((planes, 2))] * 2
+        + [dma((planes,))] * 6,
+        compiler_params=pltpu.CompilerParams(
+            collective_id=1, has_side_effects=True, vmem_limit_bytes=60 * 2**20
+        ),
+        cost_estimate=pl.CostEstimate(flops=flops, bytes_accessed=40 * 2**20, transcendentals=0),
+        name="experts_of_the_plane",
+    )(normed, grads, select, inner, inner.T, outer, outer.T, bias, router, router.T)
 
 
 def norm_parts(values):
@@ -492,12 +777,15 @@
         (chosen[:, :, None] == jnp.arange(experts, dtype=jnp.int32)).astype(f32), axis=1
     )
     grad_out = cotangent.astype(f32).reshape(rows, width) * keep_rows
+    padded = (rows + 15) // 16 * 16
+    extra = ((0, padded - rows), (0, 0))
     packed = jnp.concatenate(
         [grad_out.astype(bf16), jnp.pad(selected, ((0, 0), (0, 128 - experts))).astype(bf16)],
         axis=1,
     )
-    packed = gather_plane(packed, planes).reshape(-1, width + 128)
-    all_grad_out, all_selected = packed[:, :width], packed[:, width : width + experts].astype(f32)
+    packed = gather_plane(jnp.pad(packed, extra), planes)
+    packed = packed.reshape(planes, 4 * padded, width + 128)
+    all_grad_out, all_selected = packed[..., :width], packed[..., width:]
 
     mine_in = lax.dynamic_slice_in_dim(w_in, core * own, own, 0)
     mine_in = mine_in.reshape(own, depth, 2 * planes, slice_width).transpose(2, 0, 1, 3)
@@ -513,7 +801,7 @@
     )
     inner = jnp.take(got, up_order, axis=0).transpose(0, 2, 1, 3).reshape(width, own * slice_width)
     outer = lax.dynamic_slice_in_dim(w_out, core * own, own, 0).reshape(own * slice_width, width)
-    inner_bias = lax.dynamic_slice_in_dim(b_in_slice(b_in), core * own, own, 0)
+    inner_bias = lax.dynamic_slice_in_dim(b_in, core * own, own, 0)
     inner_bias = inner_bias.reshape(1, own * slice_width).astype(f32)
 
     flat_tokens = tokens.astype(f32).reshape(rows, width)
@@ -532,37 +820,21 @@
     normal_mid, rstd_mid = norm_parts(middle)
     normed_mid = (normal_mid * gain_second + bias_second).astype(bf16)
 
-    everyone = gather_plane(normed_mid, planes).reshape(-1, width)
-    own_experts = core * own + jnp.arange(own, dtype=jnp.int32)
-    pick = (own_experts[:, None] == jnp.arange(experts, dtype=jnp.int32)).astype(f32)
-    routing = softmax_rows(jnp.dot(everyone, full_router, preferred_element_type=f32))
-    gates = jnp.dot(routing * all_selected, pick.T, precision=lax.Precision.HIGHEST)
-    spread_gates = jnp.repeat(gates, slice_width, axis=1)
-    pre = jnp.dot(everyone, inner, preferred_element_type=f32) + inner_bias
-    cdf = 0.5 * (1.0 + lax.erf(pre * (0.5**0.5)))
-    slope = cdf + pre * jnp.exp(-0.5 * pre * pre) * 0.3989422804014327
-    act = pre * cdf
-    gated = (spread_gates * act).astype(bf16)
-    mix_parts = jnp.dot(gated, outer, preferred_element_type=f32).astype(bf16)
-    grad_act = jnp.einsum("nd,fd->nf", all_grad_out, outer, preferred_element_type=f32)
-    grad_gate = jnp.sum((act * grad_act).reshape(-1, own, slice_width), axis=2)
-    grad_pre32 = spread_gates * grad_act * slope
-    grad_pre = grad_pre32.astype(bf16)
-    outer_grad = jnp.einsum("nf,nd->fd", gated, all_grad_out, preferred_element_type=f32)
-    inner_bias_grad = jnp.sum(grad_pre32, axis=0)
-    inner_grad = jnp.einsum("nd,nf->df", everyone, grad_pre, preferred_element_type=f32)
-    grad_gate = jnp.dot(grad_gate * all_select(all_selected, pick), pick, precision=lax.Precision.HIGHEST)
-    grad_logits = (
-        routing * (grad_gate - jnp.sum(routing * grad_gate, axis=-1, keepdims=True))
-    ).astype(bf16)
-    router_grad = jnp.einsum("nd,ne->de", everyone, grad_logits, preferred_element_type=f32)
-    row_parts = jnp.einsum("nf,df->nd", grad_pre, inner, preferred_element_type=f32)
-    row_parts = row_parts + jnp.einsum(
-        "ne,de->nd", grad_logits, full_router, preferred_element_type=f32
-    )
-    row_parts = row_parts.astype(bf16)
-    grad_rows = scatter_plane(row_parts.reshape(2, planes, 2, rows, width), planes)
-    mixture = scatter_plane(mix_parts.reshape(2, planes, 2, rows, width), planes)
+    wide_router = jnp.pad(full_router, ((0, 0), (0, 128 - experts)))
+    mix_parts, grad_rows, inner_grad, outer_grad, inner_bias_grad, router_grad = experts_of_the_plane(
+        planes,
+        own,
+        jnp.pad(normed_mid, extra),
+        all_grad_out,
+        all_selected,
+        inner,
+        outer,
+        inner_bias,
+        wide_router,
+    )
+    grad_rows = grad_rows[:rows]
+    router_grad = router_grad[:, :experts]
+    mixture = scatter_plane(mix_parts.reshape(planes, 2, 2, padded, width), planes)[:rows]
 
     own_routing = softmax_rows(jnp.dot(normed_mid, full_router, preferred_element_type=f32))
     own_gates = own_routing * selected
@@ -672,14 +944,6 @@
     )
 
 
-def b_in_slice(b_in):
-    return b_in
-
-
-def all_select(selected, pick):
-    return jnp.dot(selected, pick.T, precision=lax.Precision.HIGHEST)
-
-
 def solution(mesh):
     n_seq, n_fsdp = mesh.shape["seq"], mesh.shape["fsdp"]
 

time: 593 us -> 589 us (level)
  Pallas kernels: 0 us -> 110 us
  matrix products: 87.9 us -> 27.7 us
  waiting for transfers between devices: 244 us -> 204 us
  local copies, waits for them, and re-layouts: 61.1 us -> 81.2 us
  starting transfers between devices: 101 us -> 85.4 us
  other arithmetic: 86.7 us -> 73 us
    pallas_call x0 -> x1, Pallas kernels: none -> 110 us  [experts_of_the_plane(): pl.pallas_call(functools.partial(expert_kernel, planes, own, rows), out_s...]
    dot_general x12 -> x0, matrix products: 55.7 us -> none  [the longest x1 13.3 us: move_tokens_plan(): jnp.einsum('nd,fd->nf', all_grad_out, outer, preferred_element_type=f32)]
    ppermute x1, waiting for transfers between devices: 3.38 us -> 41.2 us  [move_tokens_plan(): across = lax.ppermute(mine_in[:, 1], 'fsdp', x_swap(planes))]
    ppermute x9 -> x6, waiting for transfers between devices: 71.2 us -> 35.4 us  [gather_fsdp(): lax.ppermute(block, 'fsdp', z_shift(planes, k))]
    ppermute x3 -> x2, waiting for transfers between devices: 26.8 us -> 0.01 us  [gather_fsdp(): across = lax.ppermute(column, 'fsdp', x_swap(planes))]
    ppermute x9 -> x6, starting transfers between devices: 51.5 us -> 24.9 us  [gather_fsdp(): lax.ppermute(block, 'fsdp', z_shift(planes, k))]
    ppermute x4 -> x3, waiting for transfers between devices: 44.1 us -> 18.8 us  [scatter_fsdp(): lax.ppermute(parts[:, 1], 'fsdp', x_swap(planes))]
    reduce_sum x3 -> x0, other arithmetic: 16.7 us -> none  [the longest x1 11.1 us: move_tokens_plan(): inner_bias_grad = jnp.sum(grad_pre32, axis=0)]
  transfers between devices with their start and end apart: 52 -> 42, of which waited for: 26 -> 19; matrix products, arithmetic and copies ran while one was open for 24% -> 26% of each run, Pallas kernels for 0% -> 0%
where the time goes in v2:
time: 589 us; the launch traced here: 584 us
  waiting for transfers between devices  204 us (35%)
  Pallas kernels  110 us (19%)
  starting transfers between devices  85.4 us (14%)
  local copies, waits for them, and re-layouts  81.2 us (14%)
  other arithmetic  73 us (12%)
  matrix products  27.7 us (5%)
    pallas_call x1, Pallas kernels, experts_of_the_plane(): pl.pallas_call(functools.partial(expert_kernel, planes, own, rows), out_s...  110 us
    ppermute x6, waiting for transfers between devices, move_tokens_plan(): lax.ppermute(pairs[k], 'fsdp', z_shift(planes, -k))  42.5 us
    ppermute x1, waiting for transfers between devices, move_tokens_plan(): across = lax.ppermute(mine_in[:, 1], 'fsdp', x_swap(planes))  41.2 us
    ppermute x6, waiting for transfers between devices, gather_fsdp(): lax.ppermute(block, 'fsdp', z_shift(planes, k))  35.4 us
    ppermute x9, waiting for transfers between devices, scatter_fsdp(): lax.ppermute(column[k], 'fsdp', z_shift(planes, -k)).astype(jnp.float32)  31.5 us
    ppermute x6, starting transfers between devices, gather_fsdp(): lax.ppermute(block, 'fsdp', z_shift(planes, k))  24.9 us
    ppermute x3, waiting for transfers between devices, scatter_fsdp(): lax.ppermute(parts[:, 1], 'fsdp', x_swap(planes))  18.8 us
    ppermute x6, starting transfers between devices, move_tokens_plan(): lax.ppermute(pairs[k], 'fsdp', z_shift(planes, -k))  18.7 us
  transfers between devices with their start and end apart: 42, of which 19 were waited for; matrix products, arithmetic and copies ran while one was open for 26% of the time, Pallas kernels for 0%

profile of v2, /device:TPU:0, one launch (start us, length us, event | category | flops | bytes accessed | tf_op | source)
XLA Modules:
  0.0 583.5 jit_solution(8139294049582003735)
XLA Ops:
  0.7 2.4 concatenate.49
  3.2 2.2 fusion.130
  5.4 4.0 collective-permute-start.1
  14.9 2.1 collective-permute-start.5
  18.4 20.1 %collective-permute-done.1 = bf16[96,3200]{1,0:T(8,128)(2,1)} collective-permute-done((bf16[96,3200]{1,0:T(8,128)(2,1)}, bf16[96,3200]{1,0:T(8,128)(2,1)}, u32[]{:S(2)}, u32[]{:S(2)}) %collective-permute-start.1) | collective-permute-done | bytes 614432 | tf_op jit(solution)/shard_map/ppermute | solution.py:367
  38.5 15.1 %collective-permute-start.6 = (bf16[208,896]{1,0:T(8,128)(2,1)}, bf16[208,896]{1,0:T(8,128)(2,1)S(1)}, u32[]{:S(2)}, u32[]{:S(2)}) collective-permute-start(bf16[208,896]{1,0:T(8,128)(2,1)} %get-tuple-element.169), channel_id=1, source_target_pairs={{0,6},{1,7},{2,0},{3,1},{4,2},{5,3},{6,4},{7,5},{8,14},{9,15},{10,... | collective-permute-start | bytes 1118216 | tf_op jit(solution)/shard_map/ppermute | solution.py:367
  53.6 2.8 fusion.133
  56.5 14.0 %collective-permute-start.3 = (bf16[4,96,3200]{2,1,0:T(8,128)(2,1)}, bf16[4,96,3200]{2,1,0:T(8,128)(2,1)}, u32[]{:S(2)}, u32[]{:S(2)}) collective-permute-start(bf16[4,96,3200]{2,1,0:T(8,128)(2,1)} %get-tuple-element.140), channel_id=1, source_target_pairs={{0,1},{1,0},{2,3},{3,2},{4,5},{5,4},{6,7},{7,6},{8,9},{9,8},{10,11... | collective-permute-start | bytes 7372808 | tf_op jit(solution)/shard_map/ppermute | solution.py:369
  72.6 15.4 %collective-permute-done.5 = bf16[208,896]{1,0:T(8,128)(2,1)} collective-permute-done((bf16[208,896]{1,0:T(8,128)(2,1)}, bf16[208,896]{1,0:T(8,128)(2,1)}, u32[]{:S(2)}, u32[]{:S(2)}) %collective-permute-start.5) | collective-permute-done | bytes 372768 | tf_op jit(solution)/shard_map/ppermute | solution.py:367
  88.0 3.0 fusion.132
  93.0 2.4 copy.251
  96.4 41.2 %collective-permute-done.9 = bf16[4,2,96,384]{3,2,1,0:T(8,128)(2,1)} collective-permute-done((bf16[4,2,96,384]{3,2,1,0:T(8,128)(2,1)}, bf16[4,2,96,384]{3,2,1,0:T(8,128)(2,1)}, u32[]{:S(2)}, u32[]{:S(2)}) %collective-permute-start.9) | collective-permute-done | bytes 589856 | tf_op jit(solution)/shard_map/ppermute | solution.py:793
  139.0 16.4 %collective-permute-start.11 = (bf16[2,2,96,384]{3,2,1,0:T(8,128)(2,1)S(1)}, bf16[2,2,96,384]{3,2,1,0:T(8,128)(2,1)S(1)}, u32[]{:S(2)}, u32[]{:S(2)}) collective-permute-start(bf16[2,2,96,384]{3,2,1,0:T(8,128)(2,1)S(1)} %get-tuple-element.158), channel_id=1, source_target_pairs={{0,4},{1,5},{2,6},{3,7},{4,0},{5,1},{6,2},{7,3},{8,12},{9,13},{10,... | collective-permute-start | bytes 884744 | tf_op jit(solution)/shard_map/ppermute | solution.py:796
  155.4 2.0 collective-permute-start.12
  159.4 20.0 %collective-permute-done.11 = bf16[2,2,96,384]{3,2,1,0:T(8,128)(2,1)S(1)} collective-permute-done((bf16[2,2,96,384]{3,2,1,0:T(8,128)(2,1)S(1)}, bf16[2,2,96,384]{3,2,1,0:T(8,128)(2,1)S(1)}, u32[]{:S(2)}, u32[]{:S(2)}) %collective-permute-start.11) | collective-permute-done | bytes 294944 | tf_op jit(solution)/shard_map/ppermute | solution.py:796
  180.5 3.0 gather_fusion.4
  187.3 2.4 copy.222
  189.7 4.9 fusion.131
  194.6 4.4 pad_maximum_fusion.1
  198.9 5.7 gather_fusion
  204.6 7.5 %copy.214 = bf16[768,3200]{0,1:T(8,128)(2,1)} copy(bf16[768,3200]{1,0:T(8,128)(2,1)} %bitcast.306) | data formatting | bytes 9830400 | tf_op jit(solution)/shard_map/jit(_take)/gather | solution.py:765
  212.1 2.9 broadcast_select_fusion
  215.0 2.1 copy-done.10
  219.3 2.5 fusion.138
  221.8 2.1 convolution_convert_fusion.3
  223.9 2.1 fusion.139
  233.2 3.3 pad_maximum_fusion
  237.0 2.7 slice.262.grads_ref
  240.7 109.9 %experts_of_the_plane.1 = (bf16[4,832,768]{2,1,0:T(8,128)(2,1)}, f32[208,768]{1,0:T(8,128)}, bf16[768,768]{1,0:T(8,128)(2,1)}, bf16[768,768]{1,0:T(8,128)(2,1)}, f32[1,768]{1,0:T(1,128)}, /*index=5*/f32[768,128]{1,0:T(8,128)}) custom-call(bf16[208,768]{1,0:T(8,128)(2,1)} %pad.37.normed_ref, bf16[4,832,768]{2,1,0:T(8,128)(2,1)} %slice.262.grads_ref, ...), custom_call_target="tpu_custom_call" | custom-call | flops 23555211264 | bytes 41943040 | tf_op jit(solution)/shard_map/experts_of_the_plane/pallas_call | solution.py:672
  350.6 2.2 multiply_reduce_fusion.1
  353.8 1.9 convolution_convert_fusion.4
  355.9 2.5 multiply_reduce_fusion
  364.5 3.9 reshape.375
  368.4 5.5 gather_fusion.5
  373.9 2.4 broadcast_select_fusion.1
  378.8 3.0 collective-permute-start.34
  386.2 4.5 fusion.39
  399.1 5.1 fusion.135
  404.3 5.7 collective-permute-done.27
  410.8 2.5 gather_fusion.2
  413.3 2.0 copy.239
  416.8 2.2 fusion.64
  422.1 2.2 collective-permute-done.28
  425.9 5.9 %collective-permute-done.35 = bf16[2,96,2,384]{3,1,2,0:T(8,128)(2,1)S(1)} collective-permute-done((bf16[2,96,2,384]{3,1,2,0:T(8,128)(2,1)S(1)}, bf16[2,96,2,384]{3,1,2,0:T(8,128)(2,1)S(1)}, u32[]{:S(2)}, u32[]{:S(2)}) %collective-permute-start.35) | collective-permute-done | bytes 294944 | tf_op jit(solution)/shard_map/ppermute | solution.py:923
  431.8 2.1 collective-permute-start.29
  433.9 15.3 %collective-permute-done.36 = bf16[2,96,2,384]{3,1,2,0:T(8,128)(2,1)S(1)} collective-permute-done((bf16[2,96,2,384]{3,1,2,0:T(8,128)(2,1)S(1)}, bf16[2,96,2,384]{3,1,2,0:T(8,128)(2,1)S(1)}, u32[]{:S(2)}, u32[]{:S(2)}) %collective-permute-start.36) | collective-permute-done | bytes 294944 | tf_op jit(solution)/shard_map/ppermute | solution.py:923
  452.0 3.1 gather_fusion.6
  461.5 2.6 add_convert_fusion.1
  470.7 2.4 add_convert_fusion
  473.7 15.2 %collective-permute-done.38 = bf16[2,96,3072]{2,1,0:T(8,128)(2,1)} collective-permute-done((bf16[2,96,3072]{2,1,0:T(8,128)(2,1)}, bf16[2,96,3072]{2,1,0:T(8,128)(2,1)}, u32[]{:S(2)}, u32[]{:S(2)}) %collective-permute-start.38) | collective-permute-done | bytes 1179680 | tf_op jit(solution)/shard_map/ppermute | solution.py:927
  488.9 2.0 add_convert_fusion.2
  493.5 2.6 fusion.7
  496.1 12.7 %collective-permute-done.19 = bf16[8,96,640]{2,1,0:T(8,128)(2,1)S(1)} collective-permute-done((bf16[8,96,640]{2,1,0:T(8,128)(2,1)S(1)}, bf16[8,96,640]{2,1,0:T(8,128)(2,1)S(1)}, u32[]{:S(2)}, u32[]{:S(2)}) %collective-permute-start.19) | collective-permute-done | bytes 983072 | tf_op jit(solution)/shard_map/ppermute | solution.py:414
  511.9 2.5 fusion.1
  516.0 8.6 %collective-permute-done.20 = bf16[4,96,640]{2,1,0:T(8,128)(2,1)S(1)} collective-permute-done((bf16[4,96,640]{2,1,0:T(8,128)(2,1)S(1)}, bf16[4,96,640]{2,1,0:T(8,128)(2,1)S(1)}, u32[]{:S(2)}, u32[]{:S(2)}) %collective-permute-start.20) | collective-permute-done | bytes 491552 | tf_op jit(solution)/shard_map/ppermute | solution.py:380
  524.7 2.2 collective-permute-start.21
  530.1 2.6 collective-permute-done.21
  532.7 4.0 collective-permute-done.22
  538.4 2.5 maximum_convert_fusion.1
  541.8 8.1 %collective-permute-done.14 = bf16[4,208,768]{2,1,0:T(8,128)(2,1)S(1)} collective-permute-done((bf16[4,208,768]{2,1,0:T(8,128)(2,1)S(1)}, bf16[4,208,768]{2,1,0:T(8,128)(2,1)S(1)}, u32[]{:S(2)}, u32[]{:S(2)}) %collective-permute-start.14) | collective-permute-done | bytes 1277984 | tf_op jit(solution)/shard_map/ppermute | solution.py:380
  550.4 2.6 collective-permute-start.15
  556.6 4.5 collective-permute-done.15
  561.1 20.2 %collective-permute-done.16 = bf16[208,768]{1,0:T(8,128)(2,1)S(1)} collective-permute-done((bf16[208,768]{1,0:T(8,128)(2,1)S(1)}, bf16[208,768]{1,0:T(8,128)(2,1)S(1)}, u32[]{:S(2)}, u32[]{:S(2)}) %collective-permute-start.16) | collective-permute-done | bytes 319520 | tf_op jit(solution)/shard_map/ppermute | solution.py:385
  581.3 2.1 fusion.62
  (346 shorter events, 93.8 us)
Async XLA Ops:
  5.4 33.1 %collective-permute-start.1 = (bf16[96,3200]{1,0:T(8,128)(2,1)}, bf16[96,3200]{1,0:T(8,128)(2,1)}, u32[]{:S(2)}, u32[]{:S(2)}) collective-permute-start(bf16[96,3200]{1,0:T(8,128)(2,1)} %get-tuple-element.162), channel_id=1, source_target_pairs={{0,4},{1,5},{2,6},{3,7},{4,0},{5,1},{6,2},{7,3},{8,12},{9,13},{10,... | collective-permute-start | bytes 1843208 | tf_op jit(solution)/shard_map/ppermute | solution.py:367
  9.4 44.2 %collective-permute-start.2 = (bf16[96,3200]{1,0:T(8,128)(2,1)}, bf16[96,3200]{1,0:T(8,128)(2,1)}, u32[]{:S(2)}, u32[]{:S(2)}) collective-permute-start(bf16[96,3200]{1,0:T(8,128)(2,1)} %get-tuple-element.162), channel_id=1, source_target_pairs={{0,6},{1,7},{2,0},{3,1},{4,2},{5,3},{6,4},{7,5},{8,14},{9,15},{10,... | collective-permute-start | bytes 1843208 | tf_op jit(solution)/shard_map/ppermute | solution.py:367
  10.8 42.8 %collective-permute-start = (bf16[96,3200]{1,0:T(8,128)(2,1)}, bf16[96,3200]{1,0:T(8,128)(2,1)}, u32[]{:S(2)}, u32[]{:S(2)}) collective-permute-start(bf16[96,3200]{1,0:T(8,128)(2,1)} %get-tuple-element.162), channel_id=1, source_target_pairs={{0,2},{1,3},{2,4},{3,5},{4,6},{5,7},{6,0},{7,1},{8,10},{9,11},{10,... | collective-permute-start | bytes 1843208 | tf_op jit(solution)/shard_map/ppermute | solution.py:367
  11.5 220.4 %copy-start.37 = (f32[200,4]{0,1:T(4,128)}, f32[200,4]{0,1:T(4,128)S(1)}, u32[]{:S(2)}) copy-start(f32[200,4]{0,1:T(4,128)S(1)} %convert_reduce_fusion.3) | copy-start | bytes 9604
  13.4 59.2 %collective-permute-start.4 = (bf16[208,896]{1,0:T(8,128)(2,1)}, bf16[208,896]{1,0:T(8,128)(2,1)}, u32[]{:S(2)}, u32[]{:S(2)}) collective-permute-start(bf16[208,896]{1,0:T(8,128)(2,1)} %get-tuple-element.169), channel_id=1, source_target_pairs={{0,2},{1,3},{2,4},{3,5},{4,6},{5,7},{6,0},{7,1},{8,10},{9,11},{10,... | collective-permute-start | bytes 1118216 | tf_op jit(solution)/shard_map/ppermute | solution.py:367
  14.9 73.0 %collective-permute-start.5 = (bf16[208,896]{1,0:T(8,128)(2,1)}, bf16[208,896]{1,0:T(8,128)(2,1)}, u32[]{:S(2)}, u32[]{:S(2)}) collective-permute-start(bf16[208,896]{1,0:T(8,128)(2,1)} %get-tuple-element.169), channel_id=1, source_target_pairs={{0,4},{1,5},{2,6},{3,7},{4,0},{5,1},{6,2},{7,3},{8,12},{9,13},{10,... | collective-permute-start | bytes 1118216 | tf_op jit(solution)/shard_map/ppermute | solution.py:367
  17.4 75.5 %copy-start.69 = (pred[8]{0:T(512)(128)(4,1)}, pred[8]{0:T(512)(128)(4,1)S(1)}, u32[]{:S(2)}) copy-start(pred[8]{0:T(512)(128)(4,1)S(1)} %get-tuple-element.196) | copy-start | bytes 28
  17.4 166.2 %copy-start.67 = (pred[8]{0:T(512)(128)(4,1)}, pred[8]{0:T(512)(128)(4,1)S(1)}, u32[]{:S(2)}) copy-start(pred[8]{0:T(512)(128)(4,1)S(1)} %get-tuple-element.129) | copy-start | bytes 28
  18.2 35.4 %copy-start.20 = (bf16[1,96,3200]{2,1,0:T(8,128)(2,1)S(1)}, bf16[1,96,3200]{2,1,0:T(8,128)(2,1)}, u32[]{:S(2)}) copy-start(bf16[1,96,3200]{2,1,0:T(8,128)(2,1)} %get-tuple-element.161) | copy-start | bytes 1843204
  38.5 49.4 %collective-permute-start.6 = (bf16[208,896]{1,0:T(8,128)(2,1)}, bf16[208,896]{1,0:T(8,128)(2,1)S(1)}, u32[]{:S(2)}, u32[]{:S(2)}) collective-permute-start(bf16[208,896]{1,0:T(8,128)(2,1)} %get-tuple-element.169), channel_id=1, source_target_pairs={{0,6},{1,7},{2,0},{3,1},{4,2},{5,3},{6,4},{7,5},{8,14},{9,15},{10,... | collective-permute-start | bytes 1118216 | tf_op jit(solution)/shard_map/ppermute | solution.py:367
  56.5 138.1 %collective-permute-start.3 = (bf16[4,96,3200]{2,1,0:T(8,128)(2,1)}, bf16[4,96,3200]{2,1,0:T(8,128)(2,1)}, u32[]{:S(2)}, u32[]{:S(2)}) collective-permute-start(bf16[4,96,3200]{2,1,0:T(8,128)(2,1)} %get-tuple-element.140), channel_id=1, source_target_pairs={{0,1},{1,0},{2,3},{3,2},{4,5},{5,4},{6,7},{7,6},{8,9},{9,8},{10,11... | collective-permute-start | bytes 7372808 | tf_op jit(solution)/shard_map/ppermute | solution.py:369
  71.4 16.6 %copy-start.26 = (bf16[1,208,896]{2,1,0:T(8,128)(2,1)S(1)}, bf16[1,208,896]{2,1,0:T(8,128)(2,1)}, u32[]{:S(2)}) copy-start(bf16[1,208,896]{2,1,0:T(8,128)(2,1)} %get-tuple-element.168) | copy-start | bytes 1118212
  71.4 66.3 %collective-permute-start.9 = (bf16[4,2,96,384]{3,2,1,0:T(8,128)(2,1)}, bf16[4,2,96,384]{3,2,1,0:T(8,128)(2,1)}, u32[]{:S(2)}, u32[]{:S(2)}) collective-permute-start(bf16[4,2,96,384]{3,2,1,0:T(8,128)(2,1)} %get-tuple-element.160), channel_id=1, source_target_pairs={{0,1},{1,0},{2,3},{3,2},{4,5},{5,4},{6,7},{7,6},{8,9},{9,8},{10,11... | collective-permute-start | bytes 1769480 | tf_op jit(solution)/shard_map/ppermute | solution.py:793
  71.4 109.1 %copy-start.64 = (s32[1024]{0:T(1024)}, s32[1024]{0:T(1024)S(1)}, u32[]{:S(2)}) copy-start(s32[1024]{0:T(1024)S(1)} %pad_clamp_fusion) | copy-start | bytes 12292
  90.9 98.8 %collective-permute-start.7 = (bf16[4,208,896]{2,1,0:T(8,128)(2,1)}, bf16[4,208,896]{2,1,0:T(8,128)(2,1)}, u32[]{:S(2)}, u32[]{:S(2)}) collective-permute-start(bf16[4,208,896]{2,1,0:T(8,128)(2,1)} %get-tuple-element.144), channel_id=1, source_target_pairs={{0,1},{1,0},{2,3},{3,2},{4,5},{5,4},{6,7},{7,6},{8,9},{9,8},{10,11... | collective-permute-start | bytes 4472840 | tf_op jit(solution)/shard_map/ppermute | solution.py:369
  96.0 102.9 %copy-start.63 = (s32[1024]{0:T(1024)}, s32[1024]{0:T(1024)S(1)}, u32[]{:S(2)}) copy-start(s32[1024]{0:T(1024)S(1)} %pad_clamp_fusion.2) | copy-start | bytes 12292
  96.2 131.7 %copy-start.44 = (f32[200]{0:T(256)}, f32[200]{0:T(256)S(1)}, u32[]{:S(2)}) copy-start(f32[200]{0:T(256)S(1)} %broadcast_multiply_fusion.5) | copy-start | bytes 2404
  138.9 20.4 %collective-permute-start.10 = (bf16[2,2,96,384]{3,2,1,0:T(8,128)(2,1)S(1)}, bf16[2,2,96,384]{3,2,1,0:T(8,128)(2,1)S(1)}, u32[]{:S(2)}, u32[]{:S(2)}) collective-permute-start(bf16[2,2,96,384]{3,2,1,0:T(8,128)(2,1)S(1)} %get-tuple-element.156), channel_id=1, source_target_pairs={{0,6},{1,7},{2,0},{3,1},{4,2},{5,3},{6,4},{7,5},{8,14},{9,15},{10,... | collective-permute-start | bytes 884744 | tf_op jit(solution)/shard_map/ppermute | solution.py:796
  139.0 40.3 %collective-permute-start.11 = (bf16[2,2,96,384]{3,2,1,0:T(8,128)(2,1)S(1)}, bf16[2,2,96,384]{3,2,1,0:T(8,128)(2,1)S(1)}, u32[]{:S(2)}, u32[]{:S(2)}) collective-permute-start(bf16[2,2,96,384]{3,2,1,0:T(8,128)(2,1)S(1)} %get-tuple-element.158), channel_id=1, source_target_pairs={{0,4},{1,5},{2,6},{3,7},{4,0},{5,1},{6,2},{7,3},{8,12},{9,13},{10,... | collective-permute-start | bytes 884744 | tf_op jit(solution)/shard_map/ppermute | solution.py:796
  155.4 24.0 %collective-permute-start.12 = (bf16[2,2,96,384]{3,2,1,0:T(8,128)(2,1)S(1)}, bf16[2,2,96,384]{3,2,1,0:T(8,128)(2,1)S(1)}, u32[]{:S(2)}, u32[]{:S(2)}) collective-permute-start(bf16[2,2,96,384]{3,2,1,0:T(8,128)(2,1)S(1)} %get-tuple-element.157), channel_id=1, source_target_pairs={{0,2},{1,3},{2,4},{3,5},{4,6},{5,7},{6,0},{7,1},{8,10},{9,11},{10,... | collective-permute-start | bytes 884744 | tf_op jit(solution)/shard_map/ppermute | solution.py:796
  157.9 70.0 %copy-start.57 = (f32[200]{0:T(256)}, f32[200]{0:T(256)S(1)}, u32[]{:S(2)}) copy-start(f32[200]{0:T(256)S(1)} %add_rsqrt_fusion.1) | copy-start | bytes 2404
  194.6 38.6 %collective-permute-start.8 = (bf16[4,2,208,896]{3,2,0,1:T(8,128)(2,1)}, bf16[4,2,208,896]{3,2,0,1:T(8,128)(2,1)}, u32[]{:S(2)}, u32[]{:S(2)}) collective-permute-start(bf16[4,2,208,896]{3,2,0,1:T(8,128)(2,1)} %get-tuple-element.136), channel_id=1, source_target_pairs={{0,8},{8,0},{16,24},{24,16},{1,9},{9,1},{17,25},{25,17},{2,10},{10... | collective-permute-start | bytes 8945672 | tf_op jit(solution)/shard_map/ppermute | solution.py:375
  221.8 136.6 %copy-start.47 = (f32[12,200]{1,0:T(8,128)}, f32[12,200]{1,0:T(8,128)S(1)}, u32[]{:S(2)}) copy-start(f32[12,200]{1,0:T(8,128)S(1)} %get-tuple-element.184) | copy-start | bytes 28804
  226.0 126.9 %copy-start.2 = (f32[200,768]{1,0:T(8,128)}, f32[200,768]{1,0:T(8,128)S(1)}, u32[]{:S(2)}) copy-start(f32[200,768]{1,0:T(8,128)S(1)} %get-tuple-element.187) | copy-start | bytes 1843204
  230.0 120.6 %copy-start.41 = (f32[200]{0:T(256)}, f32[200]{0:T(256)S(1)}, u32[]{:S(2)}) copy-start(f32[200]{0:T(256)S(1)} %get-tuple-element.188) | copy-start | bytes 2404
  230.1 120.5 %copy-start.54 = (f32[200]{0:T(256)}, f32[200]{0:T(256)S(1)}, u32[]{:S(2)}) copy-start(f32[200]{0:T(256)S(1)} %fusion.99) | copy-start | bytes 2404
  233.2 117.5 %copy-start.49 = (f32[200,4]{0,1:T(4,128)}, f32[200,4]{0,1:T(4,128)S(1)}, u32[]{:S(2)}) copy-start(f32[200,4]{0,1:T(4,128)S(1)} %get-tuple-element.191) | copy-start | bytes 9604
  233.2 117.5 %copy-start.71 = (f32[200]{0:T(256)}, f32[200]{0:T(256)S(1)}, u32[]{:S(2)}) copy-start(f32[200]{0:T(256)S(1)} %get-tuple-element.190) | copy-start | bytes 2404
  353.8 29.0 %copy-start.8 = (f32[200,768]{1,0:T(8,128)}, f32[200,768]{1,0:T(8,128)S(1)}, u32[]{:S(2)}) copy-start(f32[200,768]{1,0:T(8,128)S(1)} %get-tuple-element.128) | copy-start | bytes 1843204
  362.9 98.5 %collective-permute-start.40 = (bf16[2,400,768]{2,1,0:T(8,128)(2,1)}, bf16[2,400,768]{2,1,0:T(8,128)(2,1)}, u32[]{:S(2)}, u32[]{:S(2)}) collective-permute-start(bf16[2,400,768]{2,1,0:T(8,128)(2,1)} %fusion.14), channel_id=1, source_target_pairs={{0,16},{8,24},{16,0},{24,8},{1,17},{9,25},{17,1},{25,9},{2,18},{10... | collective-permute-start | bytes 3686408 | tf_op jit(solution)/shard_map/ppermute | solution.py:916
  378.8 41.9 %collective-permute-start.34 = (bf16[4,96,2,384]{3,1,2,0:T(8,128)(2,1)}, bf16[4,96,2,384]{3,1,2,0:T(8,128)(2,1)}, u32[]{:S(2)}, u32[]{:S(2)}) collective-permute-start(bf16[4,96,2,384]{3,1,2,0:T(8,128)(2,1)} %bitcast.301), channel_id=1, source_target_pairs={{0,1},{1,0},{2,3},{3,2},{4,5},{5,4},{6,7},{7,6},{8,9},{9,8},{10,11... | collective-permute-start | bytes 1769480 | tf_op jit(solution)/shard_map/ppermute | solution.py:920
  385.5 11.5 %collective-permute-start.26 = (bf16[8,96,512]{2,1,0:T(8,128)(2,1)}, bf16[8,96,512]{2,1,0:T(8,128)(2,1)}, u32[]{:S(2)}, u32[]{:S(2)}) collective-permute-start(bf16[8,96,512]{2,1,0:T(8,128)(2,1)} %fusion.22), channel_id=1, source_target_pairs={{0,8},{8,0},{16,24},{24,16},{1,9},{9,1},{17,25},{25,17},{2,10},{10... | collective-permute-start | bytes 2359304 | tf_op jit(solution)/shard_map/ppermute | solution.py:410
  395.6 75.1 %collective-permute-start.18 = (bf16[8,96,1280]{2,1,0:T(8,128)(2,1)}, bf16[8,96,1280]{2,1,0:T(8,128)(2,1)}, u32[]{:S(2)}, u32[]{:S(2)}) collective-permute-start(bf16[8,96,1280]{2,1,0:T(8,128)(2,1)} %fusion.9), channel_id=1, source_target_pairs={{0,8},{8,0},{16,24},{24,16},{1,9},{9,1},{17,25},{25,17},{2,10},{10... | collective-permute-start | bytes 5898248 | tf_op jit(solution)/shard_map/ppermute | solution.py:410
  398.6 11.4 %collective-permute-start.27 = (bf16[8,96,256]{2,1,0:T(8,128)(2,1)S(1)}, bf16[8,96,256]{2,1,0:T(8,128)(2,1)S(1)}, u32[]{:S(2)}, u32[]{:S(2)}) collective-permute-start(bf16[8,96,256]{2,1,0:T(8,128)(2,1)S(1)} %constant_dynamic-slice_fusion), channel_id=1, source_target_pairs={{0,16},{8,24},{16,0},{24,8},{1,17},{9,25},{17,1},{25,9},{2,18},{10... | collective-permute-start | bytes 1179656 | tf_op jit(solution)/shard_map/ppermute | solution.py:414
  416.6 7.7 %collective-permute-start.28 = (bf16[4,96,256]{1,2,0:T(8,128)(2,1)S(1)}, bf16[4,96,256]{1,2,0:T(8,128)(2,1)S(1)}, u32[]{:S(2)}, u32[]{:S(2)}) collective-permute-start(bf16[4,96,256]{1,2,0:T(8,128)(2,1)S(1)} %slice_bitcast_fusion.18), channel_id=1, source_target_pairs={{0,1},{1,0},{2,3},{3,2},{4,5},{5,4},{6,7},{7,6},{8,9},{9,8},{10,11... | collective-permute-start | bytes 589832 | tf_op jit(solution)/shard_map/ppermute | solution.py:380
  422.0 9.8 %collective-permute-start.35 = (bf16[2,96,2,384]{3,1,2,0:T(8,128)(2,1)S(1)}, bf16[2,96,2,384]{3,1,2,0:T(8,128)(2,1)S(1)}, u32[]{:S(2)}, u32[]{:S(2)}) collective-permute-start(bf16[2,96,2,384]{3,1,2,0:T(8,128)(2,1)S(1)} %get-tuple-element.150), channel_id=1, source_target_pairs={{0,6},{1,7},{2,0},{3,1},{4,2},{5,3},{6,4},{7,5},{8,14},{9,15},{10,... | collective-permute-start | bytes 884744 | tf_op jit(solution)/shard_map/ppermute | solution.py:923
  422.0 27.1 %collective-permute-start.36 = (bf16[2,96,2,384]{3,1,2,0:T(8,128)(2,1)S(1)}, bf16[2,96,2,384]{3,1,2,0:T(8,128)(2,1)S(1)}, u32[]{:S(2)}, u32[]{:S(2)}) collective-permute-start(bf16[2,96,2,384]{3,1,2,0:T(8,128)(2,1)S(1)} %get-tuple-element.152), channel_id=1, source_target_pairs={{0,4},{1,5},{2,6},{3,7},{4,0},{5,1},{6,2},{7,3},{8,12},{9,13},{10,... | collective-permute-start | bytes 884744 | tf_op jit(solution)/shard_map/ppermute | solution.py:923
  424.3 24.8 %collective-permute-start.37 = (bf16[2,96,2,384]{3,1,2,0:T(8,128)(2,1)S(1)}, bf16[2,96,2,384]{3,1,2,0:T(8,128)(2,1)S(1)}, u32[]{:S(2)}, u32[]{:S(2)}) collective-permute-start(bf16[2,96,2,384]{3,1,2,0:T(8,128)(2,1)S(1)} %get-tuple-element.151), channel_id=1, source_target_pairs={{0,2},{1,3},{2,4},{3,5},{4,6},{5,7},{6,0},{7,1},{8,10},{9,11},{10,... | collective-permute-start | bytes 884744 | tf_op jit(solution)/shard_map/ppermute | solution.py:923
  431.8 23.3 %collective-permute-start.29 = (bf16[96,256]{0,1:T(8,128)(2,1)}, bf16[96,256]{0,1:T(8,128)(2,1)}, u32[]{:S(2)}, u32[]{:S(2)}) collective-permute-start(bf16[96,256]{0,1:T(8,128)(2,1)} %get-tuple-element.177), channel_id=1, source_target_pairs={{0,6},{1,7},{2,0},{3,1},{4,2},{5,3},{6,4},{7,5},{8,14},{9,15},{10,... | collective-permute-start | bytes 147464 | tf_op jit(solution)/shard_map/ppermute | solution.py:385
  449.1 6.0 %collective-permute-start.30 = (bf16[96,256]{0,1:T(8,128)(2,1)}, bf16[96,256]{0,1:T(8,128)(2,1)}, u32[]{:S(2)}, u32[]{:S(2)}) collective-permute-start(bf16[96,256]{0,1:T(8,128)(2,1)} %get-tuple-element.179), channel_id=1, source_target_pairs={{0,4},{1,5},{2,6},{3,7},{4,0},{5,1},{6,2},{7,3},{8,12},{9,13},{10,... | collective-permute-start | bytes 147464 | tf_op jit(solution)/shard_map/ppermute | solution.py:385
  449.1 6.4 %collective-permute-start.31 = (bf16[96,256]{0,1:T(8,128)(2,1)}, bf16[96,256]{0,1:T(8,128)(2,1)}, u32[]{:S(2)}, u32[]{:S(2)}) collective-permute-start(bf16[96,256]{0,1:T(8,128)(2,1)} %get-tuple-element.178), channel_id=1, source_target_pairs={{0,2},{1,3},{2,4},{3,5},{4,6},{5,7},{6,0},{7,1},{8,10},{9,11},{10,... | collective-permute-start | bytes 147464 | tf_op jit(solution)/shard_map/ppermute | solution.py:385
  455.1 56.8 %collective-permute-start.13 = (bf16[4,2,208,768]{3,2,0,1:T(8,128)(2,1)}, bf16[4,2,208,768]{3,2,0,1:T(8,128)(2,1)}, u32[]{:S(2)}, u32[]{:S(2)}) collective-permute-start(bf16[4,2,208,768]{3,2,0,1:T(8,128)(2,1)} %bitcast.333), channel_id=1, source_target_pairs={{0,8},{8,0},{16,24},{24,16},{1,9},{9,1},{17,25},{25,17},{2,10},{10... | collective-permute-start | bytes 7667720 | tf_op jit(solution)/shard_map/ppermute | solution.py:390
  456.5 4.8 collective-permute-start.32
  459.8 29.2 %collective-permute-start.38 = (bf16[2,96,3072]{2,1,0:T(8,128)(2,1)}, bf16[2,96,3072]{2,1,0:T(8,128)(2,1)}, u32[]{:S(2)}, u32[]{:S(2)}) collective-permute-start(bf16[2,96,3072]{2,1,0:T(8,128)(2,1)} %bitcast.136), channel_id=1, source_target_pairs={{0,16},{8,24},{16,0},{24,8},{1,17},{9,25},{17,1},{25,9},{2,18},{10... | collective-permute-start | bytes 3538952 | tf_op jit(solution)/shard_map/ppermute | solution.py:927
  461.4 3.2 collective-permute-start.33
  464.1 27.0 %collective-permute-start.41 = (bf16[2,400,768]{2,1,0:T(8,128)(2,1)}, bf16[2,400,768]{2,1,0:T(8,128)(2,1)}, u32[]{:S(2)}, u32[]{:S(2)}) collective-permute-start(bf16[2,400,768]{2,1,0:T(8,128)(2,1)} %add_convert_fusion.1), channel_id=1, source_target_pairs={{0,8},{8,0},{16,24},{24,16},{1,9},{9,1},{17,25},{25,17},{2,10},{10... | collective-permute-start | bytes 3686408 | tf_op jit(solution)/shard_map/ppermute | solution.py:907
  473.2 35.6 %collective-permute-start.19 = (bf16[8,96,640]{2,1,0:T(8,128)(2,1)S(1)}, bf16[8,96,640]{2,1,0:T(8,128)(2,1)S(1)}, u32[]{:S(2)}, u32[]{:S(2)}) collective-permute-start(bf16[8,96,640]{2,1,0:T(8,128)(2,1)S(1)} %constant_dynamic-slice_fusion.1), channel_id=1, source_target_pairs={{0,16},{8,24},{16,0},{24,8},{1,17},{9,25},{17,1},{25,9},{2,18},{10... | collective-permute-start | bytes 2949128 | tf_op jit(solution)/shard_map/ppermute | solution.py:414
  491.0 37.7 %collective-permute-start.39 = (bf16[2,96,3072]{2,1,0:T(8,128)(2,1)S(1)}, bf16[2,96,3072]{2,1,0:T(8,128)(2,1)}, u32[]{:S(2)}, u32[]{:S(2)}) collective-permute-start(bf16[2,96,3072]{2,1,0:T(8,128)(2,1)S(1)} %add_convert_fusion.2), channel_id=1, source_target_pairs={{0,8},{8,0},{16,24},{24,16},{1,9},{9,1},{17,25},{25,17},{2,10},{10... | collective-permute-start | bytes 3538952 | tf_op jit(solution)/shard_map/ppermute | solution.py:907
  510.3 14.2 %collective-permute-start.20 = (bf16[4,96,640]{2,1,0:T(8,128)(2,1)S(1)}, bf16[4,96,640]{2,1,0:T(8,128)(2,1)S(1)}, u32[]{:S(2)}, u32[]{:S(2)}) collective-permute-start(bf16[4,96,640]{2,1,0:T(8,128)(2,1)S(1)} %slice_bitcast_fusion.3), channel_id=1, source_target_pairs={{0,1},{1,0},{2,3},{3,2},{4,5},{5,4},{6,7},{7,6},{8,9},{9,8},{10,11... | collective-permute-start | bytes 1474568 | tf_op jit(solution)/shard_map/ppermute | solution.py:380
  514.5 35.4 %collective-permute-start.14 = (bf16[4,208,768]{2,1,0:T(8,128)(2,1)S(1)}, bf16[4,208,768]{2,1,0:T(8,128)(2,1)S(1)}, u32[]{:S(2)}, u32[]{:S(2)}) collective-permute-start(bf16[4,208,768]{2,1,0:T(8,128)(2,1)S(1)} %slice_bitcast_fusion), channel_id=1, source_target_pairs={{0,1},{1,0},{2,3},{3,2},{4,5},{5,4},{6,7},{7,6},{8,9},{9,8},{10,11... | collective-permute-start | bytes 3833864 | tf_op jit(solution)/shard_map/ppermute | solution.py:380
  524.7 8.0 %collective-permute-start.21 = (bf16[96,640]{1,0:T(8,128)(2,1)S(1)}, bf16[96,640]{1,0:T(8,128)(2,1)S(1)}, u32[]{:S(2)}, u32[]{:S(2)}) collective-permute-start(bf16[96,640]{1,0:T(8,128)(2,1)S(1)} %get-tuple-element.165), channel_id=1, source_target_pairs={{0,6},{1,7},{2,0},{3,1},{4,2},{5,3},{6,4},{7,5},{8,14},{9,15},{10,... | collective-permute-start | bytes 368648 | tf_op jit(solution)/shard_map/ppermute | solution.py:385
  526.9 9.7 %collective-permute-start.22 = (bf16[96,640]{1,0:T(8,128)(2,1)S(1)}, bf16[96,640]{1,0:T(8,128)(2,1)S(1)}, u32[]{:S(2)}, u32[]{:S(2)}) collective-permute-start(bf16[96,640]{1,0:T(8,128)(2,1)S(1)} %get-tuple-element.167), channel_id=1, source_target_pairs={{0,4},{1,5},{2,6},{3,7},{4,0},{5,1},{6,2},{7,3},{8,12},{9,13},{10,... | collective-permute-start | bytes 368648 | tf_op jit(solution)/shard_map/ppermute | solution.py:385
  528.7 8.0 %collective-permute-start.23 = (bf16[96,640]{1,0:T(8,128)(2,1)S(1)}, bf16[96,640]{1,0:T(8,128)(2,1)S(1)}, u32[]{:S(2)}, u32[]{:S(2)}) collective-permute-start(bf16[96,640]{1,0:T(8,128)(2,1)S(1)} %get-tuple-element.166), channel_id=1, source_target_pairs={{0,2},{1,3},{2,4},{3,5},{4,6},{5,7},{6,0},{7,1},{8,10},{9,11},{10,... | collective-permute-start | bytes 368648 | tf_op jit(solution)/shard_map/ppermute | solution.py:385
  536.7 4.9 collective-permute-start.24
  541.7 13.1 %collective-permute-start.25 = (bf16[96,1280]{1,0:T(8,128)(2,1)S(1)}, bf16[96,1280]{1,0:T(8,128)(2,1)S(1)}, u32[]{:S(2)}, u32[]{:S(2)}) collective-permute-start(bf16[96,1280]{1,0:T(8,128)(2,1)S(1)} %pad_maximum_fusion.11), channel_id=1, source_target_pairs={{0,8},{8,0},{16,24},{24,16},{1,9},{9,1},{17,25},{25,17},{2,10},{10... | collective-permute-start | bytes 737288 | tf_op jit(solution)/shard_map/ppermute | solution.py:421
  550.3 30.9 %copy-start.3 = (f32[200,768]{1,0:T(8,128)S(1)}, f32[200,768]{1,0:T(8,128)}, u32[]{:S(2)}) copy-start(f32[200,768]{1,0:T(8,128)} %copy-done.2) | copy-start | bytes 1843204
  550.4 30.9 %copy-start.38 = (f32[200,4]{0,1:T(4,128)S(1)}, f32[200,4]{0,1:T(4,128)}, u32[]{:S(2)}) copy-start(f32[200,4]{0,1:T(4,128)} %copy-done.37) | copy-start | bytes 9604
  550.4 30.9 %copy-start.43 = (f32[200]{0:T(256)S(1)}, f32[200]{0:T(256)}, u32[]{:S(2)}) copy-start(f32[200]{0:T(256)} %copy-done.41) | copy-start | bytes 2404
  550.4 30.9 %copy-start.53 = (f32[1,200]{1,0:T(1,128)S(1)}, f32[1,200]{1,0:T(1,128)}, u32[]{:S(2)}) copy-start(f32[1,200]{1,0:T(1,128)} %copy-done.51) | copy-start | bytes 2404
  550.4 30.9 %copy-start.56 = (f32[200]{0:T(256)S(1)}, f32[200]{0:T(256)}, u32[]{:S(2)}) copy-start(f32[200]{0:T(256)} %copy-done.54) | copy-start | bytes 2404
  550.4 10.7 %collective-permute-start.15 = (bf16[208,768]{1,0:T(8,128)(2,1)S(1)}, bf16[208,768]{1,0:T(8,128)(2,1)S(1)}, u32[]{:S(2)}, u32[]{:S(2)}) collective-permute-start(bf16[208,768]{1,0:T(8,128)(2,1)S(1)} %get-tuple-element.145), channel_id=1, source_target_pairs={{0,6},{1,7},{2,0},{3,1},{4,2},{5,3},{6,4},{7,5},{8,14},{9,15},{10,... | collective-permute-start | bytes 958472 | tf_op jit(solution)/shard_map/ppermute | solution.py:385
  553.0 28.2 %collective-permute-start.16 = (bf16[208,768]{1,0:T(8,128)(2,1)S(1)}, bf16[208,768]{1,0:T(8,128)(2,1)S(1)}, u32[]{:S(2)}, u32[]{:S(2)}) collective-permute-start(bf16[208,768]{1,0:T(8,128)(2,1)S(1)} %get-tuple-element.147), channel_id=1, source_target_pairs={{0,4},{1,5},{2,6},{3,7},{4,0},{5,1},{6,2},{7,3},{8,12},{9,13},{10,... | collective-permute-start | bytes 958472 | tf_op jit(solution)/shard_map/ppermute | solution.py:385
  554.8 26.4 %collective-permute-start.17 = (bf16[208,768]{1,0:T(8,128)(2,1)S(1)}, bf16[208,768]{1,0:T(8,128)(2,1)S(1)}, u32[]{:S(2)}, u32[]{:S(2)}) collective-permute-start(bf16[208,768]{1,0:T(8,128)(2,1)S(1)} %get-tuple-element.146), channel_id=1, source_target_pairs={{0,2},{1,3},{2,4},{3,5},{4,6},{5,7},{6,0},{7,1},{8,10},{9,11},{10,... | collective-permute-start | bytes 958472 | tf_op jit(solution)/shard_map/ppermute | solution.py:385
  554.9 28.4 %copy-start.1 = (bf16[4,96,3072]{2,1,0:T(8,128)(2,1)S(1)}, bf16[4,96,3072]{2,1,0:T(8,128)(2,1)}, u32[]{:S(2)}) copy-start(bf16[4,96,3072]{2,1,0:T(8,128)(2,1)} %param.32) | copy-start | bytes 7077892
  (58 other events, 250.9 us)

commit v3 on v2

--- a/solution.py
+++ b/solution.py
@@ -350,79 +350,6 @@
     )
 
 
-def z_shift(planes, step):
-    return [(2 * z + x, 2 * ((z + step) % planes) + x) for z in range(planes) for x in range(2)]
-
-
-def x_swap(planes):
-    return [(2 * z + x, 2 * z + 1 - x) for z in range(planes) for x in range(2)]
-
-
-core_swap = [(0, 1), (1, 0), (2, 3), (3, 2)]
-y_swap = [(0, 2), (1, 3), (2, 0), (3, 1)]
-
-
-def gather_fsdp(block, planes):
-    column = jnp.stack(
-        [block] + [lax.ppermute(block, "fsdp", z_shift(planes, k)) for k in range(1, planes)]
-    )
-    across = lax.ppermute(column, "fsdp", x_swap(planes))
-    return jnp.stack([column, across], axis=1)
-
-
-def gather_plane(block, planes):
-    mine = gather_fsdp(block, planes)
-    return jnp.stack([mine, lax.ppermute(mine, "seq", core_swap)], axis=1)
-
-
-def scatter_fsdp(parts, planes):
-    add = lambda a, b: a.astype(jnp.float32) + b.astype(jnp.float32)
-    column = add(parts[:, 0], lax.ppermute(parts[:, 1], "fsdp", x_swap(planes))).astype(
-        jnp.bfloat16
-    )
-    total = column[0].astype(jnp.float32)
-    for k in range(1, planes):
-        total = total + lax.ppermute(column[k], "fsdp", z_shift(planes, -k)).astype(jnp.float32)
-    return total
-
-
-def scatter_plane(parts, planes):
-    other = lax.ppermute(parts[:, 1], "seq", core_swap)
-    mine = (parts[:, 0].astype(jnp.float32) + other.astype(jnp.float32)).astype(jnp.bfloat16)
-    return scatter_fsdp(mine, planes)
-
-
-def shard_order(planes):
-    f = lax.axis_index("fsdp")
-    z, x = f // 2, f % 2
-    g = jnp.arange(2 * planes, dtype=jnp.int32)
-    return ((z - g // 2) % planes) * 2 + (x ^ (g % 2))
-
-
-def sum_everywhere(parts, planes):
-    order = shard_order(planes)
-    shards, rows, columns = parts.shape
-    s = lax.axis_index("seq")
-    y, c = s // 2, s % 2
-    half, quarter = columns // 2, columns // 4
-    keep = lax.dynamic_slice_in_dim(parts, c * half, half, 2)
-    give = lax.dynamic_slice_in_dim(parts, (1 - c) * half, half, 2)
-    got = lax.ppermute(give, "seq", core_swap)
-    keep = (keep.astype(jnp.float32) + got.astype(jnp.float32)).astype(jnp.bfloat16)
-    give = lax.dynamic_slice_in_dim(keep, (1 - y) * quarter, quarter, 2)
-    keep = lax.dynamic_slice_in_dim(keep, y * quarter, quarter, 2)
-    got = lax.ppermute(give, "seq", y_swap)
-    keep = (keep.astype(jnp.float32) + got.astype(jnp.float32)).astype(jnp.bfloat16)
-    place = jnp.take(keep, order, axis=0).reshape(planes, 2, rows, quarter)
-    total = scatter_fsdp(place, planes).astype(jnp.bfloat16)
-    other = lax.ppermute(total, "seq", y_swap)
-    first, second = jnp.where(y == 0, total, other), jnp.where(y == 0, other, total)
-    total = jnp.concatenate([first, second], axis=1)
-    other = lax.ppermute(total, "seq", core_swap)
-    first, second = jnp.where(c == 0, total, other), jnp.where(c == 0, other, total)
-    return jnp.concatenate([first, second], axis=1).astype(jnp.float32)
-
-
 MESH = pl.DeviceIdType.MESH
 NT = (((1,), (1,)), ((), ()))
 TN = (((0,), (0,)), ((), ()))
@@ -465,22 +392,21 @@
     planes,
     own,
     rows,
-    normed_ref,
-    grads_ref,
-    select_ref,
+    packed_ref,
     inner_ref,
-    inner_t_ref,
     outer_ref,
-    outer_t_ref,
     bias_ref,
-    router_ref,
-    router_t_ref,
+    small_ref,
     mix_ref,
     out_ref,
     inner_grad_ref,
     outer_grad_ref,
+    router_grad_ref,
+    inner_t_ref,
+    outer_t_ref,
+    router_ref,
+    router_t_ref,
     bias_grad_ref,
-    router_grad_ref,
     tokens,
     part,
     from_core,
@@ -506,7 +432,7 @@
 ):
     f32, bf16 = jnp.float32, jnp.bfloat16
     place = Place(planes)
-    width = normed_ref.shape[1]
+    width = inner_ref.shape[0]
     lanes = inner_ref.shape[1] // own
 
     def remote(src, dst, send, recv, device):
@@ -538,11 +464,19 @@
         return remote(slot(part, k, 0), from_z.at[k], sum_z_send.at[k], sum_z_recv.at[k], place.level(-k))
 
     greet([place.other_core(), place.other_x()] + [place.level(k) for k in range(1, planes)])
-    tokens[0, 0:rows, :] = normed_ref[...]
+    tokens[0, 0:rows, :] = packed_ref[...]
     c_copy(0, 0).start()
     x_copy(0).start()
     for k in range(1, planes):
         z_copy(k).start()
+    inner_t_ref[...] = jnp.transpose(inner_ref[...])
+    outer_t_ref[...] = jnp.transpose(outer_ref[...])
+    place_row = lax.broadcasted_iota(jnp.int32, (128, 128), 0)
+    place_lane = lax.broadcasted_iota(jnp.int32, (128, 128), 1)
+    take = (place_row == place_lane + 5) & (place_lane < 2 * own)
+    router = dot(small_ref[...], take.astype(bf16))
+    router_ref[...] = router.astype(bf16)
+    router_t_ref[...] = jnp.transpose(router).astype(bf16)
     inner_acc[...] = jnp.zeros_like(inner_acc)
     outer_acc[...] = jnp.zeros_like(outer_acc)
     bias_grad_ref[...] = jnp.zeros_like(bias_grad_ref)
@@ -550,8 +484,8 @@
 
     def tile(k, t):
         here = pl.ds(pl.multiple_of(t * rows, 16), rows)
-        normed, grad_out = tokens[k, here, :], grads_ref[k, here, :]
-        select = select_ref[k, here, :].astype(f32)
+        normed, grad_out = tokens[k, here, :width], tokens[k, here, width : 2 * width]
+        select = tokens[k, here, 2 * width :].astype(f32)
         lane = lax.broadcasted_iota(jnp.int32, select.shape, 1)
         logits = dot(normed, router_ref[...])
         logits = jnp.where(lane < 2 * own, logits, -1e30)
@@ -628,15 +562,15 @@
         def columns(j, carry):
             some = pl.ds(pl.multiple_of(j * 256, 256), 256)
             outer_acc[:, some] += lax.dot_general(
-                hidden[...], grads_ref[k, :, some], TN, preferred_element_type=f32
+                hidden[...], tokens[k, :, pl.ds(pl.multiple_of(width + j * 256, 256), 256)], TN, preferred_element_type=f32
             )
             inner_acc[:, some] += lax.dot_general(
-                tokens[k], hidden_grad[:, some], TN, preferred_element_type=f32
+                tokens[k, :, :width], hidden_grad[:, some], TN, preferred_element_type=f32
             )
             return carry
 
         lax.fori_loop(0, width // 256, columns, 0)
-        router_grad_ref[...] += lax.dot_general(tokens[k], logit_grad[...], TN, preferred_element_type=f32)
+        router_grad_ref[...] += lax.dot_general(tokens[k, :, :width], logit_grad[...], TN, preferred_element_type=f32)
         return carry
 
     lax.fori_loop(0, planes, step, 0)
@@ -644,7 +578,9 @@
     add_x(planes - 2)
     add_x(planes - 1)
     inner_grad_ref[...] = inner_acc[...].astype(bf16)
-    outer_grad_ref[...] = outer_acc[...].astype(bf16)
+    units = outer_acc.shape[0]
+    outer_grad_ref[0:units, :] = outer_acc[...].astype(bf16)
+    outer_grad_ref[units : units + 16, :] = jnp.broadcast_to(bias_grad_ref[...], (16, width)).astype(bf16)
     total = part[0, 0:rows, :].astype(f32)
     for k in range(1, planes):
         sum_z_copy(k).wait_recv()
@@ -661,11 +597,11 @@
             sum_z_copy(k).wait_send()
 
 
-def experts_of_the_plane(planes, own, normed, grads, select, inner, outer, bias, router):
+def experts_of_the_plane(planes, own, packed, inner, outer, bias, small):
     f32, bf16 = jnp.float32, jnp.bfloat16
-    rows, width = normed.shape
+    rows, wide = packed.shape
     chunk = 4 * rows
-    units = inner.shape[1]
+    width, units = inner.shape
     vmem = pl.BlockSpec(memory_space=pltpu.VMEM)
     dma = pltpu.SemaphoreType.DMA
     flops = 12 * planes * chunk * width * units
@@ -675,14 +611,18 @@
             jax.ShapeDtypeStruct((planes, chunk, width), bf16),
             jax.ShapeDtypeStruct((rows, width), f32),
             jax.ShapeDtypeStruct((width, units), bf16),
-            jax.ShapeDtypeStruct((units, width), bf16),
-            jax.ShapeDtypeStruct((1, units), f32),
+            jax.ShapeDtypeStruct((units + 16, width), bf16),
             jax.ShapeDtypeStruct((width, 128), f32),
         ],
-        in_specs=[vmem] * 10,
-        out_specs=[vmem] * 6,
+        in_specs=[vmem] * 5,
+        out_specs=[vmem] * 5,
         scratch_shapes=[
-            pltpu.VMEM((planes, chunk, width), bf16),
+            pltpu.VMEM((units, width), bf16),
+            pltpu.VMEM((width, units), bf16),
+            pltpu.VMEM((width, 128), bf16),
+            pltpu.VMEM((128, width), bf16),
+            pltpu.VMEM((1, units), f32),
+            pltpu.VMEM((planes, chunk, wide), bf16),
             pltpu.VMEM((planes, chunk, width), bf16),
             pltpu.VMEM((planes, 2 * rows, width), bf16),
             pltpu.VMEM((planes, rows, width), bf16),
@@ -701,7 +641,811 @@
         ),
         cost_estimate=pl.CostEstimate(flops=flops, bytes_accessed=40 * 2**20, transcendentals=0),
         name="experts_of_the_plane",
-    )(normed, grads, select, inner, inner.T, outer, outer.T, bias, router, router.T)
+    )(packed, inner, outer, bias, small)
+
+
+def front_kernel(
+    planes,
+    heads,
+    real,
+    tokens_ref,
+    keys_ref,
+    keep_ref,
+    cotangent_ref,
+    select_ref,
+    small_ref,
+    qkv_part_ref,
+    proj_part_ref,
+    inner_part_ref,
+    small_all,
+    w_qkv_all,
+    w_proj_all,
+    inner_all,
+    normed_in_ref,
+    qkv_ref,
+    attended_ref,
+    middle_ref,
+    packed_ref,
+    up_send,
+    up_recv,
+    down_send,
+    down_recv,
+    x_send,
+    x_recv,
+    c_send,
+    c_recv,
+    spread_send,
+    spread_recv,
+    own_sem,
+    y_send,
+    y_recv,
+):
+    f32, bf16 = jnp.float32, jnp.bfloat16
+    place = Place(planes)
+    rows, width = tokens_ref.shape
+    depth = small_ref.shape[0]
+    half = depth // 2
+    lanes = inner_part_ref.shape[2] // (2 * planes)
+    head_dim = width // heads
+    y, c, z, x = place.y, place.c, place.z, place.x
+    gathered = [small_all, w_qkv_all, w_proj_all]
+
+    def remote(src, dst, send, recv, device):
+        return pltpu.make_async_remote_copy(
+            src_ref=src, dst_ref=dst, send_sem=send, recv_sem=recv, device_id=device, device_id_type=MESH
+        )
+
+    def piece(j, level, across):
+        start = (level * 2 + across) * depth + c * half
+        return gathered[j].at[pl.ds(pl.multiple_of(start, 16), half)]
+
+    def up_copy(j, level):
+        here = piece(j, level, x)
+        return remote(here, here, up_send.at[j, level], up_recv.at[j, level], place.at(y, c, z + 1, x))
+
+    def down_copy(j, level):
+        here = piece(j, level, x)
+        return remote(here, here, down_send.at[j, level], down_recv.at[j, level], place.at(y, c, z - 1, x))
+
+    def x_copy(j, level, across):
+        here = piece(j, level, across)
+        return remote(here, here, x_send.at[j, level], x_recv.at[j, level], place.other_x())
+
+    def c_copy(j, level, across):
+        here = piece(j, level, across)
+        at = level * 2 + across
+        return remote(here, here, c_send.at[j, at], c_recv.at[j, at], place.other_core())
+
+    def sibling_piece(j, level, across):
+        start = (level * 2 + across) * depth + (1 - c) * half
+        here = gathered[j].at[pl.ds(pl.multiple_of(start, 16), half)]
+        at = level * 2 + across
+        return remote(here, here, c_send.at[j, at], c_recv.at[j, at], place.other_core())
+
+    def columns_of(f):
+        return pl.ds(pl.multiple_of(f * lanes, 128), lanes)
+
+    here_rows = pl.ds(pl.multiple_of((z * 2 + x) * depth, 16), depth)
+    my_units = pl.ds(pl.multiple_of(y * lanes, 128), lanes)
+
+    def spread_copy(k, r):
+        level, across = lax.rem(z + k, planes), (x + r) % 2
+        return remote(
+            inner_part_ref.at[c * 2 + y, :, columns_of(level * 2 + across)],
+            inner_all.at[here_rows, my_units],
+            spread_send.at[k, r],
+            spread_recv.at[k, r],
+            place.at(y, c, level, across),
+        )
+
+    own_copy = pltpu.make_async_copy(
+        inner_part_ref.at[c * 2 + y, :, columns_of(z * 2 + x)], inner_all.at[here_rows, my_units], own_sem
+    )
+    y_copy = remote(inner_all.at[:, my_units], inner_all.at[:, my_units], y_send, y_recv, place.other_y())
+    their_units = pl.ds(pl.multiple_of((1 - y) * lanes, 128), lanes)
+    from_y = remote(inner_all.at[:, their_units], inner_all.at[:, their_units], y_send, y_recv, place.other_y())
+
+    others = [(k, r) for k in range(planes) for r in range(2) if k or r]
+    partners = [place.other_core(), place.other_y()]
+    partners += [place.at(y, c, lax.rem(z + k, planes), (x + r) % 2) for k, r in others]
+    greet(partners)
+
+    small_all[here_rows, :] = small_ref[...]
+    w_qkv_all[here_rows, :] = qkv_part_ref[...]
+    w_proj_all[here_rows, :] = proj_part_ref[...]
+
+    def forward(level, flows):
+        for j in flows:
+            x_copy(j, level, x).start()
+
+    def line(flows):
+        @pl.when(z < planes - 1)
+        def _():
+            for j in flows:
+                up_copy(j, z).start()
+
+        @pl.when(z > 0)
+        def _():
+            for j in flows:
+                down_copy(j, z).start()
+
+        forward(z, flows)
+
+    def hops(flows):
+        for h in range(1, planes):
+            @pl.when(z >= h)
+            def _():
+                for j in flows:
+                    up_copy(j, z - h).wait_recv()
+
+                @pl.when(z < planes - 1)
+                def _():
+                    for j in flows:
+                        up_copy(j, z - h).start()
+
+                forward(z - h, flows)
+                for j in flows:
+                    c_copy(j, z - h, x).start()
+
+            @pl.when(z + h < planes)
+            def _():
+                for j in flows:
+                    down_copy(j, z + h).wait_recv()
+
+                @pl.when(z > 0)
+                def _():
+                    for j in flows:
+                        down_copy(j, z + h).start()
+
+                forward(z + h, flows)
+                for j in flows:
+                    c_copy(j, z + h, x).start()
+
+    def arrive(flows):
+        for level in range(planes):
+            for j in flows:
+                x_copy(j, level, 1 - x).wait_recv()
+                c_copy(j, level, 1 - x).start()
+
+    def gather_done(flows):
+        for level in range(planes):
+            for j in flows:
+                sibling_piece(j, level, 1 - x).wait_recv()
+
+            @pl.when(level != z)
+            def _():
+                for j in flows:
+                    sibling_piece(j, level, x).wait_recv()
+
+    line([0, 1])
+    line([2])
+    values = tokens_ref[...].astype(f32)
+    normal, _ = norm_parts(values)
+    hops([0, 1])
+    hops([2])
+    own_copy.start()
+    for k, r in others:
+        spread_copy(k, r).start()
+    arrive([0, 1])
+    gather_done([0, 1])
+    vectors = jnp.transpose(small_all[...].astype(f32))
+    normed_in = (normal * vectors[0:1] + vectors[1:2]).astype(bf16)
+    normed_in_ref[...] = normed_in
+    for j in range(3):
+        part = slice(j * width, (j + 1) * width)
+        qkv_ref[:, part] = dot(normed_in, w_qkv_all[:, part]).astype(bf16)
+    arrive([2])
+    lane = lax.broadcasted_iota(jnp.int32, (rows, 2 * head_dim), 1)
+    usable = keys_ref[...] > 0
+    for pair in range(heads // 2):
+        at = pair * 2 * head_dim
+        queries = qkv_ref[:, at : at + 2 * head_dim]
+        keys = qkv_ref[:, width + at : width + at + 2 * head_dim]
+        held = qkv_ref[:, 2 * width + at : 2 * width + at + 2 * head_dim]
+        outs = []
+        for side in range(2):
+            only = (lane < head_dim) if side == 0 else (lane >= head_dim)
+            scores = lax.dot_general(
+                jnp.where(only, queries, 0).astype(bf16), keys, NT, preferred_element_type=f32
+            )
+            scores = jnp.where(usable, scores * head_dim ** (-0.5), masked_score)
+            shifted = jnp.exp(scores - jnp.max(scores, axis=1, keepdims=True))
+            probs = (shifted / jnp.sum(shifted, axis=1, keepdims=True)).astype(bf16)
+            outs.append(dot(probs, held))
+        attended_ref[:, at : at + 2 * head_dim] = jnp.where(lane < head_dim, outs[0], outs[1]).astype(bf16)
+    own_copy.wait()
+    for k, r in others:
+        spread_copy(k, r).wait_recv()
+    y_copy.start()
+    gather_done([2])
+    middle = values + dot(attended_ref[...], w_proj_all[...]) + vectors[2:3]
+    middle_ref[...] = middle
+    normal_mid, _ = norm_parts(middle)
+    normed = normal_mid * vectors[3:4] + vectors[4:5]
+    row = lax.broadcasted_iota(jnp.int32, normed.shape, 0)
+    packed_ref[:, :width] = jnp.where(row < real, normed, 0.0).astype(bf16)
+    packed_ref[:, width : 2 * width] = (cotangent_ref[...].astype(f32) * keep_ref[...]).astype(bf16)
+    packed_ref[:, 2 * width :] = select_ref[...]
+    from_y.wait_recv()
+    y_copy.wait_send()
+    for k, r in others:
+        spread_copy(k, r).wait_send()
+    for j in range(3):
+        for level in range(planes):
+            x_copy(j, level, x).wait_send()
+            c_copy(j, level, 1 - x).wait_send()
+
+            @pl.when(level != z)
+            def _():
+                c_copy(j, level, x).wait_send()
+
+            @pl.when((z >= level) & (z < planes - 1))
+            def _():
+                up_copy(j, level).wait_send()
+
+            @pl.when((z <= level) & (z > 0))
+            def _():
+                down_copy(j, level).wait_send()
+
+
+def front(planes, real, tokens, keys, keep, cotangent, select, small, w_qkv, w_proj, w_in):
+    f32, bf16 = jnp.float32, jnp.bfloat16
+    rows, width = tokens.shape
+    lanes = w_in.shape[2] // (2 * planes)
+    shape = jax.ShapeDtypeStruct
+    vmem = pl.BlockSpec(memory_space=pltpu.VMEM)
+    dma = pltpu.SemaphoreType.DMA
+    return pl.pallas_call(
+        functools.partial(front_kernel, planes, HEADS, real),
+        out_shape=[
+            shape((width, small.shape[1]), bf16),
+            shape((width, 3 * width), bf16),
+            shape((width, width), bf16),
+            shape((width, 2 * lanes), bf16),
+            shape((rows, width), bf16),
+            shape((rows, 3 * width), bf16),
+            shape((rows, width), bf16),
+            shape((rows, width), f32),
+            shape((rows, 2 * width + 128), bf16),
+        ],
+        in_specs=[vmem] * 8 + [pl.BlockSpec(memory_space=pl.ANY)],
+        out_specs=[vmem] * 9,
+        scratch_shapes=[dma((3, planes))] * 6
+        + [dma((3, 2 * planes))] * 2
+        + [dma((planes, 2))] * 2
+        + [dma] * 3,
+        compiler_params=pltpu.CompilerParams(
+            collective_id=2, has_side_effects=True, vmem_limit_bytes=60 * 2**20
+        ),
+        cost_estimate=pl.CostEstimate(flops=2**32, bytes_accessed=40 * 2**20, transcendentals=0),
+        name="dense_weights_and_attention",
+    )(tokens, keys, keep, cotangent, select, small, w_qkv, w_proj, w_in)
+
+
+def back_kernel(planes, heads, own, groups, real, *refs):
+    (
+        row_grad_ref,
+        packed_ref,
+        middle_ref,
+        tokens_ref,
+        normed_in_ref,
+        qkv_ref,
+        attended_ref,
+        small_ref,
+        w_qkv_ref,
+        w_proj_ref,
+        keys_ref,
+        keep_ref,
+        mix_ref,
+        inner_ref,
+        outer_ref,
+        router_grad_ref,
+    ) = refs[:16]
+    mixed_ref, token_grad_ref, qkv_out, proj_out, small_out, inner_out, outer_out = refs[16:23]
+    (
+        grad_attended,
+        grad_qkv,
+        mix_x,
+        mix_z,
+        mix_from_core,
+        mix_from_x,
+        mix_from_z,
+        inner_from_y,
+        inner_sum,
+        outer_from_y,
+        held,
+        held_small,
+        from_core,
+        from_core_small,
+        from_x,
+        from_x_small,
+        from_z,
+        from_z_small,
+        plane_sum,
+        plane_sum_small,
+        from_y,
+        from_y_small,
+        final,
+        final_small,
+    ) = refs[23:47]
+    (
+        mix_c_sem,
+        mix_x_sem,
+        mix_z_send,
+        mix_z_recv,
+        inner_y_sem,
+        spread_send,
+        spread_recv,
+        inner_back_sem,
+        inner_core_sem,
+        outer_y_sem,
+        outer_c_sem,
+        own_sem,
+        flow_c_sem,
+        flow_x_sem,
+        flow_z_send,
+        flow_z_recv,
+        flow_y_sem,
+        flow_end_sem,
+    ) = refs[47:]
+    f32, bf16 = jnp.float32, jnp.bfloat16
+    place = Place(planes)
+    y, c, z, x = place.y, place.c, place.z, place.x
+    rows, width = middle_ref.shape
+    depth = width // (2 * planes)
+    half = depth // 2
+    lanes = inner_ref.shape[1] // own
+    head_dim = width // heads
+    pair_width = 2 * head_dim
+    small_at = groups + 1
+
+    def remote(src, dst, send, recv, device):
+        return pltpu.make_async_remote_copy(
+            src_ref=src, dst_ref=dst, send_sem=send, recv_sem=recv, device_id=device, device_id_type=MESH
+        )
+
+    def swap(src, dst, sem, device):
+        return remote(src, dst, sem.at[0], sem.at[1], device)
+
+    def of_flow(j, many, alone):
+        return alone if j == small_at else many.at[j]
+
+    mine, theirs = pl.ds(pl.multiple_of(c * half, 16), half), pl.ds(pl.multiple_of((1 - c) * half, 16), half)
+
+    def flow_c(j):
+        source = of_flow(j, held, held_small)
+        return swap(
+            source.at[:, :, theirs], of_flow(j, from_core, from_core_small), flow_c_sem.at[j], place.other_core()
+        )
+
+    def flow_x(j):
+        source = of_flow(j, held, held_small)
+        return swap(source.at[:, 1 - x, mine], of_flow(j, from_x, from_x_small), flow_x_sem.at[j], place.other_x())
+
+    def flow_z(j, k):
+        level = lax.rem(z + k, planes)
+        source = of_flow(j, held, held_small)
+        return remote(
+            source.at[level, x, mine],
+            of_flow(j, from_z, from_z_small).at[k],
+            flow_z_send.at[j, k],
+            flow_z_recv.at[j, k],
+            place.level(k),
+        )
+
+    def flow_y(j):
+        return swap(
+            of_flow(j, plane_sum, plane_sum_small),
+            of_flow(j, from_y, from_y_small),
+            flow_y_sem.at[j],
+            place.other_y(),
+        )
+
+    def flow_end(j):
+        here = of_flow(j, final, final_small).at[mine]
+        return swap(here, here, flow_end_sem.at[j], place.other_core())
+
+    def flow_core_sum(j):
+        flow_c(j).wait_recv()
+        kept = of_flow(j, held, held_small)
+        total = kept[:, :, mine, :].astype(f32) + of_flow(j, from_core, from_core_small)[...].astype(f32)
+        kept[:, :, mine, :] = total.astype(bf16)
+        flow_x(j).start()
+
+    def flow_x_sum(j):
+        flow_x(j).wait_recv()
+        kept = of_flow(j, held, held_small)
+        total = kept[:, x, mine, :].astype(f32) + of_flow(j, from_x, from_x_small)[...].astype(f32)
+        kept[:, x, mine, :] = total.astype(bf16)
+        for k in range(1, planes):
+            flow_z(j, k).start()
+
+    def flow_z_sum(j):
+        kept = of_flow(j, held, held_small)
+        total = kept[z, x, mine, :].astype(f32)
+        for k in range(1, planes):
+            flow_z(j, k).wait_recv()
+            total = total + of_flow(j, from_z, from_z_small)[k].astype(f32)
+        of_flow(j, plane_sum, plane_sum_small)[...] = total.astype(bf16)
+        flow_y(j).start()
+
+    def flow_y_sum(j):
+        flow_y(j).wait_recv()
+        total = of_flow(j, plane_sum, plane_sum_small)[...].astype(f32)
+        total = total + of_flow(j, from_y, from_y_small)[...].astype(f32)
+        of_flow(j, final, final_small)[mine, :] = total.astype(bf16)
+        flow_end(j).start()
+
+    def mix_c():
+        return swap(mix_ref.at[:, pl.ds(2 * rows, 2 * rows)], mix_from_core, mix_c_sem, place.other_core())
+
+    def mix_to_x():
+        return swap(mix_x, mix_from_x, mix_x_sem, place.other_x())
+
+    def mix_to_z(k):
+        return remote(mix_z.at[k], mix_from_z.at[k], mix_z_send.at[k], mix_z_recv.at[k], place.level(-k))
+
+    def mix_core_sum():
+        mix_c().wait_recv()
+        for k in range(planes):
+            total = mix_ref[k, rows : 2 * rows, :].astype(f32) + mix_from_core[k, rows:, :].astype(f32)
+            mix_x[k] = total.astype(bf16)
+        mix_to_x().start()
+        for k in range(planes):
+            total = mix_ref[k, :rows, :].astype(f32) + mix_from_core[k, :rows, :].astype(f32)
+            mix_z[k] = total.astype(bf16)
+
+    def mix_x_sum():
+        mix_to_x().wait_recv()
+        for k in range(planes):
+            mix_z[k] = (mix_z[k].astype(f32) + mix_from_x[k].astype(f32)).astype(bf16)
+            if k:
+                mix_to_z(k).start()
+
+    my_units = pl.ds(pl.multiple_of(y * lanes, 128), lanes)
+    their_units = pl.ds(pl.multiple_of((1 - y) * lanes, 128), lanes)
+    my_expert, their_expert = c * 2 + y, c * 2 + 1 - y
+    my_columns = pl.ds(pl.multiple_of((z * 2 + x) * lanes, 128), lanes)
+
+    def inner_y():
+        return swap(inner_ref.at[:, their_units], inner_from_y, inner_y_sem, place.other_y())
+
+    def shard_rows(f):
+        return pl.ds(pl.multiple_of(f * depth, 16), depth)
+
+    def spread(k, r):
+        level, across = lax.rem(z + k, planes), (x + r) % 2
+        return remote(
+            inner_sum.at[shard_rows(level * 2 + across)],
+            inner_out.at[my_expert, :, my_columns],
+            spread_send.at[k, r],
+            spread_recv.at[k, r],
+            place.at(y, c, level, across),
+        )
+
+    own_copy = pltpu.make_async_copy(
+        inner_sum.at[shard_rows(z * 2 + x)], inner_out.at[my_expert, :, my_columns], own_sem
+    )
+
+    def inner_back():
+        here = inner_out.at[my_expert]
+        return swap(here, here, inner_back_sem, place.other_y())
+
+    def inner_core(expert, at):
+        here = inner_out.at[expert]
+        return swap(here, here, inner_core_sem.at[at], place.other_core())
+
+    def outer_y():
+        return swap(outer_ref, outer_from_y, outer_y_sem, place.other_y())
+
+    def outer_c():
+        here = outer_out.at[c]
+        return swap(here, here, outer_c_sem, place.other_core())
+
+    others = [(k, r) for k in range(planes) for r in range(2) if k or r]
+
+    def inner_y_sum():
+        inner_y().wait_recv()
+        total = inner_ref[:, my_units].astype(f32) + inner_from_y[...].astype(f32)
+        inner_sum[...] = total.astype(bf16)
+        own_copy.start()
+        for k, r in others:
+            spread(k, r).start()
+        outer_y().start()
+
+    def inner_spread_done():
+        own_copy.wait()
+        for k, r in others:
+            spread(k, r).wait_recv()
+        inner_back().start()
+        inner_core(my_expert, 0).start()
+
+    def outer_y_sum():
+        outer_y().wait_recv()
+        total = outer_ref[...].astype(f32) + outer_from_y[...].astype(f32)
+        outer_out[c] = total.astype(bf16)
+        outer_c().start()
+
+    partners = [place.other_core(), place.other_y()]
+    partners += [place.at(y, c, lax.rem(z + k, planes), (x + r) % 2) for k, r in others]
+    greet(partners)
+    inner_y().start()
+    mix_c().start()
+
+    vectors = jnp.transpose(small_ref[...].astype(f32))
+    gain_first, gain_second = vectors[0:1], vectors[3:4]
+    place_row = lax.broadcasted_iota(jnp.int32, (128, 128), 0)
+    place_lane = lax.broadcasted_iota(jnp.int32, (128, 128), 1)
+
+    def lanes_from(first):
+        take = (place_row == place_lane + first) & (place_lane < 2 * own)
+        return dot(small_ref[...], take.astype(bf16)).astype(bf16)
+
+    router, outer_bias = lanes_from(5), lanes_from(5 + 2 * own)
+    normed_mid, grad_out = packed_ref[:, :width], packed_ref[:, width : 2 * width]
+    select = packed_ref[:, 2 * width :].astype(f32)
+    lane = lax.broadcasted_iota(jnp.int32, select.shape, 1)
+    logits = jnp.where(lane < 2 * own, dot(normed_mid, router), -1e30)
+    routing = jnp.exp(logits - jnp.max(logits, axis=1, keepdims=True))
+    routing = routing / jnp.sum(routing, axis=1, keepdims=True)
+    gates = routing * select
+    bias_gate = select * dot(grad_out, outer_bias)
+    bias_logits = routing * (bias_gate - jnp.sum(routing * bias_gate, axis=1, keepdims=True))
+    bias_logits = bias_logits.astype(bf16)
+    router_grad = router_grad_ref[...] + lax.dot_general(
+        normed_mid, bias_logits, TN, preferred_element_type=f32
+    )
+    outer_bias_grad = lax.dot_general(gates.astype(bf16), grad_out, TN, preferred_element_type=f32)
+    grad_normed_mid = row_grad_ref[...] + lax.dot_general(bias_logits, router, NT, preferred_element_type=f32)
+    normal_mid, rstd_mid = norm_parts(middle_ref[...])
+    gain_second_grad = jnp.sum(grad_normed_mid * normal_mid, axis=0, keepdims=True)
+    bias_second_grad = jnp.sum(grad_normed_mid, axis=0, keepdims=True)
+    grad_middle = grad_out.astype(f32) + norm_back(grad_normed_mid, normal_mid, rstd_mid, gain_second)
+    grad_proj = grad_middle.astype(bf16)
+    proj_bias_grad = jnp.sum(grad_proj.astype(f32), axis=0, keepdims=True)
+    mix_core_sum()
+
+    def hold(j, value):
+        held[j] = value.astype(bf16).reshape(planes, 2, depth, width)
+        flow_c(j).start()
+
+    hold(0, lax.dot_general(attended_ref[...], grad_proj, TN, preferred_element_type=f32))
+    grad_attended[...] = lax.dot_general(grad_proj, w_proj_ref[...], NT, preferred_element_type=f32).astype(bf16)
+    flow_core_sum(0)
+
+    pair_lane = lax.broadcasted_iota(jnp.int32, (rows, pair_width), 1)
+    usable = keys_ref[...] > 0
+    scaling = head_dim ** (-0.5)
+    group_width = width // groups
+
+    def pair_back(pair):
+        at = pair * pair_width
+        group, inside = at // group_width, at % group_width
+        queries = qkv_ref[:, at : at + pair_width]
+        keys = qkv_ref[:, width + at : width + at + pair_width]
+        values = qkv_ref[:, 2 * width + at : 2 * width + at + pair_width]
+        grads = grad_attended[:, at : at + pair_width]
+        found = []
+        for side in range(2):
+            only = (pair_lane < head_dim) if side == 0 else (pair_lane >= head_dim)
+            some_queries = jnp.where(only, queries, 0).astype(bf16)
+            some_grads = jnp.where(only, grads, 0).astype(bf16)
+            scores = lax.dot_general(some_queries, keys, NT, preferred_element_type=f32)
+            scores = jnp.where(usable, scores * scaling, masked_score)
+            shifted = jnp.exp(scores - jnp.max(scores, axis=1, keepdims=True))
+            probs = shifted / jnp.sum(shifted, axis=1, keepdims=True)
+            grad_probs = lax.dot_general(some_grads, values, NT, preferred_element_type=f32)
+            grad_scores = probs * (grad_probs - jnp.sum(probs * grad_probs, axis=1, keepdims=True))
+            grad_scores = grad_scores.astype(bf16)
+            found.append(
+                (
+                    dot(grad_scores, keys),
+                    lax.dot_general(grad_scores, some_queries, TN, preferred_element_type=f32),
+                    lax.dot_general(probs.astype(bf16), some_grads, TN, preferred_element_type=f32),
+                )
+            )
+        grad_queries = jnp.where(pair_lane < head_dim, found[0][0], found[1][0]) * scaling
+        grad_keys = (found[0][1] + found[1][1]) * scaling
+        grad_values = found[0][2] + found[1][2]
+        for part, value in enumerate((grad_queries, grad_keys, grad_values)):
+            start = part * group_width + inside
+            grad_qkv[group, :, start : start + pair_width] = value.astype(bf16)
+
+    def group_back(group):
+        per_group = heads // 2 // groups
+        for pair in range(group * per_group, (group + 1) * per_group):
+            pair_back(pair)
+        hold(
+            1 + group,
+            lax.dot_general(normed_in_ref[...], grad_qkv[group], TN, preferred_element_type=f32),
+        )
+
+    group_back(0)
+    inner_y_sum()
+    flow_core_sum(1)
+    for group in range(1, groups):
+        group_back(group)
+        if group == 1:
+            mix_x_sum()
+            flow_x_sum(0)
+        flow_core_sum(1 + group)
+    flow_x_sum(1)
+
+    grad_normed_in = jnp.zeros((rows, width), f32)
+    for group in range(groups):
+        for part in range(3):
+            grad_normed_in = grad_normed_in + lax.dot_general(
+                grad_qkv[group, :, part * group_width : (part + 1) * group_width],
+                w_qkv_ref[:, part * width + group * group_width : part * width + (group + 1) * group_width],
+                NT,
+                preferred_element_type=f32,
+            )
+    normal_first, rstd_first = norm_parts(tokens_ref[...].astype(f32))
+    gain_first_grad = jnp.sum(grad_normed_in * normal_first, axis=0, keepdims=True)
+    bias_first_grad = jnp.sum(grad_normed_in, axis=0, keepdims=True)
+    token_grad = grad_middle + norm_back(grad_normed_in, normal_first, rstd_first, gain_first)
+    token_grad_ref[...] = token_grad.astype(bf16)[:real]
+    vector_rows = jnp.concatenate(
+        [
+            gain_first_grad,
+            bias_first_grad,
+            proj_bias_grad,
+            gain_second_grad,
+            bias_second_grad,
+            jnp.zeros((3, width), f32),
+            outer_bias_grad[:8],
+            jnp.zeros((112, width), f32),
+        ],
+        axis=0,
+    )
+    vector_grads = jnp.transpose(vector_rows) + pltpu.roll(router_grad, 16, 1)
+    held_small[...] = vector_grads.astype(bf16).reshape(planes, 2, depth, 128)
+    flow_c(small_at).start()
+    inner_spread_done()
+    flow_core_sum(small_at)
+    outer_y_sum()
+    for group in range(1, groups):
+        flow_x_sum(1 + group)
+    flow_z_sum(0)
+    flow_x_sum(small_at)
+    mixture = mix_z[0].astype(f32) + dot(gates.astype(bf16), jnp.transpose(outer_bias.astype(f32)).astype(bf16))
+    for k in range(1, planes):
+        mix_to_z(k).wait_recv()
+        mixture = mixture + mix_from_z[k].astype(f32)
+    mixed = (keep_ref[...] * (middle_ref[...] + mixture)).astype(bf16)
+    mixed_ref[...] = mixed[:real]
+    flow_y_sum(0)
+    for group in range(groups):
+        flow_z_sum(1 + group)
+    flow_z_sum(small_at)
+    inner_back().wait_recv()
+    inner_core(their_expert, 1).start()
+    for group in range(groups):
+        flow_y_sum(1 + group)
+    flow_y_sum(small_at)
+
+    def arrived(j):
+        here = of_flow(j, final, final_small).at[theirs]
+        swap(here, here, flow_end_sem.at[j], place.other_core()).wait_recv()
+
+    arrived(0)
+    proj_out[...] = final[0]
+    for group in range(groups):
+        arrived(1 + group)
+        for part in range(3):
+            start = part * width + group * group_width
+            qkv_out[:, start : start + group_width] = final[
+                1 + group, :, part * group_width : (part + 1) * group_width
+            ]
+    arrived(small_at)
+    small_out[...] = final_small[...].astype(f32)
+    outer_theirs = outer_out.at[1 - c]
+    swap(outer_theirs, outer_theirs, outer_c_sem, place.other_core()).wait_recv()
+    for at, expert in enumerate(((1 - c) * 2 + y, (1 - c) * 2 + 1 - y)):
+        inner_core(expert, at).wait_recv()
+
+    mix_c().wait_send()
+    mix_to_x().wait_send()
+    inner_y().wait_send()
+    inner_back().wait_send()
+    inner_core(my_expert, 0).wait_send()
+    inner_core(their_expert, 1).wait_send()
+    outer_y().wait_send()
+    outer_c().wait_send()
+    for k, r in others:
+        spread(k, r).wait_send()
+    for k in range(1, planes):
+        mix_to_z(k).wait_send()
+    for j in range(groups + 2):
+        flow_c(j).wait_send()
+        flow_x(j).wait_send()
+        for k in range(1, planes):
+            flow_z(j, k).wait_send()
+        flow_y(j).wait_send()
+        flow_end(j).wait_send()
+
+
+def back(planes, own, real, *args):
+    f32, bf16 = jnp.float32, jnp.bfloat16
+    (
+        row_grad,
+        packed,
+        middle,
+        tokens,
+        normed_in,
+        qkv,
+        attended,
+        small,
+        w_qkv,
+        w_proj,
+        keys,
+        keep,
+        mix_parts,
+        inner_grad,
+        outer_grad,
+        router_grad,
+    ) = args
+    rows, width = middle.shape
+    depth = width // (2 * planes)
+    half = depth // 2
+    lanes = inner_grad.shape[1] // own
+    tall = outer_grad.shape[0]
+    pairs = HEADS // 2
+    groups = 3 if pairs % 3 == 0 and (pairs // 3) * 2 * (width // HEADS) % 128 == 0 else 1
+    flows = groups + 1
+    shape = jax.ShapeDtypeStruct
+    vmem = pl.BlockSpec(memory_space=pltpu.VMEM)
+    dma = pltpu.SemaphoreType.DMA
+
+    def both(*dims):
+        return [pltpu.VMEM((flows, *dims, width), bf16), pltpu.VMEM((*dims, 128), bf16)]
+
+    return pl.pallas_call(
+        functools.partial(back_kernel, planes, HEADS, own, groups, real),
+        out_shape=[
+            shape((real, width), bf16),
+            shape((real, width), bf16),
+            shape((depth, 3 * width), bf16),
+            shape((depth, width), bf16),
+            shape((depth, 128), f32),
+            shape((2 * own, depth, 2 * planes * lanes), bf16),
+            shape((2, tall, width), bf16),
+        ],
+        in_specs=[vmem] * 16,
+        out_specs=[vmem] * 7,
+        scratch_shapes=[
+            pltpu.VMEM((rows, width), bf16),
+            pltpu.VMEM((groups, rows, 3 * width // groups), bf16),
+            pltpu.VMEM((planes, rows, width), bf16),
+            pltpu.VMEM((planes, rows, width), bf16),
+            pltpu.VMEM((planes, 2 * rows, width), bf16),
+            pltpu.VMEM((planes, rows, width), bf16),
+            pltpu.VMEM((planes, rows, width), bf16),
+            pltpu.VMEM((width, lanes), bf16),
+            pltpu.VMEM((width, lanes), bf16),
+            pltpu.VMEM((tall, width), bf16),
+        ]
+        + both(planes, 2, depth)
+        + both(planes, 2, half)
+        + both(planes, half)
+        + both(planes, half)
+        + both(half)
+        + both(half)
+        + both(depth)
+        + [dma((2,))] * 2
+        + [dma((planes,))] * 2
+        + [dma((2,))]
+        + [dma((planes, 2))] * 2
+        + [dma((2,)), dma((2, 2)), dma((2,)), dma((2,)), dma]
+        + [dma((flows + 1, 2))] * 2
+        + [dma((flows + 1, planes))] * 2
+        + [dma((flows + 1, 2))] * 2,
+        compiler_params=pltpu.CompilerParams(
+            collective_id=3, has_side_effects=True, vmem_limit_bytes=60 * 2**20
+        ),
+        cost_estimate=pl.CostEstimate(flops=2**33, bytes_accessed=40 * 2**20, transcendentals=0),
+        name="attention_backward_and_sums",
+    )(*args)
 
 
 def norm_parts(values):
@@ -743,14 +1487,8 @@
     slice_width = w_out.shape[1]
     planes = hidden // slice_width // 2
     own = experts // 2
-    head_dim = width // HEADS
-    scaling = head_dim ** (-0.5)
     s = lax.axis_index("seq")
-    f = lax.axis_index("fsdp")
     core = s % 2
-    z, x = f // 2, f % 2
-    order = shard_order(planes)
-
     small = jnp.concatenate(
         [
             jnp.stack([norm1_gain, norm1_bias, proj_bias, norm2_gain, norm2_bias], axis=1),
@@ -760,187 +1498,71 @@
         axis=1,
     )
     small = jnp.pad(small, ((0, 0), (0, 128 - small.shape[1])))
-    dense = jnp.concatenate([small, w_qkv, w_proj], axis=1)
-    dense = gather_fsdp(dense, planes).reshape(2 * planes, depth, dense.shape[1])
-    dense = jnp.take(dense, order, axis=0).reshape(width, dense.shape[2])
-    small, full_qkv, full_proj = jnp.split(dense, [128, 128 + w_qkv.shape[1]], axis=1)
-    vectors = small[:, :5].T.astype(f32)
-    gain_first, bias_first, bias_proj, gain_second, bias_second = [vectors[i] for i in range(5)]
-    full_router = small[:, 5 : 5 + experts]
-    full_b_out = small[:, 5 + experts : 5 + 2 * experts].T.astype(f32)
-
-    own_mask = lax.dynamic_slice_in_dim(key_mask, s, 1, 0)
-    keep_rows = own_mask.reshape(rows, 1).astype(f32)
-    usable = (own_mask > 0)[:, None, :]
-    chosen = expert_ids.reshape(rows, 2)
+    own_mask = lax.dynamic_slice_in_dim(key_mask, s, 1, 0).astype(f32)
     selected = jnp.sum(
-        (chosen[:, :, None] == jnp.arange(experts, dtype=jnp.int32)).astype(f32), axis=1
-    )
-    grad_out = cotangent.astype(f32).reshape(rows, width) * keep_rows
+        (expert_ids[0][:, :, None] == jnp.arange(experts, dtype=jnp.int32)).astype(f32), axis=1
+    )
     padded = (rows + 15) // 16 * 16
     extra = ((0, padded - rows), (0, 0))
-    packed = jnp.concatenate(
-        [grad_out.astype(bf16), jnp.pad(selected, ((0, 0), (0, 128 - experts))).astype(bf16)],
-        axis=1,
-    )
-    packed = gather_plane(jnp.pad(packed, extra), planes)
-    packed = packed.reshape(planes, 4 * padded, width + 128)
-    all_grad_out, all_selected = packed[..., :width], packed[..., width:]
-
-    mine_in = lax.dynamic_slice_in_dim(w_in, core * own, own, 0)
-    mine_in = mine_in.reshape(own, depth, 2 * planes, slice_width).transpose(2, 0, 1, 3)
-    mine_in = jnp.take(mine_in, order, axis=0).reshape(planes, 2, own, depth, slice_width)
-    across = lax.ppermute(mine_in[:, 1], "fsdp", x_swap(planes))
-    pairs = jnp.stack([mine_in[:, 0], across], axis=1)
-    got = [pairs[0]] + [
-        lax.ppermute(pairs[k], "fsdp", z_shift(planes, -k)) for k in range(1, planes)
-    ]
-    got = jnp.stack(got).reshape(2 * planes, own, depth, slice_width)
-    up_order = ((jnp.arange(2 * planes, dtype=jnp.int32) // 2 - z) % planes) * 2 + (
-        x ^ (jnp.arange(2 * planes, dtype=jnp.int32) % 2)
-    )
-    inner = jnp.take(got, up_order, axis=0).transpose(0, 2, 1, 3).reshape(width, own * slice_width)
+    wide_tokens = jnp.pad(tokens[0], extra)
+    keys = jnp.pad(own_mask, ((0, 0), (0, padded - rows)))
+    keep = keys.reshape(padded, 1)
+    small, full_qkv, full_proj, inner, normed_in, qkv, attended, middle, packed = front(
+        planes,
+        rows,
+        wide_tokens,
+        keys,
+        keep,
+        jnp.pad(cotangent[0], extra),
+        jnp.pad(selected, ((0, padded - rows), (0, 128 - experts))).astype(bf16),
+        small,
+        w_qkv,
+        w_proj,
+        w_in,
+    )
     outer = lax.dynamic_slice_in_dim(w_out, core * own, own, 0).reshape(own * slice_width, width)
     inner_bias = lax.dynamic_slice_in_dim(b_in, core * own, own, 0)
     inner_bias = inner_bias.reshape(1, own * slice_width).astype(f32)
-
-    flat_tokens = tokens.astype(f32).reshape(rows, width)
-    normal_first, rstd_first = norm_parts(flat_tokens)
-    normed_in = (normal_first * gain_first + bias_first).astype(bf16)
-    qkv = jnp.dot(normed_in, full_qkv, preferred_element_type=f32).astype(bf16)
-    qkv = qkv.reshape(rows, 3, HEADS, head_dim).transpose(1, 2, 0, 3)
-    queries, key_rows, value_rows = qkv[0], qkv[1], qkv[2]
-    raw = jnp.einsum("had,hbd->hab", queries, key_rows, preferred_element_type=f32) * scaling
-    scores = jnp.where(usable, raw, masked_score)
-    shifted = jnp.exp(scores - jnp.max(scores, axis=-1, keepdims=True))
-    probs = shifted / jnp.sum(shifted, axis=-1, keepdims=True)
-    attended = jnp.einsum("hab,hbd->ahd", probs.astype(bf16), value_rows, preferred_element_type=f32)
-    attended = attended.astype(bf16).reshape(rows, width)
-    middle = flat_tokens + jnp.dot(attended, full_proj, preferred_element_type=f32) + bias_proj
-    normal_mid, rstd_mid = norm_parts(middle)
-    normed_mid = (normal_mid * gain_second + bias_second).astype(bf16)
-
-    wide_router = jnp.pad(full_router, ((0, 0), (0, 128 - experts)))
-    mix_parts, grad_rows, inner_grad, outer_grad, inner_bias_grad, router_grad = experts_of_the_plane(
+    mix_parts, row_grad, inner_grad, outer_grad, router_grad = experts_of_the_plane(
+        planes, own, packed, inner, outer, inner_bias, small
+    )
+    mixed, token_grad, qkv_grad, proj_grad, vector_grads, inner_grad, outer_grad = back(
         planes,
         own,
-        jnp.pad(normed_mid, extra),
-        all_grad_out,
-        all_selected,
-        inner,
-        outer,
-        inner_bias,
-        wide_router,
-    )
-    grad_rows = grad_rows[:rows]
-    router_grad = router_grad[:, :experts]
-    mixture = scatter_plane(mix_parts.reshape(planes, 2, 2, padded, width), planes)[:rows]
-
-    own_routing = softmax_rows(jnp.dot(normed_mid, full_router, preferred_element_type=f32))
-    own_gates = own_routing * selected
-    mixture = mixture + jnp.dot(own_gates, full_b_out, precision=lax.Precision.HIGHEST)
-    mixed = (keep_rows * (middle + mixture)).astype(bf16).reshape(1, rows, width)
-    bias_gate = selected * jnp.einsum(
-        "nd,ed->ne", grad_out, full_b_out, precision=lax.Precision.HIGHEST
-    )
-    bias_logits = (
-        own_routing * (bias_gate - jnp.sum(own_routing * bias_gate, axis=-1, keepdims=True))
-    ).astype(bf16)
-    router_grad = router_grad + jnp.einsum(
-        "nd,ne->de", normed_mid, bias_logits, preferred_element_type=f32
-    )
-    outer_bias_grad = jnp.einsum(
-        "ne,nd->de", own_gates, grad_out, precision=lax.Precision.HIGHEST
-    )
-    grad_normed_mid = grad_rows + jnp.einsum(
-        "ne,de->nd", bias_logits, full_router, preferred_element_type=f32
-    )
-    grad_gain_second = jnp.sum(grad_normed_mid * normal_mid, axis=0)
-    grad_bias_second = jnp.sum(grad_normed_mid, axis=0)
-    grad_middle = grad_out + norm_back(grad_normed_mid, normal_mid, rstd_mid, gain_second)
-    grad_proj = grad_middle.astype(bf16)
-    grad_bias_proj = jnp.sum(grad_proj, axis=0, dtype=f32)
-    grad_proj_weight = jnp.einsum("nd,ne->de", attended, grad_proj, preferred_element_type=f32)
-    vectors = jnp.concatenate(
-        [
-            jnp.stack([grad_gain_second, grad_bias_second, grad_bias_proj], axis=1),
-            router_grad,
-            outer_bias_grad,
-        ],
-        axis=1,
-    )
-    early = jnp.concatenate(
-        [grad_proj_weight, jnp.pad(vectors, ((0, 0), (0, 256 - vectors.shape[1])))], axis=1
-    ).astype(bf16)
-    early = sum_everywhere(early.reshape(2 * planes, depth, width + 256), planes)
-    grad_attended = jnp.einsum("ne,de->nd", grad_proj, full_proj, preferred_element_type=f32)
-    grad_attended = grad_attended.astype(bf16).reshape(rows, HEADS, head_dim)
-    grad_values = jnp.einsum(
-        "hab,ahd->bhd", probs.astype(bf16), grad_attended, preferred_element_type=f32
-    )
-    grad_probs = jnp.einsum("ahd,hbd->hab", grad_attended, value_rows, preferred_element_type=f32)
-    grad_scores = (
-        probs * (grad_probs - jnp.sum(probs * grad_probs, axis=-1, keepdims=True))
-    ).astype(bf16)
-    grad_queries = (
-        jnp.einsum("hab,hbd->ahd", grad_scores, key_rows, preferred_element_type=f32) * scaling
-    )
-    grad_keys = (
-        jnp.einsum("hab,had->bhd", grad_scores, queries, preferred_element_type=f32) * scaling
-    )
-    grad_qkv = jnp.stack([grad_queries, grad_keys, grad_values], axis=1).astype(bf16)
-    grad_qkv = grad_qkv.reshape(rows, 3 * width)
-    grad_qkv_weight = jnp.einsum("nd,ne->de", normed_in, grad_qkv, preferred_element_type=f32)
-    grad_normed_in = jnp.einsum("ne,de->nd", grad_qkv, full_qkv, preferred_element_type=f32)
-    grad_gain_first = jnp.sum(grad_normed_in * normal_first, axis=0)
-    grad_bias_first = jnp.sum(grad_normed_in, axis=0)
-    token_grad = grad_middle + norm_back(grad_normed_in, normal_first, rstd_first, gain_first)
-    token_grad = token_grad.astype(bf16).reshape(1, rows, width)
-    vectors = jnp.stack([grad_gain_first, grad_bias_first], axis=1)
-    late = jnp.concatenate(
-        [grad_qkv_weight, jnp.pad(vectors, ((0, 0), (0, 256 - vectors.shape[1])))], axis=1
-    ).astype(bf16)
-    late = sum_everywhere(late.reshape(2 * planes, depth, 3 * width + 256), planes)
-
-    def both_cores(mine):
-        mine = mine.astype(bf16)
-        other = lax.ppermute(mine, "seq", core_swap)
-        first, second = jnp.where(core == 0, mine, other), jnp.where(core == 0, other, mine)
-        return jnp.concatenate([first, second], axis=0).astype(f32)
-
-    bias_row = jnp.pad(
-        inner_bias_grad.reshape(own, 1, slice_width), ((0, 0), (0, 15), (0, width - slice_width))
-    )
-    outer_grad = jnp.concatenate([outer_grad.reshape(own, slice_width, width), bias_row], axis=1)
-    outer_grad = outer_grad.astype(bf16)
-    outer_grad = outer_grad.astype(f32) + lax.ppermute(outer_grad, "seq", y_swap).astype(f32)
-    outer_grad = both_cores(outer_grad)
-    inner_grad = inner_grad.astype(bf16).reshape(2 * planes, depth, own, slice_width)
-    inner_grad = jnp.take(inner_grad, order, axis=0).reshape(planes, 2, depth, own, slice_width)
-    across = lax.ppermute(inner_grad[:, 1], "fsdp", x_swap(planes))
-    pairs = jnp.stack([inner_grad[:, 0], across], axis=1)
-    got = [pairs[0]] + [
-        lax.ppermute(pairs[k], "fsdp", z_shift(planes, -k)) for k in range(1, planes)
-    ]
-    got = jnp.stack(got).reshape(2 * planes, depth, own, slice_width)
-    inner_grad = jnp.take(got, up_order, axis=0).transpose(2, 1, 0, 3).reshape(own, depth, hidden)
-    inner_grad = inner_grad.astype(f32) + lax.ppermute(inner_grad, "seq", y_swap).astype(f32)
-    inner_grad = both_cores(inner_grad)
+        rows,
+        row_grad,
+        packed,
+        middle,
+        wide_tokens,
+        normed_in,
+        qkv,
+        attended,
+        small,
+        full_qkv,
+        full_proj,
+        keys,
+        keep,
+        mix_parts,
+        inner_grad,
+        outer_grad,
+        router_grad,
+    )
+    units = own * slice_width
     return (
-        mixed,
-        token_grad,
-        late[:, 3 * width],
-        late[:, 3 * width + 1],
-        late[:, : 3 * width],
-        early[:, :width],
-        early[:, width + 2],
-        early[:, width],
-        early[:, width + 1],
-        early[:, width + 3 : width + 3 + experts],
-        inner_grad,
-        outer_grad[:, slice_width, :slice_width],
-        outer_grad[:, :slice_width],
-        early[:, width + 3 + experts : width + 3 + 2 * experts].T,
+        mixed[None],
+        token_grad[None],
+        vector_grads[:, 0],
+        vector_grads[:, 1],
+        qkv_grad.astype(f32),
+        proj_grad.astype(f32),
+        vector_grads[:, 2],
+        vector_grads[:, 3],
+        vector_grads[:, 4],
+        vector_grads[:, 16 : 16 + experts],
+        inner_grad.astype(f32),
+        outer_grad[:, units, :units].reshape(experts, slice_width).astype(f32),
+        outer_grad[:, :units].reshape(experts, slice_width, width).astype(f32),
+        vector_grads[:, 8 : 8 + experts].T,
     )
 
 
@@ -951,7 +1573,7 @@
         tokens, w_in, w_out = args[0], args[12], args[14]
         experts, _, hidden = w_in.shape
         lanes = hidden // n_fsdp
-        whole_tiles = lanes % 128 == 0 and w_in.shape[1] % 16 == 0
+        whole_tiles = lanes % 128 == 0 and w_in.shape[1] % 32 == 0 and 2 * lanes <= tokens.shape[2]
         if n_seq == 4 and experts == n_seq and tokens.shape[0] == 1 and whole_tiles:
             return move_tokens_plan(*args)
         return gather_weights_plan(*args)

time: 589 us -> 344 us (0.58)
  waiting for transfers between devices: 204 us -> 0 us
  Pallas kernels: 110 us -> 312 us
  starting transfers between devices: 85.4 us -> 0 us
  local copies, waits for them, and re-layouts: 81.2 us -> 18.8 us
  other arithmetic: 73 us -> 11.9 us
  matrix products: 27.7 us -> 0 us
    ppermute x42 -> x0, waiting for transfers between devices: 204 us -> none  [the longest x6 42.5 us: move_tokens_plan(): lax.ppermute(pairs[k], 'fsdp', z_shift(planes, -k))]
    pallas_call x0 -> x2, Pallas kernels: none -> 170 us  [the longest x1 107 us: back(): pl.pallas_call(functools.partial(back_kernel, planes, HEADS, own, groups,...]
    ppermute x42 -> x0, starting transfers between devices: 85.4 us -> none  [the longest x6 24.9 us: gather_fsdp(): lax.ppermute(block, 'fsdp', z_shift(planes, k))]
    pallas_call x1, Pallas kernels: 110 us -> 142 us  [experts_of_the_plane(): pl.pallas_call(functools.partial(expert_kernel, planes, own, rows), out_s...]
    gather x9 -> x0, local copies, waits for them, and re-layouts: 31 us -> none  [the longest x2 13.1 us: move_tokens_plan(): dense = jnp.take(dense, order, axis=0).reshape(width, dense.shape[2])]
    another operation x13 -> x0, other arithmetic: 25.5 us -> none  [the longest x3 10.2 us: gather_fsdp(): return jnp.stack([column, across], axis=1)]
    dot_general x17 -> x0, matrix products: 25.2 us -> none  [the longest x1 4.45 us: move_tokens_plan(): jnp.einsum('ne,de->nd', grad_qkv, full_qkv, preferred_element_type=f32)]
    unnamed x170 -> x19, local copies, waits for them, and re-layouts: 15.2 us -> 3.36 us
  transfers between devices with their start and end apart: 42 -> 0, of which waited for: 19 -> 0; matrix products, arithmetic and copies ran while one was open for 26% -> 0% of each run, Pallas kernels for 0% -> 0%
where the time goes in v3:
time: 344 us
  Pallas kernels  312 us (91%)
  local copies, waits for them, and re-layouts  18.8 us (5%)
  other arithmetic  11.9 us (3%)
    pallas_call x1, Pallas kernels, experts_of_the_plane(): pl.pallas_call(functools.partial(expert_kernel, planes, own, rows), out_s...  142 us
    pallas_call x1, Pallas kernels, back(): pl.pallas_call(functools.partial(back_kernel, planes, HEADS, own, groups,...  107 us
    pallas_call x1, Pallas kernels, front(): pl.pallas_call(functools.partial(front_kernel, planes, HEADS, real), out_...  62.7 us

profile of v3, /device:TPU:0, one launch (start us, length us, event | category | flops | bytes accessed | tf_op | source)
XLA Modules:
  0.0 343.7 jit_solution(14164880683554997398)
XLA Ops:
  0.6 0.0 copy-start
  0.7 0.8 dynamic-slice_convert_fusion
  1.5 0.6 pad_bitcast_fusion
  2.1 0.7 convert_reduce_fusion
  2.8 0.7 convert_bitcast_fusion
  3.5 0.6 copy.70
  4.1 2.2 concatenate.3
  6.3 0.1 copy.65
  6.4 0.6 pad.24.small_ref
  7.0 0.1 copy.64
  7.2 0.6 pad.23.select_ref
  7.8 0.8 copy.66.keep_ref.refs_11_
  8.6 1.7 pad.20.tokens_ref.refs_3_
  10.3 1.7 pad.22.cotangent_ref
  12.0 0.0 copy-done
  12.0 1.1 constant_dynamic-slice_fusion
  13.1 62.7 %dense_weights_and_attention.1 = (bf16[768,128]{1,0:T(8,128)(2,1)}, bf16[768,2304]{1,0:T(8,128)(2,1)}, bf16[768,768]{1,0:T(8,128)(2,1)}, bf16[768,768]{1,0:T(8,1...) custom-call(bf16[208,768]{1,0:T(8,128)(2,1)} %pad.20.tokens_ref.refs, ...), custom_call_target="tpu_custom_call" | custom-call | flops 4294967296 | bytes 41943040 | tf_op jit(solution)/shard_map/dense_weights_and_attention/pallas_call | solution.py:898
  75.8 142.2 %experts_of_the_plane.1 = (bf16[4,832,768]{2,1,0:T(8,128)(2,1)}, f32[208,768]{1,0:T(8,128)}, bf16[768,768]{1,0:T(8,128)(2,1)}, bf16[784,768]{1,0:T(8,128)(2,1)}, f32[768,128]{1,0:T(8,128)}) custom-call(bf16[208,1664]{1,0:T(8,128)(2,1)} %get-tuple-element.35.packed_ref.refs_1_, bf16[768,768]{1,0:T(8,128)(2,1)} %get-tuple-element.36.inner_ref, ...), custom_call_target="tpu_custom_call" | custom-call | flops 23555211264 | bytes 41943040 | tf_op jit(solution)/shard_map/experts_of_the_plane/pallas_call | solution.py:608
  218.0 107.5 %attention_backward_and_sums.1 = (bf16[200,768]{1,0:T(8,128)(2,1)}, bf16[200,768]{1,0:T(8,128)(2,1)}, bf16[96,2304]{1,0:T(8,128)(2,1)}, bf16[96,768]{1,0:T(8,128...) custom-call(f32[208,768]{1,0:T(8,128)} %get-tuple-element.38.refs_0_, ...), custom_call_target="tpu_custom_call" | custom-call | flops 8589934592 | bytes 41943040 | tf_op jit(solution)/shard_map/attention_backward_and_sums/pallas_call | solution.py:1403
  325.4 1.8 slice_reduce_fusion
  327.3 0.8 convert_reduce_fusion.1
  328.0 0.0 copy-start.1
  328.0 0.0 copy-start.6
  328.1 0.0 copy-start.3
  328.1 3.3 slice.34
  331.4 0.6 reshape.58
  332.0 0.0 copy-done.1
  332.0 0.1 slice_bitcast_fusion
  332.1 0.7 copy.69
  332.7 0.7 copy.68
  333.4 0.0 copy-done.6
  333.4 0.7 convert_element_type.47
  334.1 0.0 copy-done.3
  334.1 1.0 convert_element_type.46
  335.1 0.0 copy-start.2
  335.1 4.4 %convert.8 = f32[4,384,768]{2,1,0:T(8,128)} convert(bf16[4,384,768]{2,1,0:T(8,128)(2,1)} %bitcast.22) | non-fusion elementwise | flops 1179648 | bytes 7077888 | tf_op jit(solution)/shard_map/convert_element_type | solution.py:1564
  339.5 0.0 copy-done.2
  339.5 0.0 copy-start.5
  339.5 0.0 copy-start.4
  339.5 2.8 convert_element_type.48
  342.3 0.0 copy-done.5
  342.3 0.7 copy.73
  343.0 0.0 copy-done.4
  343.0 0.7 copy.74
Async XLA Ops:
  0.6 11.4 %copy-start = (bf16[4,384,768]{2,1,0:T(8,128)(2,1)S(1)}, bf16[4,384,768]{2,1,0:T(8,128)(2,1)}, u32[]{:S(2)}) copy-start(bf16[4,384,768]{2,1,0:T(8,128)(2,1)} %param.30) | copy-start | bytes 7077892
  328.0 3.9 %copy-start.1 = (f32[96,128]{1,0:T(8,128)S(1)}, f32[96,128]{1,0:T(8,128)}, u32[]{:S(2)}) copy-start(f32[96,128]{1,0:T(8,128)} %get-tuple-element.51) | copy-start | bytes 147460
  328.0 5.3 %copy-start.6 = (bf16[96,768]{1,0:T(8,128)(2,1)S(1)}, bf16[96,768]{1,0:T(8,128)(2,1)}, u32[]{:S(2)}) copy-start(bf16[96,768]{1,0:T(8,128)(2,1)} %get-tuple-element.53) | copy-start | bytes 442372
  328.1 6.0 %copy-start.3 = (bf16[96,2304]{1,0:T(8,128)(2,1)S(1)}, bf16[96,2304]{1,0:T(8,128)(2,1)}, u32[]{:S(2)}) copy-start(bf16[96,2304]{1,0:T(8,128)(2,1)} %get-tuple-element.52) | copy-start | bytes 1327108
  335.1 4.4 %copy-start.2 = (bf16[4,96,3072]{2,1,0:T(8,128)(2,1)S(1)}, bf16[4,96,3072]{2,1,0:T(8,128)(2,1)}, u32[]{:S(2)}) copy-start(bf16[4,96,3072]{2,1,0:T(8,128)(2,1)} %get-tuple-element.54) | copy-start | bytes 7077892
  339.5 2.8 copy-start.5
  339.5 3.5 %copy-start.4 = (bf16[200,768]{1,0:T(8,128)(2,1)S(1)}, bf16[200,768]{1,0:T(8,128)(2,1)}, u32[]{:S(2)}) copy-start(bf16[200,768]{1,0:T(8,128)(2,1)} %get-tuple-element.50) | copy-start | bytes 921604

commit v4 on v3

--- a/solution.py
+++ b/solution.py
@@ -388,25 +388,36 @@
     pl.semaphore_wait(barrier, len(partners))
 
 
+def nearest(place, i):
+    level = 0
+    for z in range(place.planes):
+        order = sorted(range(place.planes), key=lambda other: (abs(other - z), other))
+        for at in range(place.planes):
+            level = level + jnp.where((place.z == z) & (i == at), order[at], 0)
+    return level
+
+
 def expert_kernel(
     planes,
     own,
     rows,
+    real,
     packed_ref,
     inner_ref,
-    outer_ref,
-    bias_ref,
+    outer_all_ref,
+    bias_all_ref,
     small_ref,
     mix_ref,
     out_ref,
     inner_grad_ref,
     outer_grad_ref,
+    bias_grad_ref,
     router_grad_ref,
+    outer_ref,
     inner_t_ref,
     outer_t_ref,
     router_ref,
     router_t_ref,
-    bias_grad_ref,
     tokens,
     part,
     from_core,
@@ -417,6 +428,7 @@
     logit_grad,
     inner_acc,
     outer_acc,
+    outer_sem,
     z_send,
     z_recv,
     x_send,
@@ -432,48 +444,85 @@
 ):
     f32, bf16 = jnp.float32, jnp.bfloat16
     place = Place(planes)
+    y, c, z, x = place.y, place.c, place.z, place.x
     width = inner_ref.shape[0]
     lanes = inner_ref.shape[1] // own
+    first = real % 16
 
     def remote(src, dst, send, recv, device):
         return pltpu.make_async_remote_copy(
             src_ref=src, dst_ref=dst, send_sem=send, recv_sem=recv, device_id=device, device_id_type=MESH
         )
 
-    def slot(buffer, k, at, count=1):
-        return buffer.at[k, pl.ds(at * rows, count * rows)]
-
-    def z_copy(k):
-        return remote(slot(tokens, 0, 0), slot(tokens, k, 0), z_send.at[k], z_recv.at[k], place.level(k))
-
-    def x_copy(k):
-        return remote(slot(tokens, k, 0), slot(tokens, k, 1), x_send.at[k], x_recv.at[k], place.other_x())
-
-    def c_copy(k, r):
+    def slot(buffer, level, at, count=1):
+        return buffer.at[level, pl.ds(at * rows, count * rows)]
+
+    def up_copy(level):
+        here = slot(tokens, level, 0)
+        return remote(here, here, z_send.at[0, level], z_recv.at[0, level], place.at(y, c, z + 1, x))
+
+    def down_copy(level):
+        here = slot(tokens, level, 0)
+        return remote(here, here, z_send.at[1, level], z_recv.at[1, level], place.at(y, c, z - 1, x))
+
+    def x_copy(level):
         return remote(
-            slot(tokens, k, r), slot(tokens, k, 2 + r), c_send.at[k, r], c_recv.at[k, r], place.other_core()
+            slot(tokens, level, 0), slot(tokens, level, 1), x_send.at[level], x_recv.at[level], place.other_x()
         )
 
-    def sum_c_copy(k):
-        return remote(slot(part, k, 2, 2), from_core.at[k], sum_c_send.at[k], sum_c_recv.at[k], place.other_core())
-
-    def sum_x_copy(k):
-        return remote(slot(part, k, 1), from_x.at[k], sum_x_send.at[k], sum_x_recv.at[k], place.other_x())
-
-    def sum_z_copy(k):
-        return remote(slot(part, k, 0), from_z.at[k], sum_z_send.at[k], sum_z_recv.at[k], place.level(-k))
-
-    greet([place.other_core(), place.other_x()] + [place.level(k) for k in range(1, planes)])
-    tokens[0, 0:rows, :] = packed_ref[...]
-    c_copy(0, 0).start()
-    x_copy(0).start()
-    for k in range(1, planes):
-        z_copy(k).start()
+    def c_copy(level, r):
+        return remote(
+            slot(tokens, level, r),
+            slot(tokens, level, 2 + r),
+            c_send.at[level, r],
+            c_recv.at[level, r],
+            place.other_core(),
+        )
+
+    def sum_c_copy(level):
+        return remote(
+            slot(part, level, 2, 2),
+            from_core.at[level],
+            sum_c_send.at[level],
+            sum_c_recv.at[level],
+            place.other_core(),
+        )
+
+    def sum_x_copy(level):
+        return remote(
+            slot(part, level, 1), from_x.at[level], sum_x_send.at[level], sum_x_recv.at[level], place.other_x()
+        )
+
+    def sum_z_copy(level, source):
+        return remote(
+            slot(part, level, 0),
+            from_z.at[source],
+            sum_z_send.at[level],
+            sum_z_recv.at[source],
+            place.at(y, c, level, x),
+        )
+
+    partners = [place.other_core(), place.other_x()] + [place.level(k) for k in range(1, planes)]
+    greet(partners)
+    tokens[z, 0:rows, :] = packed_ref[...]
+
+    @pl.when(z < planes - 1)
+    def _():
+        up_copy(z).start()
+
+    @pl.when(z > 0)
+    def _():
+        down_copy(z).start()
+
+    c_copy(z, 0).start()
+    x_copy(z).start()
+    load = pltpu.make_async_copy(outer_all_ref.at[pl.ds(c * own, own)], outer_ref, outer_sem)
+    load.start()
     inner_t_ref[...] = jnp.transpose(inner_ref[...])
-    outer_t_ref[...] = jnp.transpose(outer_ref[...])
     place_row = lax.broadcasted_iota(jnp.int32, (128, 128), 0)
     place_lane = lax.broadcasted_iota(jnp.int32, (128, 128), 1)
-    take = (place_row == place_lane + 5) & (place_lane < 2 * own)
+    take = (place_row - (5 + 2 * own) == place_lane - first) & (place_lane >= first)
+    take = take & (place_lane < first + 2 * own)
     router = dot(small_ref[...], take.astype(bf16))
     router_ref[...] = router.astype(bf16)
     router_t_ref[...] = jnp.transpose(router).astype(bf16)
@@ -481,23 +530,52 @@
     outer_acc[...] = jnp.zeros_like(outer_acc)
     bias_grad_ref[...] = jnp.zeros_like(bias_grad_ref)
     router_grad_ref[...] = jnp.zeros_like(router_grad_ref)
-
-    def tile(k, t):
+    load.wait()
+    for i in range(own):
+        outer_t_ref[:, i * lanes : (i + 1) * lanes] = jnp.transpose(outer_ref[i])
+
+    def hop(h):
+        @pl.when(z >= h)
+        def _():
+            up_copy(z - h).wait_recv()
+
+            @pl.when(z < planes - 1)
+            def _():
+                up_copy(z - h).start()
+
+            c_copy(z - h, 0).start()
+
+        @pl.when(z + h < planes)
+        def _():
+            down_copy(z + h).wait_recv()
+
+            @pl.when(z > 0)
+            def _():
+                down_copy(z + h).start()
+
+            c_copy(z + h, 0).start()
+
+    def tile(level, t):
         here = pl.ds(pl.multiple_of(t * rows, 16), rows)
-        normed, grad_out = tokens[k, here, :width], tokens[k, here, width : 2 * width]
-        select = tokens[k, here, 2 * width :].astype(f32)
+        normed, grad_out = tokens[level, here, :width], tokens[level, here, width:]
+        last = pl.ds(pl.multiple_of(t * rows + real - first, 16), 16)
+        chosen = tokens[level, last, width : width + 256].astype(f32)
+        chosen = jnp.concatenate([chosen, jnp.zeros((112, 256), f32)], axis=0)
+        select = jnp.transpose(chosen)[:rows]
         lane = lax.broadcasted_iota(jnp.int32, select.shape, 1)
-        logits = dot(normed, router_ref[...])
-        logits = jnp.where(lane < 2 * own, logits, -1e30)
+        named = (lane >= first) & (lane < first + 2 * own)
+        select = jnp.where(named, select, 0.0)
+        logits = jnp.where(named, dot(normed, router_ref[...]), -1e30)
         routing = jnp.exp(logits - jnp.max(logits, axis=1, keepdims=True))
         routing = routing / jnp.sum(routing, axis=1, keepdims=True)
         gates = routing * select
         gate_grads = jnp.zeros_like(gates)
         for i in range(own):
-            mine = lane == place.c * own + i
+            mine = lane == first + c * own + i
             units = slice(i * lanes, (i + 1) * lanes)
             gate = jnp.sum(jnp.where(mine, gates, 0.0), axis=1, keepdims=True)
-            pre = dot(normed, inner_ref[:, units]) + bias_ref[:, units]
+            bias = jnp.where(c == 0, bias_all_ref[i : i + 1, :], bias_all_ref[own + i : own + i + 1, :])
+            pre = dot(normed, inner_ref[:, units]) + bias.astype(f32)
             grad_act = dot(grad_out, outer_t_ref[:, units])
             cdf = 0.5 * (1.0 + lax.erf(pre * (0.5**0.5)))
             act = pre * cdf
@@ -506,122 +584,151 @@
             gate_grads = gate_grads + jnp.where(mine, gate_grad * select, 0.0)
             slope = cdf + pre * jnp.exp(-0.5 * pre * pre) * 0.3989422804014327
             grad_pre = gate * grad_act * slope
-            bias_grad_ref[:, units] += jnp.sum(grad_pre, axis=0, keepdims=True)
+            bias_grad_ref[0:1, units] += jnp.sum(grad_pre, axis=0, keepdims=True)
             hidden_grad[here, units] = grad_pre.astype(bf16)
         grad_logits = routing * (gate_grads - jnp.sum(routing * gate_grads, axis=1, keepdims=True))
         logit_grad[here, :] = grad_logits.astype(bf16)
-        mix_ref[k, here, :] = dot(hidden[here, :], outer_ref[...]).astype(bf16)
+        mixed = jnp.zeros((rows, width), f32)
+        for i in range(own):
+            mixed = mixed + dot(hidden[here, i * lanes : (i + 1) * lanes], outer_ref[i])
+        mix_ref[level, here, :] = mixed.astype(bf16)
         row_grad = dot(hidden_grad[here, :], inner_t_ref[...])
         row_grad = row_grad + dot(logit_grad[here, :], router_t_ref[...])
-        part[k, here, :] = row_grad.astype(bf16)
-
-    def add_core(k):
-        sum_c_copy(k).wait_recv()
-        total = slot(part, k, 1)[...].astype(f32) + from_core[k, rows : 2 * rows, :].astype(f32)
-        part[k, rows : 2 * rows, :] = total.astype(bf16)
-        sum_x_copy(k).start()
-
-    def add_x(k):
-        sum_x_copy(k).wait_recv()
-        total = part[k, 0:rows, :].astype(f32) + from_core[k, 0:rows, :].astype(f32)
-        total = total + from_x[k].astype(f32)
-        part[k, 0:rows, :] = total.astype(bf16)
-
-        @pl.when(k > 0)
+        part[level, here, :] = row_grad.astype(bf16)
+
+    def tiles(level, start):
+        def one(t, carry):
+            tile(level, 2 * t + start)
+            return carry
+
+        lax.fori_loop(0, 2, one, 0)
+
+    def add_core(level):
+        sum_c_copy(level).wait_recv()
+        total = part[level, rows : 2 * rows, :].astype(f32) + from_core[level, rows : 2 * rows, :].astype(f32)
+        part[level, rows : 2 * rows, :] = total.astype(bf16)
+        sum_x_copy(level).start()
+
+    def add_x(level):
+        sum_x_copy(level).wait_recv()
+        total = part[level, 0:rows, :].astype(f32) + from_core[level, 0:rows, :].astype(f32)
+        total = total + from_x[level].astype(f32)
+        part[level, 0:rows, :] = total.astype(bf16)
+
+        @pl.when(level != z)
         def _():
-            sum_z_copy(k).start()
-
-    def step(k, carry):
-        x_copy(k).wait_recv()
-        c_copy(k, 1).start()
-
-        @pl.when(k + 1 < planes)
+            sum_z_copy(level, z).start()
+
+    def step(i, carry):
+        level, later, before = nearest(place, i), nearest(place, i + 1), nearest(place, i - 1)
+
+        @pl.when(i > 0)
         def _():
-            z_copy(k + 1).wait_recv()
-            c_copy(k + 1, 0).start()
-            x_copy(k + 1).start()
-
-        c_copy(k, 0).wait_recv()
-        c_copy(k, 1).wait_recv()
-
-        def one(t, carry):
-            tile(k, t)
-            return carry
-
-        lax.fori_loop(0, 4, one, 0)
-        sum_c_copy(k).start()
-
-        @pl.when(k > 0)
+            c_copy(level, 0).wait_recv()
+
+        @pl.when(i == 0)
         def _():
-            add_core(k - 1)
-
-        @pl.when(k > 1)
+            c_copy(z, 0).wait_recv()
+
+        tiles(level, 0)
+
+        @pl.when(i + 1 < planes)
         def _():
-            add_x(k - 2)
+            hop(i + 1)
+
+        x_copy(level).wait_recv()
+        c_copy(level, 1).start()
+
+        @pl.when(i + 1 < planes)
+        def _():
+            x_copy(later).start()
+
+        c_copy(level, 1).wait_recv()
+        tiles(level, 1)
+        sum_c_copy(level).start()
+
+        @pl.when(i > 0)
+        def _():
+            add_x(before)
+
+        add_core(level)
 
         def columns(j, carry):
             some = pl.ds(pl.multiple_of(j * 256, 256), 256)
             outer_acc[:, some] += lax.dot_general(
-                hidden[...], tokens[k, :, pl.ds(pl.multiple_of(width + j * 256, 256), 256)], TN, preferred_element_type=f32
+                hidden[...],
+                tokens[level, :, pl.ds(pl.multiple_of(width + j * 256, 256), 256)],
+                TN,
+                preferred_element_type=f32,
             )
             inner_acc[:, some] += lax.dot_general(
-                tokens[k, :, :width], hidden_grad[:, some], TN, preferred_element_type=f32
+                tokens[level, :, :width], hidden_grad[:, some], TN, preferred_element_type=f32
             )
             return carry
 
         lax.fori_loop(0, width // 256, columns, 0)
-        router_grad_ref[...] += lax.dot_general(tokens[k, :, :width], logit_grad[...], TN, preferred_element_type=f32)
+        router_grad_ref[...] += lax.dot_general(
+            tokens[level, :, :width], logit_grad[...], TN, preferred_element_type=f32
+        )
         return carry
 
     lax.fori_loop(0, planes, step, 0)
-    add_core(planes - 1)
-    add_x(planes - 2)
-    add_x(planes - 1)
     inner_grad_ref[...] = inner_acc[...].astype(bf16)
-    units = outer_acc.shape[0]
-    outer_grad_ref[0:units, :] = outer_acc[...].astype(bf16)
-    outer_grad_ref[units : units + 16, :] = jnp.broadcast_to(bias_grad_ref[...], (16, width)).astype(bf16)
-    total = part[0, 0:rows, :].astype(f32)
+    outer_grad_ref[...] = outer_acc[...].astype(bf16)
+    add_x(nearest(place, planes - 1))
+    total = part[z, 0:rows, :].astype(f32)
     for k in range(1, planes):
-        sum_z_copy(k).wait_recv()
-        total = total + from_z[k].astype(f32)
+        source = lax.rem(z + k, planes)
+        sum_z_copy(z, source).wait_recv()
+        total = total + from_z[source].astype(f32)
     out_ref[...] = total
-    for k in range(planes):
-        x_copy(k).wait_send()
-        c_copy(k, 0).wait_send()
-        c_copy(k, 1).wait_send()
-        sum_c_copy(k).wait_send()
-        sum_x_copy(k).wait_send()
-        if k > 0:
-            z_copy(k).wait_send()
-            sum_z_copy(k).wait_send()
-
-
-def experts_of_the_plane(planes, own, packed, inner, outer, bias, small):
+    for level in range(planes):
+        x_copy(level).wait_send()
+        c_copy(level, 0).wait_send()
+        c_copy(level, 1).wait_send()
+        sum_c_copy(level).wait_send()
+        sum_x_copy(level).wait_send()
+
+        @pl.when(level != z)
+        def _():
+            sum_z_copy(level, z).wait_send()
+
+        @pl.when((z >= level) & (z < planes - 1))
+        def _():
+            up_copy(level).wait_send()
+
+        @pl.when((z <= level) & (z > 0))
+        def _():
+            down_copy(level).wait_send()
+
+
+def experts_of_the_plane(planes, own, real, packed, inner, outer, bias, small):
     f32, bf16 = jnp.float32, jnp.bfloat16
     rows, wide = packed.shape
     chunk = 4 * rows
     width, units = inner.shape
+    shape = jax.ShapeDtypeStruct
     vmem = pl.BlockSpec(memory_space=pltpu.VMEM)
     dma = pltpu.SemaphoreType.DMA
     flops = 12 * planes * chunk * width * units
     return pl.pallas_call(
-        functools.partial(expert_kernel, planes, own, rows),
+        functools.partial(expert_kernel, planes, own, rows, real),
         out_shape=[
-            jax.ShapeDtypeStruct((planes, chunk, width), bf16),
-            jax.ShapeDtypeStruct((rows, width), f32),
-            jax.ShapeDtypeStruct((width, units), bf16),
-            jax.ShapeDtypeStruct((units + 16, width), bf16),
-            jax.ShapeDtypeStruct((width, 128), f32),
+            shape((planes, chunk, width), bf16),
+            shape((rows, width), f32),
+            shape((width, units), bf16),
+            shape((units, width), bf16),
+            shape((8, units), f32),
+            shape((width, 128), f32),
         ],
-        in_specs=[vmem] * 5,
-        out_specs=[vmem] * 5,
+        in_specs=[vmem] * 2 + [pl.BlockSpec(memory_space=pl.ANY)] + [vmem] * 2,
+        out_specs=[vmem] * 6,
         scratch_shapes=[
+            pltpu.VMEM((own, units // own, width), bf16),
             pltpu.VMEM((units, width), bf16),
             pltpu.VMEM((width, units), bf16),
             pltpu.VMEM((width, 128), bf16),
             pltpu.VMEM((128, width), bf16),
-            pltpu.VMEM((1, units), f32),
             pltpu.VMEM((planes, chunk, wide), bf16),
             pltpu.VMEM((planes, chunk, width), bf16),
             pltpu.VMEM((planes, 2 * rows, width), bf16),
@@ -632,8 +739,10 @@
             pltpu.VMEM((chunk, 128), bf16),
             pltpu.VMEM((width, units), f32),
             pltpu.VMEM((units, width), f32),
+            dma,
         ]
-        + [dma((planes,))] * 4
+        + [dma((2, planes))] * 2
+        + [dma((planes,))] * 2
         + [dma((planes, 2))] * 2
         + [dma((planes,))] * 6,
         compiler_params=pltpu.CompilerParams(
@@ -649,12 +758,16 @@
     heads,
     real,
     tokens_ref,
-    keys_ref,
-    keep_ref,
+    mask_ref,
+    ids_ref,
     cotangent_ref,
-    select_ref,
-    small_ref,
-    qkv_part_ref,
+    *refs,
+):
+    vector_refs, refs = refs[:5], refs[5:]
+    (
+        router_part_ref,
+        outer_bias_ref,
+        qkv_part_ref,
     proj_part_ref,
     inner_part_ref,
     small_all,
@@ -666,6 +779,10 @@
     attended_ref,
     middle_ref,
     packed_ref,
+    wide_ref,
+    select_ref,
+    keys_ref,
+    keep_ref,
     up_send,
     up_recv,
     down_send,
@@ -679,11 +796,12 @@
     own_sem,
     y_send,
     y_recv,
-):
+    ) = refs
     f32, bf16 = jnp.float32, jnp.bfloat16
     place = Place(planes)
-    rows, width = tokens_ref.shape
-    depth = small_ref.shape[0]
+    rows, width = wide_ref.shape
+    depth = qkv_part_ref.shape[0]
+    experts = inner_part_ref.shape[0]
     half = depth // 2
     lanes = inner_part_ref.shape[2] // (2 * planes)
     head_dim = width // heads
@@ -750,9 +868,7 @@
     partners += [place.at(y, c, lax.rem(z + k, planes), (x + r) % 2) for k, r in others]
     greet(partners)
 
-    small_all[here_rows, :] = small_ref[...]
     w_qkv_all[here_rows, :] = qkv_part_ref[...]
-    w_proj_all[here_rows, :] = proj_part_ref[...]
 
     def forward(level, flows):
         for j in flows:
@@ -817,10 +933,38 @@
                 for j in flows:
                     sibling_piece(j, level, x).wait_recv()
 
-    line([0, 1])
+    line([1])
+    lined = [ref[...].astype(f32) for ref in vector_refs] + [outer_bias_ref[...].astype(f32)]
+    lined = jnp.concatenate(lined, axis=0)
+    lined = jnp.concatenate([lined, jnp.zeros((128 - lined.shape[0], depth), f32)], axis=0)
+    lined = jnp.concatenate([lined, jnp.zeros((128, 128 - depth), f32)], axis=1)
+    routed = jnp.concatenate([router_part_ref[...].astype(f32), jnp.zeros((depth, 128 - experts), f32)], axis=1)
+    small = jnp.transpose(lined)[:depth] + pltpu.roll(routed, 5 + experts, 1)
+    small_all[here_rows, :] = small.astype(bf16)
+    line([0])
+    w_proj_all[here_rows, :] = proj_part_ref[...]
     line([2])
-    values = tokens_ref[...].astype(f32)
+    spare = jnp.zeros((rows - real, width), f32)
+    values = jnp.concatenate([tokens_ref[...].astype(f32), spare], axis=0)
+    wide_ref[...] = values.astype(bf16)
     normal, _ = norm_parts(values)
+    mask = mask_ref[pl.ds(y * 2 + c, 1), :].astype(f32)
+    keys = jnp.concatenate([mask, jnp.zeros((1, rows - real), f32)], axis=1)
+    keys_ref[...] = keys
+    keep = lax.broadcasted_iota(jnp.int32, (rows, rows), 0) == lax.broadcasted_iota(jnp.int32, (rows, rows), 1)
+    keep = jnp.sum(jnp.where(keep, keys, 0.0), axis=1, keepdims=True)
+    keep_ref[...] = keep
+    ids = ids_ref[...]
+    number = lax.broadcasted_iota(jnp.int32, (real, 128), 1)
+    select = ((number == ids[:, 0:1]) | (number == ids[:, 1:2])).astype(f32)
+    select = jnp.concatenate([select, jnp.zeros((rows - real, 128), f32)], axis=0)
+    select_ref[...] = select.astype(bf16)
+    chosen = jnp.transpose(jnp.concatenate([select, jnp.zeros((256 - rows, 128), f32)], axis=0))[:8]
+    chosen = jnp.concatenate([chosen, jnp.zeros((8, width - 256), f32)], axis=1)
+    if rows - real > 8:
+        chosen = jnp.concatenate([chosen, jnp.zeros((rows - real - 8, width), f32)], axis=0)
+    grad_out = cotangent_ref[...].astype(f32) * keep[:real]
+    packed_ref[:, width:] = jnp.concatenate([grad_out, chosen], axis=0).astype(bf16)
     hops([0, 1])
     hops([2])
     own_copy.start()
@@ -864,8 +1008,6 @@
     normed = normal_mid * vectors[3:4] + vectors[4:5]
     row = lax.broadcasted_iota(jnp.int32, normed.shape, 0)
     packed_ref[:, :width] = jnp.where(row < real, normed, 0.0).astype(bf16)
-    packed_ref[:, width : 2 * width] = (cotangent_ref[...].astype(f32) * keep_ref[...]).astype(bf16)
-    packed_ref[:, 2 * width :] = select_ref[...]
     from_y.wait_recv()
     y_copy.wait_send()
     for k, r in others:
@@ -888,9 +1030,9 @@
                 down_copy(j, level).wait_send()
 
 
-def front(planes, real, tokens, keys, keep, cotangent, select, small, w_qkv, w_proj, w_in):
+def front(planes, rows, tokens, mask, ids, cotangent, vectors, router, outer_bias, w_qkv, w_proj, w_in):
     f32, bf16 = jnp.float32, jnp.bfloat16
-    rows, width = tokens.shape
+    real, width = tokens.shape
     lanes = w_in.shape[2] // (2 * planes)
     shape = jax.ShapeDtypeStruct
     vmem = pl.BlockSpec(memory_space=pltpu.VMEM)
@@ -898,7 +1040,7 @@
     return pl.pallas_call(
         functools.partial(front_kernel, planes, HEADS, real),
         out_shape=[
-            shape((width, small.shape[1]), bf16),
+            shape((width, 128), bf16),
             shape((width, 3 * width), bf16),
             shape((width, width), bf16),
             shape((width, 2 * lanes), bf16),
@@ -906,10 +1048,14 @@
             shape((rows, 3 * width), bf16),
             shape((rows, width), bf16),
             shape((rows, width), f32),
-            shape((rows, 2 * width + 128), bf16),
+            shape((rows, 2 * width), bf16),
+            shape((rows, width), bf16),
+            shape((rows, 128), bf16),
+            shape((1, rows), f32),
+            shape((rows, 1), f32),
         ],
-        in_specs=[vmem] * 8 + [pl.BlockSpec(memory_space=pl.ANY)],
-        out_specs=[vmem] * 9,
+        in_specs=[vmem] * (6 + len(vectors)) + [vmem] * 2 + [pl.BlockSpec(memory_space=pl.ANY)],
+        out_specs=[vmem] * 13,
         scratch_shapes=[dma((3, planes))] * 6
         + [dma((3, 2 * planes))] * 2
         + [dma((planes, 2))] * 2
@@ -919,7 +1065,7 @@
         ),
         cost_estimate=pl.CostEstimate(flops=2**32, bytes_accessed=40 * 2**20, transcendentals=0),
         name="dense_weights_and_attention",
-    )(tokens, keys, keep, cotangent, select, small, w_qkv, w_proj, w_in)
+    )(tokens, mask, ids, cotangent, *vectors, router, outer_bias, w_qkv, w_proj, w_in)
 
 
 def back_kernel(planes, heads, own, groups, real, *refs):
@@ -936,12 +1082,15 @@
         w_proj_ref,
         keys_ref,
         keep_ref,
+        select_ref,
         mix_ref,
         inner_ref,
         outer_ref,
+        bias_ref,
         router_grad_ref,
-    ) = refs[:16]
-    mixed_ref, token_grad_ref, qkv_out, proj_out, small_out, inner_out, outer_out = refs[16:23]
+    ) = refs[:18]
+    mixed_ref, token_grad_ref, qkv_out, proj_out, small_out, inner_out, outer_out, bias_out = refs[18:26]
+    refs = refs[26:]
     (
         grad_attended,
         grad_qkv,
@@ -953,6 +1102,7 @@
         inner_from_y,
         inner_sum,
         outer_from_y,
+        bias_from_y,
         held,
         held_small,
         from_core,
@@ -967,10 +1117,11 @@
         from_y_small,
         final,
         final_small,
-    ) = refs[23:47]
+    ) = refs[:25]
     (
         mix_c_sem,
-        mix_x_sem,
+        mix_x_send,
+        mix_x_recv,
         mix_z_send,
         mix_z_recv,
         inner_y_sem,
@@ -980,6 +1131,8 @@
         inner_core_sem,
         outer_y_sem,
         outer_c_sem,
+        bias_y_sem,
+        bias_c_sem,
         own_sem,
         flow_c_sem,
         flow_x_sem,
@@ -987,7 +1140,7 @@
         flow_z_recv,
         flow_y_sem,
         flow_end_sem,
-    ) = refs[47:]
+    ) = refs[25:]
     f32, bf16 = jnp.float32, jnp.bfloat16
     place = Place(planes)
     y, c, z, x = place.y, place.c, place.z, place.x
@@ -1079,28 +1232,31 @@
     def mix_c():
         return swap(mix_ref.at[:, pl.ds(2 * rows, 2 * rows)], mix_from_core, mix_c_sem, place.other_core())
 
-    def mix_to_x():
-        return swap(mix_x, mix_from_x, mix_x_sem, place.other_x())
-
-    def mix_to_z(k):
-        return remote(mix_z.at[k], mix_from_z.at[k], mix_z_send.at[k], mix_z_recv.at[k], place.level(-k))
+    def mix_to_x(level):
+        return remote(mix_x.at[level], mix_from_x.at[level], mix_x_send.at[level], mix_x_recv.at[level], place.other_x())
+
+    def mix_to_z(level, source):
+        return remote(
+            mix_z.at[level], mix_from_z.at[source], mix_z_send.at[level], mix_z_recv.at[source], place.at(y, c, level, x)
+        )
 
     def mix_core_sum():
         mix_c().wait_recv()
-        for k in range(planes):
-            total = mix_ref[k, rows : 2 * rows, :].astype(f32) + mix_from_core[k, rows:, :].astype(f32)
-            mix_x[k] = total.astype(bf16)
-        mix_to_x().start()
-        for k in range(planes):
-            total = mix_ref[k, :rows, :].astype(f32) + mix_from_core[k, :rows, :].astype(f32)
-            mix_z[k] = total.astype(bf16)
-
-    def mix_x_sum():
-        mix_to_x().wait_recv()
-        for k in range(planes):
-            mix_z[k] = (mix_z[k].astype(f32) + mix_from_x[k].astype(f32)).astype(bf16)
-            if k:
-                mix_to_z(k).start()
+        for k in range(1, planes + 1):
+            level = lax.rem(z + k, planes)
+            total = mix_ref[level, rows : 2 * rows, :].astype(f32) + mix_from_core[level, rows:, :].astype(f32)
+            mix_x[level] = total.astype(bf16)
+            mix_to_x(level).start()
+        for level in range(planes):
+            total = mix_ref[level, :rows, :].astype(f32) + mix_from_core[level, :rows, :].astype(f32)
+            mix_z[level] = total.astype(bf16)
+
+    def mix_x_sum(k):
+        level = lax.rem(z + k, planes)
+        mix_to_x(level).wait_recv()
+        mix_z[level] = (mix_z[level].astype(f32) + mix_from_x[level].astype(f32)).astype(bf16)
+        if k < planes:
+            mix_to_z(level, z).start()
 
     my_units = pl.ds(pl.multiple_of(y * lanes, 128), lanes)
     their_units = pl.ds(pl.multiple_of((1 - y) * lanes, 128), lanes)
@@ -1142,6 +1298,13 @@
         here = outer_out.at[c]
         return swap(here, here, outer_c_sem, place.other_core())
 
+    def bias_y():
+        return swap(bias_ref, bias_from_y, bias_y_sem, place.other_y())
+
+    def bias_c():
+        here = bias_out.at[c]
+        return swap(here, here, bias_c_sem, place.other_core())
+
     others = [(k, r) for k in range(planes) for r in range(2) if k or r]
 
     def inner_y_sum():
@@ -1165,11 +1328,15 @@
         total = outer_ref[...].astype(f32) + outer_from_y[...].astype(f32)
         outer_out[c] = total.astype(bf16)
         outer_c().start()
+        bias_y().wait_recv()
+        bias_out[c] = bias_ref[...] + bias_from_y[...]
+        bias_c().start()
 
     partners = [place.other_core(), place.other_y()]
     partners += [place.at(y, c, lax.rem(z + k, planes), (x + r) % 2) for k, r in others]
     greet(partners)
     inner_y().start()
+    bias_y().start()
     mix_c().start()
 
     vectors = jnp.transpose(small_ref[...].astype(f32))
@@ -1181,9 +1348,11 @@
         take = (place_row == place_lane + first) & (place_lane < 2 * own)
         return dot(small_ref[...], take.astype(bf16)).astype(bf16)
 
-    router, outer_bias = lanes_from(5), lanes_from(5 + 2 * own)
-    normed_mid, grad_out = packed_ref[:, :width], packed_ref[:, width : 2 * width]
-    select = packed_ref[:, 2 * width :].astype(f32)
+    outer_bias, router = lanes_from(5), lanes_from(5 + 2 * own)
+    normed_mid, grad_out = packed_ref[:, :width], packed_ref[:, width:]
+    real_row = lax.broadcasted_iota(jnp.int32, grad_out.shape, 0) < real
+    grad_out = jnp.where(real_row, grad_out, 0).astype(bf16)
+    select = select_ref[...].astype(f32)
     lane = lax.broadcasted_iota(jnp.int32, select.shape, 1)
     logits = jnp.where(lane < 2 * own, dot(normed_mid, router), -1e30)
     routing = jnp.exp(logits - jnp.max(logits, axis=1, keepdims=True))
@@ -1192,9 +1361,8 @@
     bias_gate = select * dot(grad_out, outer_bias)
     bias_logits = routing * (bias_gate - jnp.sum(routing * bias_gate, axis=1, keepdims=True))
     bias_logits = bias_logits.astype(bf16)
-    router_grad = router_grad_ref[...] + lax.dot_general(
-        normed_mid, bias_logits, TN, preferred_element_type=f32
-    )
+    router_grad = lax.dot_general(normed_mid, bias_logits, TN, preferred_element_type=f32)
+    router_grad = pltpu.roll(router_grad, 16, 1) + pltpu.roll(router_grad_ref[...], 16 - real % 16, 1)
     outer_bias_grad = lax.dot_general(gates.astype(bf16), grad_out, TN, preferred_element_type=f32)
     grad_normed_mid = row_grad_ref[...] + lax.dot_general(bias_logits, router, NT, preferred_element_type=f32)
     normal_mid, rstd_mid = norm_parts(middle_ref[...])
@@ -1263,13 +1431,12 @@
     group_back(0)
     inner_y_sum()
     flow_core_sum(1)
+    mix_x_sum(1)
     for group in range(1, groups):
         group_back(group)
+        flow_core_sum(1 + group)
         if group == 1:
-            mix_x_sum()
-            flow_x_sum(0)
-        flow_core_sum(1 + group)
-    flow_x_sum(1)
+            mix_x_sum(2)
 
     grad_normed_in = jnp.zeros((rows, width), f32)
     for group in range(groups):
@@ -1298,20 +1465,26 @@
         ],
         axis=0,
     )
-    vector_grads = jnp.transpose(vector_rows) + pltpu.roll(router_grad, 16, 1)
+    vector_grads = jnp.transpose(vector_rows) + router_grad
     held_small[...] = vector_grads.astype(bf16).reshape(planes, 2, depth, 128)
     flow_c(small_at).start()
+    flow_core_sum(small_at)
+    for k in range(3, planes):
+        mix_x_sum(k)
     inner_spread_done()
-    flow_core_sum(small_at)
+    flow_x_sum(0)
+    flow_x_sum(1)
+    mix_x_sum(planes)
     outer_y_sum()
     for group in range(1, groups):
         flow_x_sum(1 + group)
     flow_z_sum(0)
     flow_x_sum(small_at)
-    mixture = mix_z[0].astype(f32) + dot(gates.astype(bf16), jnp.transpose(outer_bias.astype(f32)).astype(bf16))
+    mixture = mix_z[z].astype(f32) + dot(gates.astype(bf16), jnp.transpose(outer_bias.astype(f32)).astype(bf16))
     for k in range(1, planes):
-        mix_to_z(k).wait_recv()
-        mixture = mixture + mix_from_z[k].astype(f32)
+        source = lax.rem(z + k, planes)
+        mix_to_z(z, source).wait_recv()
+        mixture = mixture + mix_from_z[source].astype(f32)
     mixed = (keep_ref[...] * (middle_ref[...] + mixture)).astype(bf16)
     mixed_ref[...] = mixed[:real]
     flow_y_sum(0)
@@ -1341,21 +1514,27 @@
     small_out[...] = final_small[...].astype(f32)
     outer_theirs = outer_out.at[1 - c]
     swap(outer_theirs, outer_theirs, outer_c_sem, place.other_core()).wait_recv()
+    bias_theirs = bias_out.at[1 - c]
+    swap(bias_theirs, bias_theirs, bias_c_sem, place.other_core()).wait_recv()
     for at, expert in enumerate(((1 - c) * 2 + y, (1 - c) * 2 + 1 - y)):
         inner_core(expert, at).wait_recv()
 
     mix_c().wait_send()
-    mix_to_x().wait_send()
     inner_y().wait_send()
     inner_back().wait_send()
     inner_core(my_expert, 0).wait_send()
     inner_core(their_expert, 1).wait_send()
     outer_y().wait_send()
     outer_c().wait_send()
+    bias_y().wait_send()
+    bias_c().wait_send()
     for k, r in others:
         spread(k, r).wait_send()
-    for k in range(1, planes):
-        mix_to_z(k).wait_send()
+    for k in range(1, planes + 1):
+        level = lax.rem(z + k, planes)
+        mix_to_x(level).wait_send()
+        if k < planes:
+            mix_to_z(level, z).wait_send()
     for j in range(groups + 2):
         flow_c(j).wait_send()
         flow_x(j).wait_send()
@@ -1380,9 +1559,11 @@
         w_proj,
         keys,
         keep,
+        select,
         mix_parts,
         inner_grad,
         outer_grad,
+        bias_grad,
         router_grad,
     ) = args
     rows, width = middle.shape
@@ -1410,9 +1591,10 @@
             shape((depth, 128), f32),
             shape((2 * own, depth, 2 * planes * lanes), bf16),
             shape((2, tall, width), bf16),
+            shape((2, *bias_grad.shape), f32),
         ],
-        in_specs=[vmem] * 16,
-        out_specs=[vmem] * 7,
+        in_specs=[vmem] * 18,
+        out_specs=[vmem] * 8,
         scratch_shapes=[
             pltpu.VMEM((rows, width), bf16),
             pltpu.VMEM((groups, rows, 3 * width // groups), bf16),
@@ -1424,6 +1606,7 @@
             pltpu.VMEM((width, lanes), bf16),
             pltpu.VMEM((width, lanes), bf16),
             pltpu.VMEM((tall, width), bf16),
+            pltpu.VMEM(bias_grad.shape, f32),
         ]
         + both(planes, 2, depth)
         + both(planes, 2, half)
@@ -1432,11 +1615,11 @@
         + both(half)
         + both(half)
         + both(depth)
-        + [dma((2,))] * 2
-        + [dma((planes,))] * 2
+        + [dma((2,))]
+        + [dma((planes,))] * 4
         + [dma((2,))]
         + [dma((planes, 2))] * 2
-        + [dma((2,)), dma((2, 2)), dma((2,)), dma((2,)), dma]
+        + [dma((2,)), dma((2, 2)), dma((2,)), dma((2,)), dma((2,)), dma((2,)), dma]
         + [dma((flows + 1, 2))] * 2
         + [dma((flows + 1, planes))] * 2
         + [dma((flows + 1, 2))] * 2,
@@ -1481,59 +1664,39 @@
     w_out,
     b_out,
 ):
-    f32, bf16 = jnp.float32, jnp.bfloat16
+    f32 = jnp.float32
     _, rows, width = tokens.shape
     experts, depth, hidden = w_in.shape
     slice_width = w_out.shape[1]
     planes = hidden // slice_width // 2
     own = experts // 2
-    s = lax.axis_index("seq")
-    core = s % 2
-    small = jnp.concatenate(
-        [
-            jnp.stack([norm1_gain, norm1_bias, proj_bias, norm2_gain, norm2_bias], axis=1),
-            w_router,
-            b_out.T,
-        ],
-        axis=1,
-    )
-    small = jnp.pad(small, ((0, 0), (0, 128 - small.shape[1])))
-    own_mask = lax.dynamic_slice_in_dim(key_mask, s, 1, 0).astype(f32)
-    selected = jnp.sum(
-        (expert_ids[0][:, :, None] == jnp.arange(experts, dtype=jnp.int32)).astype(f32), axis=1
-    )
-    padded = (rows + 15) // 16 * 16
-    extra = ((0, padded - rows), (0, 0))
-    wide_tokens = jnp.pad(tokens[0], extra)
-    keys = jnp.pad(own_mask, ((0, 0), (0, padded - rows)))
-    keep = keys.reshape(padded, 1)
-    small, full_qkv, full_proj, inner, normed_in, qkv, attended, middle, packed = front(
+    padded = (rows + experts + 15) // 16 * 16
+    vectors = [v[None] for v in (norm1_gain, norm1_bias, proj_bias, norm2_gain, norm2_bias)]
+    small, full_qkv, full_proj, inner, normed_in, qkv, attended, middle, packed, wide, select, keys, keep = front(
         planes,
-        rows,
-        wide_tokens,
-        keys,
-        keep,
-        jnp.pad(cotangent[0], extra),
-        jnp.pad(selected, ((0, padded - rows), (0, 128 - experts))).astype(bf16),
-        small,
+        padded,
+        tokens[0],
+        key_mask,
+        expert_ids[0],
+        cotangent[0],
+        vectors,
+        w_router,
+        b_out,
         w_qkv,
         w_proj,
         w_in,
     )
-    outer = lax.dynamic_slice_in_dim(w_out, core * own, own, 0).reshape(own * slice_width, width)
-    inner_bias = lax.dynamic_slice_in_dim(b_in, core * own, own, 0)
-    inner_bias = inner_bias.reshape(1, own * slice_width).astype(f32)
-    mix_parts, row_grad, inner_grad, outer_grad, router_grad = experts_of_the_plane(
-        planes, own, packed, inner, outer, inner_bias, small
-    )
-    mixed, token_grad, qkv_grad, proj_grad, vector_grads, inner_grad, outer_grad = back(
+    mix_parts, row_grad, inner_grad, outer_grad, bias_grad, router_grad = experts_of_the_plane(
+        planes, own, rows, packed, inner, w_out, b_in, small
+    )
+    mixed, token_grad, qkv_grad, proj_grad, vector_grads, inner_grad, outer_grad, bias_grad = back(
         planes,
         own,
         rows,
         row_grad,
         packed,
         middle,
-        wide_tokens,
+        wide,
         normed_in,
         qkv,
         attended,
@@ -1542,12 +1705,13 @@
         full_proj,
         keys,
         keep,
+        select,
         mix_parts,
         inner_grad,
         outer_grad,
+        bias_grad,
         router_grad,
     )
-    units = own * slice_width
     return (
         mixed[None],
         token_grad[None],
@@ -1560,8 +1724,8 @@
         vector_grads[:, 4],
         vector_grads[:, 16 : 16 + experts],
         inner_grad.astype(f32),
-        outer_grad[:, units, :units].reshape(experts, slice_width).astype(f32),
-        outer_grad[:, :units].reshape(experts, slice_width, width).astype(f32),
+        bias_grad[:, 0].reshape(experts, slice_width),
+        outer_grad.reshape(experts, slice_width, width).astype(f32),
         vector_grads[:, 8 : 8 + experts].T,
     )
 

time: 344 us -> 295 us (0.86)
  Pallas kernels: 312 us -> 275 us
  local copies, waits for them, and re-layouts: 18.8 us -> 9.85 us
    pallas_call x1, Pallas kernels: 142 us -> 109 us  [experts_of_the_plane(): pl.pallas_call(functools.partial(expert_kernel, planes, own, rows, real),...]
    pad x4 -> x0, local copies, waits for them, and re-layouts: 4.68 us -> none  [the longest x1 1.71 us: move_tokens_plan(): wide_tokens = jnp.pad(tokens[0], extra)]
    pallas_call x1, Pallas kernels: 107 us -> 103 us  [back(): pl.pallas_call(functools.partial(back_kernel, planes, HEADS, own, groups,...]
where the time goes in v4:
time: 295 us; the launch traced here: 294 us
  Pallas kernels  275 us (93%)
  local copies, waits for them, and re-layouts  9.85 us (3%)
  other arithmetic  8.97 us (3%)
    pallas_call x1, Pallas kernels, experts_of_the_plane(): pl.pallas_call(functools.partial(expert_kernel, planes, own, rows, real),...  109 us
    pallas_call x1, Pallas kernels, back(): pl.pallas_call(functools.partial(back_kernel, planes, HEADS, own, groups,...  103 us
    pallas_call x1, Pallas kernels, front(): pl.pallas_call(functools.partial(front_kernel, planes, HEADS, real), out_...  62.8 us

profile of v4, /device:TPU:0, one launch (start us, length us, event | category | flops | bytes accessed | tf_op | source)
XLA Modules:
  0.0 294.4 jit_solution(9081563741874590496)
XLA Ops:
  0.6 1.4 copy.35.refs_5_
  2.0 1.4 copy.34
  3.5 62.8 %dense_weights_and_attention.1 = (bf16[768,128]{1,0:T(8,128)(2,1)}, bf16[768,2304]{1,0:T(8,128)(2,1)}, bf16[768,768]{1,0:T(8,128)(2,1)}, bf16[768,768]{1,0:T(8,1...) custom-call(bf16[200,768]{1,0:T(8,128)(2,1)} %bitcast.18, ...), custom_call_target="tpu_custom_call" | custom-call | flops 4294967296 | bytes 41943040 | tf_op jit(solution)/shard_map/dense_weights_and_attention/pallas_call | solution.py:1040
  66.3 109.1 %experts_of_the_plane.1 = (bf16[4,832,768]{2,1,0:T(8,128)(2,1)}, f32[208,768]{1,0:T(8,128)}, bf16[768,768]{1,0:T(8,128)(2,1)}, bf16[768,768]{1,0:T(8,128)(2,1)}, f32[8,768]{1,0:T(8,128)}, /*index=5*/f32[768,128]{1,0:T(8,128)}) custom-call(bf16[208,1536]{1,0:T(8,128)(2,1)} %get-tuple-element.41.packed_ref.refs_1_, ...), custom_call_target="tpu_custom_call" | custom-call | flops 23555211264 | bytes 41943040 | tf_op jit(solution)/shard_map/experts_of_the_plane/pallas_call | solution.py:714
  175.4 102.9 %attention_backward_and_sums.1 = (bf16[200,768]{1,0:T(8,128)(2,1)}, bf16[200,768]{1,0:T(8,128)(2,1)}, bf16[96,2304]{1,0:T(8,128)(2,1)}, bf16[96,768]{1,0:T(8,128...) custom-call(f32[208,768]{1,0:T(8,128)} %get-tuple-element.44.refs_0_, ...), custom_call_target="tpu_custom_call" | custom-call | flops 8589934592 | bytes 41943040 | tf_op jit(solution)/shard_map/attention_backward_and_sums/pallas_call | solution.py:1584
  278.3 0.0 copy-start.1
  278.4 1.9 slice_reduce_fusion
  280.2 0.8 slice_reduce_fusion.5
  281.0 0.6 reshape_squeeze.3
  281.7 1.0 slice_bitcast_fusion
  282.6 0.7 copy.37
  283.3 0.7 copy.36
  283.9 1.6 convert_element_type.16
  285.6 2.0 convert_element_type.15
  287.5 0.0 copy-done.1
  287.6 0.0 copy-start
  287.6 2.8 convert_element_type.17
  290.3 0.0 copy-done
  290.3 0.0 copy-start.3
  290.3 0.0 copy-start.2
  290.3 2.6 convert.1
  292.9 0.0 copy-done.3
  292.9 0.7 copy.40
  293.6 0.0 copy-done.2
  293.6 0.7 copy.41
Async XLA Ops:
  278.3 9.2 %copy-start.1 = (bf16[4,96,3072]{2,1,0:T(8,128)(2,1)S(1)}, bf16[4,96,3072]{2,1,0:T(8,128)(2,1)}, u32[]{:S(2)}) copy-start(bf16[4,96,3072]{2,1,0:T(8,128)(2,1)} %get-tuple-element.65) | copy-start | bytes 7077892
  287.6 2.8 copy-start
  290.3 2.6 copy-start.3
  290.3 3.3 %copy-start.2 = (bf16[200,768]{1,0:T(8,128)(2,1)S(1)}, bf16[200,768]{1,0:T(8,128)(2,1)}, u32[]{:S(2)}) copy-start(bf16[200,768]{1,0:T(8,128)(2,1)} %get-tuple-element.61) | copy-start | bytes 921604
